TPU v7x, 32 devices: a whole 2x2x4 slice. The times are simulated.
32 devices in a mesh: grp: 2 (over y), seq: 4 (over x, core), mlp: 4 (over z).
Axes of the slice: x: 2, y: 2, z: 4, core: 2. Of those that a mesh axis runs over, the one named last changes fastest.
Arguments:
- inputs: bfloat16 [16, 1024, 768], P(('grp', 'mlp'), 'seq'), parts along dimension 0, may hold values from -6 to 6
- condition: bfloat16 [16, 128], P(('grp', 'mlp')), parts along dimension 0, may hold values from -6 to 6
- attn_gain: float32 [768], replicated, may hold values from 0.1 to 1.9
- ada_weight: bfloat16 [128, 4608], replicated, may hold values from -0.25 to 0.25
- ada_bias: float32 [4608], replicated, may hold values from -3 to 3
- qkv_weight: bfloat16 [768, 2304], replicated, may hold values from -0.21875 to 0.21875
- out_weight: bfloat16 [768, 768], replicated, may hold values from -0.625 to 0.625
- ffn_gain: float32 [768], replicated, may hold values from 0.1 to 1.9
- up_weight: bfloat16 [768, 3072], P(None, 'mlp'), may hold values from -0.21875 to 0.21875
- up_bias: float32 [3072], P('mlp'), may hold values from -3 to 3
- down_weight: bfloat16 [3072, 768], P('mlp'), may hold values from -0.21875 to 0.21875
- down_bias: float32 [768], replicated, may hold values from -4 to 4
- cotangent: bfloat16 [16, 1024, 768], P(('grp', 'mlp'), 'seq'), parts along dimension 0, may hold values from -6 to 6
Outputs:
- output: float32 [16, 1024, 768], P(('grp', 'mlp'), 'seq'), parts along dimension 0
- grad_inputs: float32 [16, 1024, 768], P(('grp', 'mlp'), 'seq'), parts along dimension 0
- grad_condition: float32 [16, 128], P(('grp', 'mlp')), parts along dimension 0
- grad_attn_gain: float32 [1536], P('grp'), parts along dimension 0
- grad_ada_weight: float32 [256, 4608], P('grp'), parts along dimension 0
- grad_ada_bias: float32 [9216], P('grp'), parts along dimension 0
- grad_qkv_weight: float32 [1536, 2304], P('grp'), parts along dimension 0
- grad_out_weight: float32 [1536, 768], P('grp'), parts along dimension 0
- grad_ffn_gain: float32 [1536], P('grp'), parts along dimension 0
- grad_up_weight: float32 [1536, 3072], P('grp', 'mlp'), parts along dimension 0
- grad_up_bias: float32 [6144], P(('grp', 'mlp')), parts along dimension 0
- grad_down_weight: float32 [6144, 768], P(('grp', 'mlp')), parts along dimension 0
- grad_down_bias: float32 [1536], P('grp'), parts along dimension 0
There are 2 independent parts, one for each index of `grp`. A program takes and returns all parts, laid end to end along the dimension named above; an argument that names none is the same for every part. Nothing has to cross between parts.
All inputs are finite; a program needn't handle non-finite values.
Results may differ from a plain program's by a relative error of at most 0.019.
The roundings to bfloat16 on the way count: a program that leaves them out, or rounds other values in their place, can miss the bound.
Values may be sent and summed in bfloat16 or wider, within the bound.
A program may use at most 256 MiB of HBM per device.

v0:
```python
import math

import jax
import jax.numpy as jnp
from jax import lax
from jax.sharding import PartitionSpec as P

HEADS = 12


gelu_coef = 0.7978845608028654


def layer_norm(values):
    center = values - jnp.mean(values, axis=-1, keepdims=True)
    inv_std = lax.rsqrt(jnp.mean(center * center, axis=-1, keepdims=True) + 1e-05)
    return (center * inv_std, inv_std)


def norm_back(grad_norm, normed, inv_std):
    return inv_std * (
        grad_norm
        - jnp.mean(grad_norm, axis=-1, keepdims=True)
        - normed * jnp.mean(grad_norm * normed, axis=-1, keepdims=True)
    )


def gelu_tanh(values):
    return (
        0.5 * values * (1.0 + jnp.tanh(gelu_coef * (values + 0.044715 * values * values * values)))
    )


def gelu_slope(values):
    tanh_val = jnp.tanh(gelu_coef * (values + 0.044715 * values * values * values))
    return 0.5 * (1.0 + tanh_val) + 0.5 * values * (1.0 - tanh_val * tanh_val) * gelu_coef * (
        1.0 + 3.0 * 0.044715 * values * values
    )


def rotary_tables(positions, head_size):
    half_dim = head_size // 2
    frequencies = jnp.power(10000.0, -2.0 * jnp.arange(half_dim, dtype=jnp.float32) / head_size)
    angles = positions[:, None] * frequencies[None, :]
    return (jnp.cos(angles), jnp.sin(angles))


def rotate(tensor, cos_tab, sine_tab):
    half_dim = tensor.shape[-1] // 2
    first_half = tensor[..., :half_dim]
    second_half = tensor[..., half_dim:]
    return jnp.concatenate(
        [
            first_half * cos_tab - second_half * sine_tab,
            second_half * cos_tab + first_half * sine_tab,
        ],
        axis=-1,
    )


def unrotate(tensor, cos_tab, sine_tab):
    half_dim = tensor.shape[-1] // 2
    first_half = tensor[..., :half_dim]
    second_half = tensor[..., half_dim:]
    return jnp.concatenate(
        [
            first_half * cos_tab + second_half * sine_tab,
            second_half * cos_tab - first_half * sine_tab,
        ],
        axis=-1,
    )


def score_of(query_rows, key_rows, scale_factor):
    return (
        jnp.einsum("sghd,skhd->shgk", query_rows, key_rows, preferred_element_type=jnp.float32)
        * scale_factor
    )


def score_grads(query_rows, dout_rows, lse_rows, delta_rows, key_rows, value_rows, scale_factor):
    prob_rows = jnp.exp(score_of(query_rows, key_rows, scale_factor) - lse_rows[..., None])
    grad_probs = jnp.einsum(
        "sghd,skhd->shgk", dout_rows, value_rows, preferred_element_type=jnp.float32
    )
    grad_scores = (prob_rows * (grad_probs - delta_rows[..., None])).astype(jnp.bfloat16)
    return (prob_rows.astype(jnp.bfloat16), grad_scores)


def shards(
    inputs,
    condition,
    attn_gain,
    ada_weight,
    ada_bias,
    qkv_weight,
    out_weight,
    ffn_gain,
    up_weight,
    up_bias,
    down_weight,
    down_bias,
    cotangent,
):
    seq_count, seg_len, model_width = inputs.shape
    head_count = HEADS
    head_size = model_width // head_count
    full_len = seg_len * lax.axis_size("seq")
    block_len = math.gcd(full_len, 512)
    block_count = full_len // block_len
    scale_factor = float(head_size) ** (-0.5)
    positions = (lax.axis_index("seq") * seg_len + jnp.arange(seg_len, dtype=jnp.int32)).astype(
        jnp.float32
    )
    cos_tab, sine_tab = rotary_tables(positions, head_size)
    cos_tab = cos_tab[None, :, None, :]
    sine_tab = sine_tab[None, :, None, :]

    def heads_view(matrix):
        return matrix.reshape(seq_count, seg_len, head_count, head_size)

    x_float = inputs.astype(jnp.float32)
    modulate = jnp.dot(condition, ada_weight, preferred_element_type=jnp.float32) + ada_bias
    shift_one, scale_one, gate_one, shift_two, scale_two, gate_two = [
        modulate[:, None, member * model_width : (member + 1) * model_width] for member in range(6)
    ]
    norm_one, inv_one = layer_norm(x_float)
    attn_in = (norm_one * attn_gain * (1.0 + scale_one) + shift_one).astype(jnp.bfloat16)
    projected = jnp.dot(attn_in, qkv_weight, preferred_element_type=jnp.float32)
    queries = rotate(heads_view(projected[..., :model_width]), cos_tab, sine_tab).astype(
        jnp.bfloat16
    )
    key_rot = rotate(
        heads_view(projected[..., model_width : 2 * model_width]), cos_tab, sine_tab
    ).astype(jnp.bfloat16)
    value_low = projected[..., 2 * model_width :].astype(jnp.bfloat16)
    kv_local = jnp.concatenate(
        [key_rot.reshape(seq_count, seg_len, model_width), value_low], axis=-1
    )
    kv_whole = lax.all_gather(kv_local, "seq", axis=1, tiled=True)
    kv_view = kv_whole.reshape(seq_count, full_len, 2, head_count, head_size)

    def key_block(block_num):
        sliced = lax.dynamic_slice_in_dim(kv_view, block_num * block_len, block_len, 1)
        return (sliced[:, :, 0], sliced[:, :, 1])

    def max_pass(block_num, running):
        run_max, run_sum = running
        key_rows, value_rows = key_block(block_num)
        scores = score_of(queries, key_rows, scale_factor)
        new_max = jnp.maximum(run_max, jnp.max(scores, axis=-1))
        run_sum = run_sum * jnp.exp(run_max - new_max) + jnp.sum(
            jnp.exp(scores - new_max[..., None]), axis=-1
        )
        return (new_max, run_sum)

    stat_shape = (seq_count, head_count, seg_len)
    run_max, run_sum = lax.fori_loop(
        0,
        block_count,
        max_pass,
        (jnp.full(stat_shape, -1e30, jnp.float32), jnp.zeros(stat_shape, jnp.float32)),
    )
    log_sum = run_max + jnp.log(run_sum)

    def out_pass(block_num, accums):
        accum_out, accum_exact = accums
        key_rows, value_rows = key_block(block_num)
        prob_rows = jnp.exp(score_of(queries, key_rows, scale_factor) - log_sum[..., None])
        accum_out = accum_out + jnp.einsum(
            "shgk,skhd->sghd",
            prob_rows.astype(jnp.bfloat16),
            value_rows,
            preferred_element_type=jnp.float32,
        )
        accum_exact = accum_exact + jnp.einsum(
            "shgk,skhd->sghd",
            prob_rows,
            value_rows.astype(jnp.float32),
            preferred_element_type=jnp.float32,
        )
        return (accum_out, accum_exact)

    head_shape = (seq_count, seg_len, head_count, head_size)
    attn_float, attn_exact = lax.fori_loop(
        0,
        block_count,
        out_pass,
        (jnp.zeros(head_shape, jnp.float32), jnp.zeros(head_shape, jnp.float32)),
    )
    attn_low = attn_float.reshape(seq_count, seg_len, model_width).astype(jnp.bfloat16)
    attn_proj = jnp.dot(attn_low, out_weight, preferred_element_type=jnp.float32)
    middle = x_float + gate_one * attn_proj
    norm_two, inv_two = layer_norm(middle)
    ffn_in = (norm_two * ffn_gain * (1.0 + scale_two) + shift_two).astype(jnp.bfloat16)
    ffn_rows = lax.all_gather(ffn_in, "mlp", axis=0, tiled=True)
    pre_act = jnp.dot(ffn_rows, up_weight, preferred_element_type=jnp.float32) + up_bias
    act_low = gelu_tanh(pre_act).astype(jnp.bfloat16)
    ffn_out = (
        lax.psum_scatter(
            jnp.dot(act_low, down_weight, preferred_element_type=jnp.float32).astype(jnp.bfloat16),
            "mlp",
            scatter_dimension=0,
            tiled=True,
        ).astype(jnp.float32)
        + down_bias
    )
    output = middle + gate_two * ffn_out
    cot_float = cotangent.astype(jnp.float32)
    grad_ffn = (gate_two * cot_float).astype(jnp.bfloat16)
    down_bias_part = jnp.sum(grad_ffn.astype(jnp.float32), axis=(0, 1))
    dgate_two = jnp.sum(cot_float * ffn_out, axis=1)
    grad_ffn_rows = lax.all_gather(grad_ffn, "mlp", axis=0, tiled=True)
    down_part = jnp.einsum(
        "sgf,sgd->fd", act_low, grad_ffn_rows, preferred_element_type=jnp.float32
    )
    grad_act = jnp.einsum(
        "sgd,fd->sgf", grad_ffn_rows, down_weight, preferred_element_type=jnp.float32
    )
    grad_pre = (grad_act * gelu_slope(pre_act)).astype(jnp.bfloat16)
    up_bias_part = jnp.sum(grad_pre.astype(jnp.float32), axis=(0, 1))
    up_part = jnp.einsum("sgd,sgf->df", ffn_rows, grad_pre, preferred_element_type=jnp.float32)
    grad_ffn_in = lax.psum_scatter(
        jnp.einsum("sgf,df->sgd", grad_pre, up_weight, preferred_element_type=jnp.float32).astype(
            jnp.bfloat16
        ),
        "mlp",
        scatter_dimension=0,
        tiled=True,
    ).astype(jnp.float32)
    dshift_two = jnp.sum(grad_ffn_in, axis=1)
    dscale_two = jnp.sum(grad_ffn_in * norm_two * ffn_gain, axis=1)
    gain_two_part = jnp.sum(grad_ffn_in * (1.0 + scale_two) * norm_two, axis=(0, 1))
    grad_middle = cot_float + norm_back(
        grad_ffn_in * (1.0 + scale_two) * ffn_gain, norm_two, inv_two
    )
    grad_proj = (gate_one * grad_middle).astype(jnp.bfloat16)
    dgate_one = jnp.sum(grad_middle * attn_proj, axis=1)
    out_part = jnp.einsum("sgd,sge->de", attn_low, grad_proj, preferred_element_type=jnp.float32)
    grad_attn = jnp.einsum(
        "sge,de->sgd", grad_proj, out_weight, preferred_element_type=jnp.float32
    ).astype(jnp.bfloat16)
    grad_attn_heads = heads_view(grad_attn)
    delta_rows = jnp.sum(grad_attn_heads.astype(jnp.float32) * attn_exact, axis=-1)
    delta_heads = jnp.transpose(delta_rows, (0, 2, 1))

    def back_pass(block_num, state_in):
        grad_query, key_grads = state_in
        key_rows, value_rows = key_block(block_num)
        prob_low, grad_scores = score_grads(
            queries, grad_attn_heads, log_sum, delta_heads, key_rows, value_rows, scale_factor
        )
        grad_query = (
            grad_query
            + jnp.einsum(
                "shgk,skhd->sghd", grad_scores, key_rows, preferred_element_type=jnp.float32
            )
            * scale_factor
        )
        grad_key = (
            jnp.einsum("shgk,sghd->skhd", grad_scores, queries, preferred_element_type=jnp.float32)
            * scale_factor
        )
        grad_value = jnp.einsum(
            "shgk,sghd->skhd", prob_low, grad_attn_heads, preferred_element_type=jnp.float32
        )
        stacked = jnp.concatenate(
            [
                grad_key.reshape(seq_count, block_len, model_width),
                grad_value.reshape(seq_count, block_len, model_width),
            ],
            axis=-1,
        )
        key_grads = lax.dynamic_update_slice_in_dim(key_grads, stacked, block_num * block_len, 1)
        return (grad_query, key_grads)

    grad_query, key_grads = lax.fori_loop(
        0,
        block_count,
        back_pass,
        (
            jnp.zeros(head_shape, jnp.float32),
            jnp.zeros((seq_count, full_len, 2 * model_width), jnp.float32),
        ),
    )
    kv_grads = lax.psum_scatter(
        key_grads.astype(jnp.bfloat16), "seq", scatter_dimension=1, tiled=True
    ).astype(jnp.float32)
    grad_key_rot = heads_view(kv_grads[..., :model_width])
    grad_values = kv_grads[..., model_width:]
    grad_qkv = jnp.concatenate(
        [
            unrotate(grad_query, cos_tab, sine_tab).reshape(seq_count, seg_len, model_width),
            unrotate(grad_key_rot, cos_tab, sine_tab).reshape(seq_count, seg_len, model_width),
            grad_values,
        ],
        axis=-1,
    ).astype(jnp.bfloat16)
    qkv_part = jnp.einsum("sgd,sge->de", attn_in, grad_qkv, preferred_element_type=jnp.float32)
    grad_attn_in = jnp.einsum(
        "sge,de->sgd", grad_qkv, qkv_weight, preferred_element_type=jnp.float32
    )
    dshift_one = jnp.sum(grad_attn_in, axis=1)
    dscale_one = jnp.sum(grad_attn_in * norm_one * attn_gain, axis=1)
    gain_one_part = jnp.sum(grad_attn_in * (1.0 + scale_one) * norm_one, axis=(0, 1))
    grad_inputs = grad_middle + norm_back(
        grad_attn_in * (1.0 + scale_one) * attn_gain, norm_one, inv_one
    )
    grad_modulate = jnp.concatenate(
        [dshift_one, dscale_one, dgate_one, dshift_two, dscale_two, dgate_two], axis=-1
    )
    ada_weight_part = jnp.dot(
        condition.astype(jnp.float32).T, grad_modulate, precision=lax.Precision.HIGHEST
    )
    ada_bias_part = jnp.sum(grad_modulate, axis=0)
    cond_part = jnp.dot(
        grad_modulate, ada_weight.astype(jnp.float32).T, precision=lax.Precision.HIGHEST
    )
    summed_all = lax.psum(
        (
            qkv_part,
            out_part,
            ada_weight_part,
            ada_bias_part,
            gain_one_part,
            gain_two_part,
            down_bias_part,
        ),
        ("seq", "mlp"),
    )
    summed_seq = (
        lax.psum(up_part.astype(jnp.bfloat16), "seq").astype(jnp.float32),
        lax.psum(up_bias_part.astype(jnp.bfloat16), "seq").astype(jnp.float32),
        lax.psum(down_part.astype(jnp.bfloat16), "seq").astype(jnp.float32),
        lax.psum(cond_part.astype(jnp.bfloat16), "seq").astype(jnp.float32),
    )
    return (
        output,
        grad_inputs,
        summed_seq[3],
        summed_all[4],
        summed_all[2],
        summed_all[3],
        summed_all[0],
        summed_all[1],
        summed_all[5],
        summed_seq[0],
        summed_seq[1],
        summed_seq[2],
        summed_all[6],
    )


def solution(mesh):
    placed = (
        P(("grp", "mlp"), "seq", None),
        P(("grp", "mlp"), None),
        P(),
        P(),
        P(),
        P(),
        P(),
        P(),
        P(None, "mlp"),
        P("mlp"),
        P("mlp", None),
        P(),
        P(("grp", "mlp"), "seq", None),
    )
    return jax.shard_map(
        shards,
        mesh=mesh,
        in_specs=placed,
        out_specs=(
            P(("grp", "mlp"), "seq", None),
            P(("grp", "mlp"), "seq", None),
            P(("grp", "mlp"), None),
            P("grp"),
            P("grp", None),
            P("grp"),
            P("grp", None),
            P("grp", None),
            P("grp"),
            P("grp", "mlp"),
            P(("grp", "mlp")),
            P(("grp", "mlp"), None),
            P("grp"),
        ),
        check_vma=False,
    )
```

profile of v0, /device:TPU:0, one launch (start us, length us, event | category | flops | bytes accessed | tf_op | source)
XLA Modules:
  0.0 859.0 jit_solution(3387192701589081611)
XLA Ops:
  35.1 48.6 %all-gather.4.cloned.1.call-done = bf16[2,1024,1536]{2,1,0:T(8,128)(2,1)} async-done(((bf16[2,256,1536]{2,1,0:T(8,128)(2,1)}), bf16[2,1024,1536]{2,1,0:T(8,128)(2,1)}) %all-gather.4.cloned.1.call-update) | async-done | bytes 6291472 | tf_op jit(solution)/shard_map/all_gather | solution.py:140
  83.7 8.6 %copy.82 = bf16[2,1024,1536]{1,2,0:T(8,128)(2,1)} copy(bf16[2,1024,1536]{2,1,0:T(8,128)(2,1)} %all-gather.4.cloned.1.call-done) | data formatting | bytes 12582912 | tf_op jit(solution)/shard_map/all_gather | solution.py:140
  92.3 6.6 copy.85
  98.9 12.6 %while.48 = (s32[]{:T(128)}, f32[2,12,256]{2,1,0:T(8,128)}, f32[2,12,256]{2,1,0:T(8,128)}, bf16[2,1024,2,12,64]{1,4,3,0,2:T(8,128)(2,1)}, bf16[2,256,12,64]{1,3,...) while((s32[]{:T(128)}, f32[2,12,256]{2,1,0:T(8,128)}, ...), condition=%wide.region_5.0_spmd.clone, body=%wide.region_2.0_spmd.clone.sunk | while | flops 418412544 | bytes 28139764 | solution.py:158
  112.9 20.2 %while.49 = (s32[]{:T(128)}, f32[2,256,12,64]{1,3,2,0:T(8,128)}, f32[2,256,12,64]{1,3,2,0:T(8,128)}, bf16[2,1024,2,12,64]{1,4,3,0,2:T(8,128)(2,1)}, bf16[2,256,1...) while((s32[]{:T(128)}, f32[2,256,12,64]{1,3,2,0:T(8,128)}, ...), condition=%wide.region_7.0_spmd.clone, body=%wide.region_6.0_spmd.clone.sunk | while | flops 1225261056 | bytes 100041064 | solution.py:185
  142.6 60.6 %all-gather.6.cloned.1.call-done = bf16[8,256,768]{2,1,0:T(8,128)(2,1)} async-done(((bf16[2,256,768]{2,1,0:T(8,128)(2,1)}), bf16[8,256,768]{2,1,0:T(8,128)(2,1)}) %all-gather.6.cloned.1.call-update) | async-done | bytes 3145744 | tf_op jit(solution)/shard_map/all_gather | solution.py:196
  203.2 7.5 fusion.77
  210.8 56.8 %all-gather.8.cloned.1.call-done = bf16[8,256,768]{2,1,0:T(8,128)(2,1)} async-done(((bf16[2,256,768]{2,1,0:T(8,128)(2,1)}), bf16[8,256,768]{2,1,0:T(8,128)(2,1)}) %all-gather.8.cloned.1.call-update) | async-done | bytes 3145744 | tf_op jit(solution)/shard_map/all_gather | solution.py:213
  267.6 9.1 %fusion.90 = (bf16[768]{0:T(1024)(128)(2,1)}, bf16[8,256,768]{2,1,0:T(8,128)(2,1)S(1)}) fusion(f32[8,256,768]{2,1,0:T(8,128)} %fusion.77, f32[768]{0:T(1024)} %param.28, bf16[8,256,768]{2,1,0:T(8,128)(2,1)} %all-gather.8.cloned.1.call-done, bf16[768,768]{1,0:T(8,128)(2,1)} %param.29), kind=kOutput, calls=%fused_computation.170 | convolution fusion | flops 2448948480 | bytes 13767168 | tf_op jit(solution)/shard_map/sgd,fd->sgf/dot_general | solution.py:217
  282.4 8.8 %convolution_convert_fusion.1 = bf16[8,256,768]{2,1,0:T(8,128)(2,1)} fusion(bf16[768,768]{1,0:T(8,128)(2,1)} %param.29, f32[8,256,768]{2,1,0:T(8,128)} %fusion.77, f32[768]{0:T(1024)} %param.28), kind=kOutput, calls=%fused_computation.75 | convolution fusion | flops 2433220608 | bytes 10619904 | tf_op jit(solution)/shard_map/dot_general | solution.py:201
  291.6 49.9 %reduce-scatter.6.cloned.1.call-done = bf16[2,256,768]{2,1,0:T(8,128)(2,1)} async-done(((bf16[8,256,768]{2,1,0:T(8,128)(2,1)}), bf16[2,256,768]{2,1,0:T(8,128)(2,1)}) %reduce-scatter.6.cloned.1.call-update) | async-done | bytes 786448 | tf_op jit(solution)/shard_map/reduce_scatter | solution.py:223
  345.9 58.0 %reduce-scatter.4.cloned.1.call-done = bf16[2,256,768]{2,1,0:T(8,128)(2,1)} async-done(((bf16[8,256,768]{2,1,0:T(8,128)(2,1)}), bf16[2,256,768]{2,1,0:T(8,128)(2,1)}) %reduce-scatter.4.cloned.1.call-update) | async-done | bytes 786448 | tf_op jit(solution)/shard_map/reduce_scatter | solution.py:200
  403.9 5.6 multiply_reduce_fusion
  420.1 74.5 %while.50 = (s32[]{:T(128)}, f32[2,256,12,64]{1,3,2,0:T(8,128)}, bf16[2,1024,1536]{2,1,0:T(8,128)(2,1)}, bf16[2,1024,2,12,64]{1,4,3,0,2:T(8,128)(2,1)}, bf16[2,2...) while((s32[]{:T(128)}, f32[2,256,12,64]{1,3,2,0:T(8,128)}, ...), condition=%wide.region_16.0_spmd.clone, body=%wide.region_15.0_spmd.clone.sunk | while | flops 2047475712 | bytes 115106176 | solution.py:277
  420.1 8.1 fusion.141
  428.3 7.0 fusion.142
  435.3 6.6 multiply_convert_fusion.8
  448.2 4.6 copy.123
  456.7 8.1 fusion.141
  464.8 7.0 fusion.142
  471.9 6.6 multiply_convert_fusion.8
  486.2 4.6 copy.123
  495.2 6.7 bitcast_convert_fusion.1
  501.8 8.7 %bitcast_convert_fusion = bf16[768,768]{1,0:T(8,128)(2,1)} fusion(bf16[8,256,768]{2,1,0:T(8,128)(2,1)S(1)} %copy-done.52, f32[8,256,768]{2,1,0:T(8,128)} %fusion.77, f32[768]{0:T(1024)S(1)} %copy-done.54), kind=kOutput, calls=%fused_computation.72 | convolution fusion | flops 2432237568 | bytes 10619904 | tf_op jit(solution)/shard_map/sgf,sgd->fd/dot_general | solution.py:214
  514.7 38.5 %reduce-scatter.8.cloned.1.call-done = bf16[2,256,1536]{2,1,0:T(8,128)(2,1)} async-done(((bf16[2,1024,1536]{2,1,0:T(8,128)(2,1)}), bf16[2,256,1536]{2,1,0:T(8,128)(2,1)}) %reduce-scatter.8.cloned.1.call-update) | async-done | bytes 1572880 | tf_op jit(solution)/shard_map/reduce_scatter | solution.py:286
  570.2 6.1 fusion.67
  580.5 5.2 convolution_bitcast_fusion.1
  585.7 25.9 %all-reduce.9.cloned.1.call-done = (bf16[768,768]{1,0:T(8,128)(2,1)}, bf16[768,768]{1,0:T(8,128)(2,1)}) async-done(((bf16[768,768]{1,0:T(8,128)(2,1)}, bf16[768,768]{1,0:T(8,128)(2,1)}), (bf16[768,768]{1,0:T(8,128)(2,1)}, bf16[768,768]{1,0:T(8,128)(2,1)})) %all-reduce.9.cloned.1.call-update) | async-done | bytes 2359312 | tf_op jit(solution)/shard_map/psum | solution.py:332
  620.4 6.8 all-reduce.2
  629.6 65.5 %all-reduce = (f32[768]{0:T(1024)}, f32[4608]{0:T(1024)}, f32[768]{0:T(1024)}, f32[768]{0:T(1024)}) all-reduce(f32[768]{0:T(1024)} %get-tuple-element.560, f32[4608]{0:T(1024)} %reduce_sum.212, f32[768]{0:T(1024)} %get-tuple-element.558, f32[768]{0:T(1024)S(1)} %copy-done.43), channel_id=1, replica_groups=mesh['grp'=2,'seq'=4,'mlp'=4] {'seq','mlp'}, use_global_device_ids=true, to_apply=%region_28.0 | all-reduce | flops 6912 | bytes 55296 | tf_op jit(solution)/shard_map/psum | solution.py:319
  700.4 140.6 %all-reduce.7.cloned.1.call-done = (f32[128,4608]{0,1:T(8,128)}, f32[768,2304]{1,0:T(8,128)}, f32[768,768]{1,0:T(8,128)}) async-done(((f32[128,4608]{0,1:T(8,128)}, f32[768,2304]{1,0:T(8,128)}, f32[768,768]{1,0:T(8,128)}), (f32[128,4608]{0,1:T(8,128)}, f32[768,2304]{1,0:T(8,128)}, f32[768,768]{1,0:T(8,128)})) %all-reduce.7.cloned.1.call-update) | async-done | bytes 11796496 | tf_op jit(solution)/shard_map/psum | solution.py:319
  844.0 6.6 copy.162
  (253 shorter events, 160.3 us)
Async XLA Ops:
  7.2 6.0 copy-start
  7.2 76.5 %all-gather.4.cloned.1.call-start = ((), (), s32[]{:S(2)}) async-start(), calls=%async_computation.3 | async-start | bytes 7864320 | tf_op jit(solution)/shard_map/all_gather | solution.py:140
  9.5 5.9 copy-start.41
  34.4 168.8 %all-gather.6.cloned.1.call-start = ((), (), s32[]{:S(2)}) async-start(), calls=%async_computation.4 | async-start | bytes 3932160 | tf_op jit(solution)/shard_map/all_gather | solution.py:196
  139.6 128.0 %all-gather.8.cloned.1.call-start = ((), (), s32[]{:S(2)}) async-start(), calls=%async_computation.6 | async-start | bytes 3932160 | tf_op jit(solution)/shard_map/all_gather | solution.py:213
  142.4 199.0 %reduce-scatter.6.cloned.1.call-start = ((), (), s32[]{:S(2)}) async-start(), calls=%async_computation.7 | async-start | bytes 3932160 | tf_op jit(solution)/shard_map/reduce_scatter | solution.py:223
  267.6 10.8 %copy-start.53 = (bf16[768,768]{1,0:T(8,128)(2,1)S(1)}, bf16[768,768]{1,0:T(8,128)(2,1)}, u32[]{:S(2)}) copy-start(bf16[768,768]{1,0:T(8,128)(2,1)} %param.27) | copy-start | bytes 3538948
  282.4 121.5 %reduce-scatter.4.cloned.1.call-start = ((), (), s32[]{:S(2)}) async-start(), calls=%async_computation.5 | async-start | bytes 3932160 | tf_op jit(solution)/shard_map/reduce_scatter | solution.py:200
  291.3 261.9 %reduce-scatter.8.cloned.1.call-start = ((), (), s32[]{:S(2)}) async-start(), calls=%async_computation.8 | async-start | bytes 7864320 | tf_op jit(solution)/shard_map/reduce_scatter | solution.py:286
  403.9 6.7 copy-start.23
  420.1 8.1 copy-start.3
  420.1 8.1 copy-start.10
  420.1 15.2 %slice-start = ((s8[6291456]{0:T(1024)(128)(4,1)}), s8[4194304]{0:T(1024)(128)(4,1)S(1)}, s32[]{:S(2)}) async-start(s8[6291456]{0:T(1024)(128)(4,1)} %bitcast.150), calls=%async_computation.11 | async-start | bytes 8388608 | tf_op jit(solution)/shard_map/while
  428.3 7.0 slice-start.1
  428.3 7.0 copy-start.18
  456.7 8.1 copy-start.3
  456.7 8.1 copy-start.10
  456.7 15.2 %slice-start = ((s8[6291456]{0:T(1024)(128)(4,1)}), s8[4194304]{0:T(1024)(128)(4,1)S(1)}, s32[]{:S(2)}) async-start(s8[6291456]{0:T(1024)(128)(4,1)} %bitcast.150), calls=%async_computation.11 | async-start | bytes 8388608 | tf_op jit(solution)/shard_map/while
  464.8 7.0 slice-start.1
  464.8 7.0 copy-start.18
  494.7 7.1 copy-start.54
  494.7 116.9 %all-reduce.9.cloned.1.call-start = ((), (), s32[]{:S(2)}) async-start(), calls=%async_computation.10 | async-start | bytes 4718592 | tf_op jit(solution)/shard_map/psum | solution.py:332
  495.1 6.7 copy-start.52
  510.6 330.4 %all-reduce.7.cloned.1.call-start = ((), (), s32[]{:S(2)}) async-start(), calls=%async_computation.9 | async-start | bytes 23592960 | tf_op jit(solution)/shard_map/psum | solution.py:319
  570.1 6.2 copy-start.37
  570.1 6.2 copy-start.39
  570.1 6.2 copy-start.38
  570.1 6.3 copy-start.36
  570.2 6.9 copy-start.51
  570.2 10.3 %copy-start.26 = (bf16[2,256,768]{2,1,0:T(8,128)(2,1)S(1)}, bf16[2,256,768]{2,1,0:T(8,128)(2,1)}, u32[]{:S(2)}) copy-start(bf16[2,256,768]{2,1,0:T(8,128)(2,1)} %get-tuple-element.636) | copy-start | bytes 2359300
  614.5 15.1 %copy-start.43 = (f32[768]{0:T(1024)S(1)}, f32[768]{0:T(1024)}, u32[]{:S(2)}) copy-start(f32[768]{0:T(1024)} %get-tuple-element.617) | copy-start | bytes 9220
  844.0 6.6 copy-start.17
  (49 other events, 138.9 us)
Sparse Core Ops, SparseCore 0:
  34.6 49.0 all-gather.3
  139.7 63.5 all-gather.5
  205.4 62.1 all-gather.7
  282.5 58.8 reduce-scatter.5
  343.6 60.2 reduce-scatter.3
  494.8 58.3 reduce-scatter.7
  555.7 55.8 all-reduce.8
  616.7 224.2 all-reduce.6
where the time goes:
time: 865 us; the launch traced here: 859 us
  waiting for transfers between devices  479 us (55%)
  matrix products  152 us (18%)
  local copies, waits for them, and re-layouts  76.2 us (9%)
  blocking collectives  72.3 us (8%)
  other arithmetic  63 us (7%)
  between operations  14.8 us (2%)
    psum x1, waiting for transfers between devices, shards(): lax.psum((qkv_part, out_part, ada_weight_part, ada_bias_part, gain_one_pa...  141 us
    psum x1, blocking collectives, shards(): lax.psum((qkv_part, out_part, ada_weight_part, ada_bias_part, gain_one_pa...  65.5 us
    all_gather x1, waiting for transfers between devices, shards(): ffn_rows = lax.all_gather(ffn_in, 'mlp', axis=0, tiled=True)  60.6 us
    reduce_scatter x1, waiting for transfers between devices, shards(): lax.psum_scatter(jnp.dot(act_low, down_weight, preferred_element_type=jnp...  58 us
    all_gather x1, waiting for transfers between devices, shards(): grad_ffn_rows = lax.all_gather(grad_ffn, 'mlp', axis=0, tiled=True)  56.8 us
    reduce_scatter x1, waiting for transfers between devices, shards(): lax.psum_scatter(jnp.einsum('sgf,df->sgd', grad_pre, up_weight, preferred...  49.9 us
    all_gather x1, waiting for transfers between devices, shards(): kv_whole = lax.all_gather(kv_local, 'seq', axis=1, tiled=True)  48.6 us
    reduce_scatter x1, waiting for transfers between devices, shards(): lax.psum_scatter(key_grads.astype(jnp.bfloat16), 'seq', scatter_dimension...  38.5 us
  transfers between devices with their start and end apart: 8, of which 8 were waited for; matrix products, arithmetic and copies ran while one was open for 11% of the time, Pallas kernels for 0%

commit v1 on v0

--- a/solution.py
+++ b/solution.py
@@ -1,11 +1,16 @@
+import functools
 import math
 
 import jax
 import jax.numpy as jnp
+import numpy as np
 from jax import lax
+from jax.experimental import pallas as pl
+from jax.experimental.pallas import tpu as pltpu
 from jax.sharding import PartitionSpec as P
 
 HEADS = 12
+VMEM_LIMIT = 62 * 2**20
 
 
 gelu_coef = 0.7978845608028654
@@ -351,6 +356,733 @@
     )
 
 
+BF = jnp.bfloat16
+F32 = jnp.float32
+MESH = pl.DeviceIdType.MESH
+
+
+def dot(a, b):
+    return jnp.dot(a, b, preferred_element_type=F32)
+
+
+def dot_t(a, b):
+    return lax.dot_general(a, b, (((1,), (1,)), ((), ())), preferred_element_type=F32)
+
+
+def rows_of(start, size):
+    return pl.ds(pl.multiple_of(start, size), size)
+
+
+def pick(table, index):
+    value = jnp.int32(table[0])
+    for place in range(1, len(table)):
+        value = jnp.where(index == place, jnp.int32(table[place]), value)
+    return value
+
+
+def swap_halves(tile):
+    lane = lax.broadcasted_iota(jnp.int32, tile.shape, 1)
+    return jnp.where(
+        lane % 64 < 32, pltpu.roll(tile, 96, 1), pltpu.roll(tile, 32, 1)
+    )
+
+
+def fast_kernel(
+    chain,
+    inputs, cond, again, adaw_h, adab, qkv_h, outw_h, fgain, up_h, upb, down_h, downb, cot_h,
+    cos_h, sin_h, cost_h, sint_h,
+    out_o, gin_o, g_o, b_o, vec_o, ubg_o,
+    adaw, wq, wo, wu, wd, ub, cos_v, sin_v, cost, sint,
+    xb, ctb, mod2, n1, i1, ai, ait, q_s, k_s, v_s, kt_s, vt_s, ot_s, lse, att, att_s,
+    ap, n2, i2, fi, fit, gf, gft, oacc, gacc, a_s, gp_s, g_s, osend, orecv, gsend, grecv,
+    gm, do_s, dlt, qm, dom, dqt, gq, b_s, xs, xr, fst, vec, ubg,
+    lsem, ssem, rsem, wss, wrs, yss, yrs,
+):
+    Z = chain
+    grp = lax.axis_index("grp")
+    seq = lax.axis_index("seq")
+    z = lax.axis_index("mlp")
+    x, c = seq // 2, seq % 2
+    D = 768
+    own = c * 512
+    other = (1 - c) * 512
+    TO_CORE = {"seq": x * 2 + (1 - c)}
+    TO_X = {"seq": (1 - x) * 2 + c}
+    TO_Y = {"grp": 1 - grp}
+    RIGHT = {"mlp": jnp.minimum(z + 1, Z - 1)}
+    LEFT = {"mlp": jnp.maximum(z - 1, 0)}
+
+    def remote(src, dst, index, device):
+        return pltpu.make_async_remote_copy(
+            src_ref=src, dst_ref=dst, send_sem=ssem.at[index], recv_sem=rsem.at[index],
+            device_id=device, device_id_type=MESH,
+        )
+
+    def local(src, dst, index):
+        return pltpu.make_async_copy(src, dst, lsem.at[index])
+
+    half = pl.ds(pl.multiple_of(c * 384, 128), 384)
+    loads = [local(inputs.at[x], xb.at[rows_of(x * 256, 256)], 0), local(adaw_h, adaw, 1)]
+    loads += [local(cos_h, cos_v, 2), local(sin_h, sin_v, 3), local(cost_h, cost, 4), local(sint_h, sint, 5)]
+    for p in range(3):
+        for part in range(3):
+            loads.append(
+                local(
+                    qkv_h.at[:, pl.ds(pl.multiple_of(part * D + c * 384 + p * 128, 128), 128)],
+                    wq.at[p, :, pl.ds(part * 128, 128)],
+                    6 + p * 3 + part,
+                )
+            )
+    loads.append(local(outw_h, wo, 15))
+    loads.append(local(up_h.at[:, half], wu.at[z], 16))
+    loads.append(local(down_h.at[rows_of(c * 384, 384)], wd.at[z], 17))
+    loads.append(local(cot_h.at[x], ctb.at[rows_of(x * 256, 256)], 18))
+    loads.append(local(upb, ub.at[z], 19))
+    for item in loads:
+        item.start()
+
+    barrier = pltpu.get_barrier_semaphore()
+    for device in (TO_CORE, TO_X, TO_Y):
+        pl.semaphore_signal(barrier, 1, device_id=device, device_id_type=MESH)
+
+    @pl.when(z > 0)
+    def _():
+        pl.semaphore_signal(barrier, 1, device_id=LEFT, device_id_type=MESH)
+
+    @pl.when(z < Z - 1)
+    def _():
+        pl.semaphore_signal(barrier, 1, device_id=RIGHT, device_id_type=MESH)
+
+    ends = jnp.where(z > 0, 1, 0) + jnp.where(z < Z - 1, 1, 0)
+    pl.semaphore_wait(barrier, 3 + ends)
+
+    swap_x = remote(inputs.at[1 - x], xb.at[rows_of(x * 256, 256)], 0, TO_X)
+    swap_x.start()
+    swap_c = remote(cot_h.at[1 - x], ctb.at[rows_of(x * 256, 256)], 1, TO_X)
+    swap_c.start()
+
+    def up_half(ref, which):
+        return ref.at[rows_of(which * 384, 384)]
+
+    def down_half(ref, which):
+        return ref.at[rows_of(which * 192, 192)]
+
+    def z_copies(j, way, device, first):
+        if first:
+            src = (
+                up_h.at[rows_of(grp * 384, 384), half],
+                down_h.at[rows_of(c * 384 + grp * 192, 192)],
+                upb,
+            )
+        else:
+            src = (up_half(wu.at[j], grp), down_half(wd.at[j], grp), ub.at[j])
+        dst = (up_half(wu.at[j], grp), down_half(wd.at[j], grp), ub.at[j])
+        return [
+            pltpu.make_async_remote_copy(
+                src_ref=src[i], dst_ref=dst[i], send_sem=wss.at[way, j, i], recv_sem=wrs.at[way, j, i],
+                device_id=device, device_id_type=MESH,
+            )
+            for i in range(3)
+        ]
+
+    def y_copies(j, which):
+        return [
+            pltpu.make_async_remote_copy(
+                src_ref=ref, dst_ref=ref, send_sem=yss.at[j, i], recv_sem=yrs.at[j, i],
+                device_id=TO_Y, device_id_type=MESH,
+            )
+            for i, ref in enumerate((up_half(wu.at[j], which), down_half(wd.at[j], which)))
+        ]
+
+    def start_all(items):
+        for item in items:
+            item.start()
+
+    @pl.when(z < Z - 1)
+    def _():
+        start_all(z_copies(z, 0, RIGHT, True))
+
+    @pl.when(z > 0)
+    def _():
+        start_all(z_copies(z, 1, LEFT, True))
+
+    def weight_step(k):
+        @pl.when(z - k >= 0)
+        def _():
+            j = z - k
+            for item in z_copies(j, 0, RIGHT, False):
+                item.wait_recv()
+
+            @pl.when(z < Z - 1)
+            def _():
+                start_all(z_copies(j, 0, RIGHT, False))
+
+            start_all(y_copies(j, grp))
+
+        @pl.when(z + k <= Z - 1)
+        def _():
+            j = z + k
+            for item in z_copies(j, 1, LEFT, False):
+                item.wait_recv()
+
+            @pl.when(z > 0)
+            def _():
+                start_all(z_copies(j, 1, LEFT, False))
+
+            start_all(y_copies(j, grp))
+
+    local(adaw_h, adaw, 1).wait()
+    for part in range(6):
+        span = pl.ds(part * D, D)
+        mod2[:, span] = dot(cond[...], adaw[:, span]) + adab[:, span]
+    modrow = mod2[pl.ds(x, 1), :]
+    shift_one, scale_one, gate_one, shift_two, scale_two, gate_two = [
+        modrow[:, part * D : (part + 1) * D] for part in range(6)
+    ]
+
+    def layer_norm(values):
+        center = values - jnp.mean(values, axis=-1, keepdims=True)
+        inv = lax.rsqrt(jnp.mean(center * center, axis=-1, keepdims=True) + 1e-05)
+        return center * inv, inv
+
+    TILE = 64
+    mul_one = again[...] * (1.0 + scale_one)
+    mul_two = fgain[...] * (1.0 + scale_two)
+
+    def norm_one_block(block):
+        @pl.loop(0, 256 // TILE)
+        def _(i):
+            at = block * 256 + i * TILE
+            rows = rows_of(at, TILE)
+            normed, inv = layer_norm(xb[rows].astype(F32))
+            n1[rows] = normed
+            i1[rows] = inv
+            ai[rows_of(own + at, TILE)] = (normed * mul_one + shift_one).astype(BF)
+
+    def core_rows(ref, start, size, index):
+        part = ref.at[rows_of(start, size)]
+        return remote(part, part, index, TO_CORE)
+
+    for item in loads[2:15]:
+        item.wait()
+
+    def project_block(block):
+        @pl.loop(0, 2)
+        def _(half_core):
+            start = half_core * 512 + block * 256
+            rows = rows_of(start, 256)
+            tile = ai[rows]
+            ait[:, rows] = tile.T
+            cos_t, sin_t = cos_v[rows], sin_v[rows]
+
+            @pl.loop(0, 3)
+            def _(p):
+                projected = dot(tile, wq[p])
+                query = projected[:, :128]
+                key = projected[:, 128:256]
+                value = projected[:, 256:].astype(BF)
+                query = (query * cos_t + swap_halves(query) * sin_t).astype(BF)
+                key = (key * cos_t + swap_halves(key) * sin_t).astype(BF)
+                q_s[p, rows] = query * jnp.asarray(0.125, BF)
+                k_s[p, rows] = key
+                v_s[p, rows] = value
+                kt_s[p, :, rows] = key.T
+                vt_s[p, :, rows] = value.T
+
+    loads[0].wait()
+    norm_one_block(x)
+    core_rows(ai, own + x * 256, 256, 2).start()
+    core_rows(ai, other + x * 256, 256, 2).wait_recv()
+    project_block(x)
+    swap_x.wait_recv()
+    norm_one_block(1 - x)
+    core_rows(ai, own + (1 - x) * 256, 256, 3).start()
+    core_rows(ai, other + (1 - x) * 256, 256, 3).wait_recv()
+    project_block(1 - x)
+    loads[16].wait()
+    loads[17].wait()
+    loads[19].wait()
+    weight_step(1)
+
+    low_lane = lax.broadcasted_iota(jnp.int32, (1, 128), 1) < 64
+    keep = [low_lane.astype(F32).astype(BF), (~low_lane).astype(F32).astype(BF)]
+
+    def att_copy(p, start):
+        return remote(
+            att_s.at[:, pl.ds(p * 128, 128)],
+            att.at[:, pl.ds(pl.multiple_of(c * 384 + p * 128, 128), 128)],
+            4 + p,
+            TO_CORE,
+        )
+
+    def attend(p):
+        @pl.loop(0, 4)
+        def _(t):
+            cols = rows_of(t * 256, 256)
+            query = q_s[p, cols]
+            keys = k_s[p]
+            outs = []
+            for h in range(2):
+                masked = query * keep[h]
+                scores = dot_t(keys, masked)
+                top = jnp.max(scores, axis=0, keepdims=True)
+                expd = jnp.exp(scores - top)
+                total = jnp.sum(expd, axis=0, keepdims=True)
+                lse[p, pl.ds(h, 1), cols] = top + jnp.log(total)
+                out = dot(vt_s[p, pl.ds(h * 64, 64), :], expd.astype(BF)) / total
+                ot_s[p, pl.ds(h * 64, 64), cols] = out
+                outs.append(out)
+            natural = jnp.concatenate(outs, axis=0).T.astype(BF)
+            lanes = pl.ds(pl.multiple_of(c * 384 + p * 128, 128), 128)
+
+            @pl.when(t // 2 == c)
+            def _():
+                att[rows_of((t % 2) * 256, 256), lanes] = natural
+
+            @pl.when(t // 2 != c)
+            def _():
+                att_s[rows_of((t % 2) * 256, 256), pl.ds(p * 128, 128)] = natural
+
+        att_copy(p, True).start()
+
+    attend(0)
+    attend(1)
+    weight_step(2)
+
+    loads[18].wait()
+    swap_c.wait_recv()
+
+    @pl.loop(0, 512 // TILE)
+    def _(i):
+        at = i * TILE
+        gf[rows_of(own + at, TILE)] = (gate_two * ctb[rows_of(at, TILE)].astype(F32)).astype(BF)
+
+    core_rows(gf, own, 512, 7).start()
+    attend(2)
+    vec[...] = jnp.zeros_like(vec)
+
+    @pl.loop(0, 512 // TILE)
+    def _(i):
+        vec[8:9] += jnp.sum(gf[rows_of(own + i * TILE, TILE)].astype(F32), axis=0, keepdims=True)
+
+    for p in range(3):
+        remote(
+            att_s.at[:, pl.ds(p * 128, 128)],
+            att.at[:, pl.ds(pl.multiple_of((1 - c) * 384 + p * 128, 128), 128)],
+            4 + p,
+            TO_CORE,
+        ).wait_recv()
+    loads[15].wait()
+
+    @pl.loop(0, 2)
+    def _(b):
+        rows = rows_of(b * 256, 256)
+        ap[rows] = dot(att[rows], wo[...])
+
+        @pl.loop(0, 256 // TILE)
+        def _(i):
+            at = b * 256 + i * TILE
+            tile = rows_of(at, TILE)
+            middle = xb[tile].astype(F32) + gate_one * ap[tile]
+            normed, inv = layer_norm(middle)
+            n2[tile] = normed
+            i2[tile] = inv
+            fi[rows_of(own + at, TILE)] = (normed * mul_two + shift_two).astype(BF)
+
+    core_rows(fi, own, 512, 8).start()
+    core_rows(gf, other, 512, 7).wait_recv()
+
+    @pl.loop(0, 4)
+    def _(t):
+        rows = rows_of(t * 256, 256)
+        gft[:, rows] = gf[rows].T
+
+    core_rows(fi, other, 512, 8).wait_recv()
+
+    @pl.loop(0, 4)
+    def _(t):
+        rows = rows_of(t * 256, 256)
+        fit[:, rows] = fi[rows].T
+
+    orders = [sorted(range(Z), key=lambda j, a=a: (abs(j - a), j)) for a in range(Z)]
+    coef = 0.7978845608028654
+
+    @pl.loop(0, Z)
+    def _(k):
+        j = pick([pick([orders[a][n] for a in range(Z)], z) for n in range(Z)], k)
+
+        @pl.when(k >= 3)
+        def _():
+            weight_step(k)
+
+        @pl.when(k > 0)
+        def _():
+            for item in y_copies(j, 1 - grp):
+                item.wait_recv()
+
+        bias = ub[j][:, pl.ds(0, 384)]
+        bias = jnp.where(c == 0, bias, ub[j][:, pl.ds(384, 384)])
+        up_j, down_j = wu[j], wd[j]
+
+        @pl.loop(0, 4)
+        def _(t):
+            rows = rows_of(t * 256, 256)
+            pre = dot(fi[rows], wu[j]) + bias
+            sq = pre * pre
+            th = jnp.tanh(coef * (pre + 0.044715 * pre * sq))
+            act = (0.5 * pre * (1.0 + th)).astype(BF)
+            slope = 0.5 * (1.0 + th) + 0.5 * pre * (1.0 - th * th) * coef * (1.0 + 3.0 * 0.044715 * sq)
+            a_s[rows] = act
+            grad_pre = (dot_t(gf[rows], wd[j]) * slope).astype(BF)
+            gp_s[rows] = grad_pre
+            bsum = jnp.sum(grad_pre.astype(F32), axis=0, keepdims=True)
+            out = dot(act, wd[j])
+            gin = dot_t(grad_pre, wu[j])
+
+            @pl.when(k == 0)
+            def _():
+                oacc[rows] = out
+                gacc[rows] = gin
+
+            @pl.when(k > 0)
+            def _():
+                oacc[rows] += out
+                gacc[rows] += gin
+
+            @pl.when(t == 0)
+            def _():
+                ubg[j] = bsum
+
+            @pl.when(t > 0)
+            def _():
+                ubg[j] += bsum
+
+        @pl.loop(0, 3)
+        def _(r):
+            rows = rows_of(r * 256, 256)
+            g_s[0, j, rows] = dot(fit[rows], gp_s[...]).astype(BF)
+            g_s[1, j, rows] = dot(gft[rows], a_s[...]).astype(BF)
+
+    g_out = local(g_s, g_o, 0)
+    g_out.start()
+
+    @pl.loop(0, 512 // TILE)
+    def _(i):
+        tile = rows_of(i * TILE, TILE)
+        far = rows_of(other + i * TILE, TILE)
+        gsend[tile] = gacc[far].astype(BF)
+        osend[tile] = oacc[far].astype(BF)
+
+    remote(gsend, grecv, 9, TO_CORE).start()
+    remote(osend, orecv, 10, TO_CORE).start()
+    remote(gsend, grecv, 9, TO_CORE).wait_recv()
+    core_rows(gf, own, 512, 7).wait_send()
+
+    def norm_back(grad, normed, inv):
+        return inv * (
+            grad
+            - jnp.mean(grad, axis=-1, keepdims=True)
+            - normed * jnp.mean(grad * normed, axis=-1, keepdims=True)
+        )
+
+    @pl.loop(0, 512 // TILE)
+    def _(i):
+        tile = rows_of(i * TILE, TILE)
+        near = rows_of(own + i * TILE, TILE)
+        grad = gacc[near] + grecv[tile].astype(F32)
+        normed = n2[tile]
+        vec[3:4] += jnp.sum(grad, axis=0, keepdims=True)
+        vec[4:5] += jnp.sum(grad * normed, axis=0, keepdims=True)
+        middle = ctb[tile].astype(F32) + norm_back(grad * mul_two, normed, i2[tile])
+        gm[tile] = middle
+        gf[near] = (gate_one * middle).astype(BF)
+        vec[2:3] += jnp.sum(middle * ap[tile], axis=0, keepdims=True)
+
+    gproj = gf
+    core_rows(gproj, own, 512, 11).start()
+
+    remote(osend, orecv, 10, TO_CORE).wait_recv()
+
+    @pl.loop(0, 512 // TILE)
+    def _(i):
+        tile = rows_of(i * TILE, TILE)
+        ffn = oacc[rows_of(own + i * TILE, TILE)] + orecv[tile].astype(F32) + downb[...]
+        vec[5:6] += jnp.sum(ctb[tile].astype(F32) * ffn, axis=0, keepdims=True)
+        oacc[rows_of(own + i * TILE, TILE)] = (
+            xb[tile].astype(F32) + gate_one * ap[tile] + gate_two * ffn
+        )
+
+    def hand_over(src, out_ref, number):
+        @pl.loop(0, 256 // TILE)
+        def _(i):
+            xs[number, rows_of(i * TILE, TILE)] = src[
+                rows_of(own + (1 - x) * 256 + i * TILE, TILE)
+            ].astype(BF)
+            fst[2 * number, rows_of(i * TILE, TILE)] = src[rows_of(own + x * 256 + i * TILE, TILE)]
+
+        remote(xs.at[number], xr.at[number], 12 + number, TO_X).start()
+        local(fst.at[2 * number], out_ref.at[x], 1 + 2 * number).start()
+
+    def take_over(out_ref, number):
+        remote(xs.at[number], xr.at[number], 12 + number, TO_X).wait_recv()
+        fst[2 * number + 1] = xr[number].astype(F32)
+        local(fst.at[2 * number + 1], out_ref.at[1 - x], 2 + 2 * number).start()
+
+    hand_over(oacc, out_o, 0)
+
+    core_rows(gproj, other, 512, 11).wait_recv()
+
+    @pl.loop(0, 4)
+    def _(t):
+        rows = rows_of(t * 256, 256)
+        grad = dot_t(gproj[rows], wo[rows_of(c * 384, 384)])
+        for p in range(3):
+            part = grad[:, p * 128 : (p + 1) * 128].astype(BF)
+            do_s[p, rows] = part
+            product = part.astype(F32).T * ot_s[p, :, rows]
+            for h in range(2):
+                dlt[p, pl.ds(h, 1), rows] = jnp.sum(
+                    product[h * 64 : (h + 1) * 64], axis=0, keepdims=True
+                )
+
+    for p in range(3):
+        @pl.loop(0, 2)
+        def _(n):
+            lanes = pl.ds(pl.multiple_of(n * 384, 128), 384)
+            b_s[0, rows_of(n * 384 + p * 128, 128)] = dot(
+                ot_s[p].astype(BF), gproj[:, lanes]
+            ).astype(BF)
+
+    def attend_back(p):
+        for h in range(2):
+            qm[h] = q_s[p] * keep[h]
+            dom[h] = do_s[p] * keep[h]
+        dqt[...] = jnp.zeros_like(dqt)
+
+        @pl.loop(0, 4)
+        def _(t):
+            rows = rows_of(t * 256, 256)
+            keys, values = k_s[p, rows], v_s[p, rows]
+            dv, dk = None, None
+            for h in range(2):
+                probs = jnp.exp(dot_t(keys, qm[h]) - lse[p, pl.ds(h, 1), :])
+                grads = dot_t(values, dom[h])
+                ds = (probs * (grads - dlt[p, pl.ds(h, 1), :])).astype(BF)
+                dv_h = dot(probs.astype(BF), dom[h])
+                dk_h = dot(ds, qm[h])
+                dv = dv_h if dv is None else dv + dv_h
+                dk = dk_h if dk is None else dk + dk_h
+                dqt[pl.ds(h * 64, 64)] += dot(kt_s[p, pl.ds(h * 64, 64), rows], ds)
+            cos_t, sin_t = cos_v[rows], sin_v[rows]
+            gq[rows, pl.ds(128, 128)] = (dk * cos_t - swap_halves(dk) * sin_t).astype(BF)
+            gq[rows, pl.ds(256, 128)] = dv.astype(BF)
+
+        @pl.loop(0, 4)
+        def _(t):
+            rows = rows_of(t * 256, 256)
+            block = dqt[:, rows] * 0.125
+            cos_t, sin_t = cost[:, rows], sint[:, rows]
+            parts = []
+            for h in range(2):
+                u, w = block[h * 64 : h * 64 + 32], block[h * 64 + 32 : h * 64 + 64]
+                parts += [u * cos_t + w * sin_t, w * cos_t - u * sin_t]
+            gq[rows, pl.ds(0, 128)] = jnp.concatenate(parts, axis=0).T.astype(BF)
+
+        @pl.loop(0, 3)
+        def _(r):
+            rows = rows_of(r * 256, 256)
+            b_s[1 + p, rows] = dot(ait[rows], gq[...]).astype(BF)
+
+        @pl.loop(0, 4)
+        def _(t):
+            rows = rows_of(t * 256, 256)
+            part = dot_t(gq[rows], wq[p])
+            if p == 0:
+                gacc[rows] = part
+            else:
+                gacc[rows] += part
+
+    for p in range(3):
+        attend_back(p)
+        if p == 0:
+            take_over(out_o, 0)
+    remote(gsend, grecv, 9, TO_CORE).wait_send()
+
+    b_out = local(b_s, b_o, 6)
+    b_out.start()
+
+    @pl.loop(0, 512 // TILE)
+    def _(i):
+        gsend[rows_of(i * TILE, TILE)] = gacc[rows_of(other + i * TILE, TILE)].astype(BF)
+
+    remote(gsend, grecv, 14, TO_CORE).start()
+    remote(gsend, grecv, 14, TO_CORE).wait_recv()
+
+    @pl.loop(0, 512 // TILE)
+    def _(i):
+        tile = rows_of(i * TILE, TILE)
+        near = rows_of(own + i * TILE, TILE)
+        grad = gacc[near] + grecv[tile].astype(F32)
+        normed = n1[tile]
+        vec[0:1] += jnp.sum(grad, axis=0, keepdims=True)
+        vec[1:2] += jnp.sum(grad * normed, axis=0, keepdims=True)
+        gacc[near] = gm[tile] + norm_back(grad * mul_one, normed, i1[tile])
+
+    hand_over(gacc, gin_o, 1)
+    sums = vec[...]
+    vec[6:7] = sums[1:2] * (1.0 + scale_one)
+    vec[7:8] = sums[4:5] * (1.0 + scale_two)
+    vec[1:2] = sums[1:2] * again[...]
+    vec[4:5] = sums[4:5] * fgain[...]
+    take_over(gin_o, 1)
+    v_out = local(vec, vec_o, 7)
+    v_out.start()
+    u_out = local(ubg, ubg_o, 8)
+    u_out.start()
+
+    v_out.wait()
+    u_out.wait()
+    g_out.wait()
+    b_out.wait()
+    for number, ref in ((0, out_o), (1, gin_o)):
+        local(fst.at[2 * number], ref.at[x], 1 + 2 * number).wait()
+        local(fst.at[2 * number + 1], ref.at[1 - x], 2 + 2 * number).wait()
+        remote(xs.at[number], xr.at[number], 12 + number, TO_X).wait_send()
+    swap_x.wait_send()
+    swap_c.wait_send()
+    core_rows(ai, own + x * 256, 256, 2).wait_send()
+    core_rows(ai, own + (1 - x) * 256, 256, 3).wait_send()
+    for p in range(3):
+        att_copy(p, False).wait_send()
+    core_rows(fi, own, 512, 8).wait_send()
+    remote(osend, orecv, 10, TO_CORE).wait_send()
+    core_rows(gproj, own, 512, 11).wait_send()
+    remote(gsend, grecv, 14, TO_CORE).wait_send()
+
+    @pl.when(z < Z - 1)
+    def _():
+        for item in z_copies(z, 0, RIGHT, False):
+            item.wait_send()
+
+    @pl.when(z > 0)
+    def _():
+        for item in z_copies(z, 1, LEFT, False):
+            item.wait_send()
+
+    @pl.loop(1, Z)
+    def _(k):
+        @pl.when(z - k >= 0)
+        def _():
+            @pl.when(z < Z - 1)
+            def _():
+                for item in z_copies(z - k, 0, RIGHT, False):
+                    item.wait_send()
+
+            for item in y_copies(z - k, grp):
+                item.wait_send()
+
+        @pl.when(z + k <= Z - 1)
+        def _():
+            @pl.when(z > 0)
+            def _():
+                for item in z_copies(z + k, 1, LEFT, False):
+                    item.wait_send()
+
+            for item in y_copies(z + k, grp):
+                item.wait_send()
+
+
+def tables(seg_len, seq_size):
+    half = np.arange(32)
+    frequency = 10000.0 ** (-2.0 * half / 64)
+    core, chip, token = np.meshgrid(
+        np.arange(2), np.arange(seq_size // 2), np.arange(seg_len), indexing="ij"
+    )
+    place = ((chip * 2 + core) * seg_len + token).reshape(-1)
+    angle = place[:, None] * frequency[None, :]
+    cos, sin = np.cos(angle).astype(np.float32), np.sin(angle).astype(np.float32)
+    return (
+        np.tile(cos, (1, 4)),
+        np.concatenate([-sin, sin, -sin, sin], axis=1),
+        np.ascontiguousarray(cos.T),
+        np.ascontiguousarray(sin.T),
+    )
+
+
+def fast_shards(
+    inputs, condition, attn_gain, ada_weight, ada_bias, qkv_weight, out_weight, ffn_gain,
+    up_weight, up_bias, down_weight, down_bias, cotangent,
+):
+    Z = lax.axis_size("mlp")
+    tabs = [jnp.asarray(t) for t in tables(inputs.shape[1], lax.axis_size("seq"))]
+    hbm, vm = pl.BlockSpec(memory_space=pl.ANY), pl.BlockSpec(memory_space=pltpu.VMEM)
+    shape = jax.ShapeDtypeStruct
+    row = lambda v: v.reshape(1, -1)
+    V = pltpu.VMEM
+    dma = pltpu.SemaphoreType.DMA
+    scratch = [
+        V((128, 4608), BF), V((3, 768, 384), BF), V((768, 768), BF), V((Z, 768, 384), BF),
+        V((Z, 384, 768), BF), V((Z, 1, 768), F32), V((1024, 128), F32), V((1024, 128), F32),
+        V((32, 1024), F32), V((32, 1024), F32),
+        V((512, 768), BF), V((512, 768), BF), V((2, 4608), F32), V((512, 768), F32), V((512, 1), F32),
+        V((1024, 768), BF), V((768, 1024), BF),
+        V((3, 1024, 128), BF), V((3, 1024, 128), BF), V((3, 1024, 128), BF),
+        V((3, 128, 1024), BF), V((3, 128, 1024), BF), V((3, 128, 1024), F32), V((3, 2, 1024), F32),
+        V((512, 768), BF), V((512, 384), BF),
+        V((512, 768), F32), V((512, 768), F32), V((512, 1), F32),
+        V((1024, 768), BF), V((768, 1024), BF), V((1024, 768), BF), V((768, 1024), BF),
+        V((1024, 768), F32), V((1024, 768), F32), V((1024, 384), BF), V((1024, 384), BF),
+        V((2, Z, 768, 384), BF), V((512, 768), BF), V((512, 768), BF), V((512, 768), BF), V((512, 768), BF),
+        V((512, 768), F32), V((3, 1024, 128), BF), V((3, 2, 1024), F32),
+        V((2, 1024, 128), BF), V((2, 1024, 128), BF), V((128, 1024), F32), V((1024, 384), BF),
+        V((4, 768, 384), BF), V((2, 256, 768), BF), V((2, 256, 768), BF), V((4, 256, 768), F32),
+        V((16, 768), F32), V((Z, 1, 384), F32),
+        dma((20,)), dma((16,)), dma((16,)), dma((2, Z, 3)), dma((2, Z, 3)), dma((Z, 2)), dma((Z, 2)),
+    ]
+    token = shape(inputs.shape, F32)
+    out, gin, g, b, vec, ubg = pl.pallas_call(
+        functools.partial(fast_kernel, Z),
+        out_shape=[
+            token, token, shape((2, Z, 768, 384), BF), shape((4, 768, 384), BF),
+            shape((16, 768), F32), shape((Z, 1, 384), F32),
+        ],
+        in_specs=[hbm, vm, vm, hbm, vm, hbm, hbm, vm, hbm, vm, hbm, vm, hbm, hbm, hbm, hbm, hbm],
+        out_specs=[hbm] * 6,
+        scratch_shapes=scratch,
+        compiler_params=pltpu.CompilerParams(
+            collective_id=0, has_side_effects=True, vmem_limit_bytes=VMEM_LIMIT
+        ),
+        name="block",
+    )(
+        inputs, condition, row(attn_gain), ada_weight, row(ada_bias), qkv_weight, out_weight,
+        row(ffn_gain), up_weight, row(up_bias), down_weight, row(down_bias), cotangent, *tabs,
+    )
+    g = lax.psum_scatter(g, "mlp", scatter_dimension=1, tiled=True)
+    g = lax.all_gather(g, "seq").astype(F32)[:, :, 0]
+    g = g[:2] + g[2:]
+    grad_up = jnp.concatenate([g[0, 0], g[1, 0]], axis=-1)
+    grad_down = jnp.concatenate([g[0, 1], g[1, 1]], axis=-1).T
+    b = lax.all_gather(lax.psum(b, "mlp"), "seq").astype(F32)
+    b = b[:2] + b[2:]
+    grad_out = b[:, 0].reshape(2, 2, 384, 384).transpose(0, 2, 1, 3).reshape(768, 768)
+    grad_qkv = b[:, 1:].reshape(2, 3, 768, 3, 128).transpose(2, 3, 0, 1, 4).reshape(768, 2304)
+    vec = lax.all_gather(lax.all_gather(vec, "seq"), "mlp")
+    vec = vec.reshape(Z, 2, 2, 16, 768).sum(axis=2)
+    dmod = vec[:, :, :6].reshape(2 * Z, 4608)
+    cond = lax.all_gather(condition, "mlp", tiled=True).astype(F32)
+    high = lax.Precision.HIGHEST
+    grad_ada = jnp.dot(cond.T, dmod, precision=high)
+    mine = lax.dynamic_slice_in_dim(dmod, lax.axis_index("mlp") * 2, 2, 0)
+    grad_cond = jnp.dot(mine, ada_weight.astype(F32).T, precision=high)
+    tail = vec[:, :, 6:9].sum(axis=(0, 1))
+    ubg = lax.all_gather(lax.all_gather(ubg[:, 0], "seq"), "mlp").reshape(Z, 2, 2, Z, 384).sum(axis=(0, 1))
+    grad_ub = lax.dynamic_index_in_dim(ubg, lax.axis_index("mlp"), 1, False).reshape(-1)
+    return (
+        out, gin, grad_cond, tail[0], grad_ada, dmod.sum(axis=0), grad_qkv, grad_out, tail[1],
+        grad_up, grad_ub, grad_down, tail[2],
+    )
+
+
 def solution(mesh):
     placed = (
         P(("grp", "mlp"), "seq", None),
@@ -367,8 +1099,10 @@
         P(),
         P(("grp", "mlp"), "seq", None),
     )
+    sizes = dict(mesh.shape)
+    small = sizes["seq"] == 4 and sizes["grp"] == 2 and sizes["mlp"] == 4
     return jax.shard_map(
-        shards,
+        fast_shards if small else shards,
         mesh=mesh,
         in_specs=placed,
         out_specs=(

time: 865 us -> 586 us (0.68)
  waiting for transfers between devices: 479 us -> 274 us
  Pallas kernels: 0 us -> 149 us
  matrix products: 152 us -> 4.51 us
  other arithmetic: 63 us -> 33.3 us
  blocking collectives: 72.3 us -> 51.4 us
  local copies, waits for them, and re-layouts: 76.2 us -> 58.2 us
    pallas_call x0 -> x1, Pallas kernels: none -> 149 us  [fast_shards(): pl.pallas_call(functools.partial(fast_kernel, Z), out_shape=[token, token...]
    dot_general x33 -> x2, matrix products: 152 us -> 4.51 us  [the longest x1 2.5 us: fast_shards(): grad_cond = jnp.dot(mine, ada_weight.astype(F32).T, precision=high)]
    reduce_scatter x3 -> x0, waiting for transfers between devices: 146 us -> none  [the longest x1 58 us: shards(): lax.psum_scatter(jnp.dot(act_low, down_weight, preferred_element_type=jnp...]
    all_gather x3 -> x2, waiting for transfers between devices: 166 us -> 26.3 us  [the longest x1 26.3 us: fast_shards(): b = lax.all_gather(lax.psum(b, 'mlp'), 'seq').astype(F32)]
    psum x2 -> x1, waiting for transfers between devices: 166 us -> 247 us  [fast_shards(): b = lax.all_gather(lax.psum(b, 'mlp'), 'seq').astype(F32)]
    psum x2 -> x0, blocking collectives: 72.3 us -> none  [the longest x1 65.5 us: shards(): lax.psum((qkv_part, out_part, ada_weight_part, ada_bias_part, gain_one_pa...]
    all_gather x0 -> x5, blocking collectives: none -> 51.4 us  [the longest x2 23.3 us: fast_shards(): vec = lax.all_gather(lax.all_gather(vec, 'seq'), 'mlp')]
    reduce_sum x10 -> x5, other arithmetic: 23.2 us -> 1.74 us  [the longest x1 1.03 us: fast_shards(): tail = vec[:, :, 6:9].sum(axis=(0, 1))]
  transfers between devices with their start and end apart: 8 -> 3, of which waited for: 8 -> 2; matrix products, arithmetic and copies ran while one was open for 11% -> 4% of each run, Pallas kernels for 0% -> 0%
where the time goes in v1:
time: 586 us; the launch traced here: 584 us
  waiting for transfers between devices  274 us (47%)
  Pallas kernels  149 us (25%)
  local copies, waits for them, and re-layouts  58.2 us (10%)
  blocking collectives  51.4 us (9%)
  other arithmetic  33.3 us (6%)
  between operations  13.9 us (2%)
    psum x1, waiting for transfers between devices, fast_shards(): b = lax.all_gather(lax.psum(b, 'mlp'), 'seq').astype(F32)  247 us
    pallas_call x1, Pallas kernels, fast_shards(): pl.pallas_call(functools.partial(fast_kernel, Z), out_shape=[token, token...  149 us
    all_gather x1, waiting for transfers between devices, fast_shards(): b = lax.all_gather(lax.psum(b, 'mlp'), 'seq').astype(F32)  26.3 us
    all_gather x2, blocking collectives, fast_shards(): vec = lax.all_gather(lax.all_gather(vec, 'seq'), 'mlp')  23.3 us
    unnamed x32, local copies, waits for them, and re-layouts  22.5 us
    all_gather x1, blocking collectives, fast_shards(): lax.all_gather(lax.all_gather(ubg[:, 0], 'seq'), 'mlp')  13.2 us
    all_gather x1, local copies, waits for them, and re-layouts, fast_shards(): b = lax.all_gather(lax.psum(b, 'mlp'), 'seq').astype(F32)  12.7 us
    convert_element_type x1, other arithmetic, fast_shards(): b = lax.all_gather(lax.psum(b, 'mlp'), 'seq').astype(F32)  12.3 us
  transfers between devices with their start and end apart: 3, of which 2 were waited for; matrix products, arithmetic and copies ran while one was open for 4% of the time, Pallas kernels for 0%

profile of v1, /device:TPU:0, one launch (start us, length us, event | category | flops | bytes accessed | tf_op | source)
XLA Modules:
  0.0 584.4 jit_solution(1252532115452100196)
XLA Ops:
  7.2 1.3 reshape.67.adab
  8.6 1.3 reshape.66.again
  9.8 1.3 reshape.68.fgain
  11.1 1.3 reshape.69.upb
  13.6 149.3 %block.1 = (f32[2,256,768]{2,1,0:T(8,128)}, f32[2,256,768]{2,1,0:T(8,128)}, bf16[2,4,768,384]{3,2,1,0:T(8,128)(2,1)}, bf16[4,768,384]{2,1,0:T(8,128)(2,1)}, f32[16,768]{1,0:T(8,128)}, /*index=5*/f32[4,1,384]{2,1,0:T(1,128)}) custom-call(bf16[2,256,768]{2,1,0:T(8,128)(2,1)} %inputs.1, bf16[2,128]{1,0:T(2,128)(2,1)} %cond.1, f32[1,768]{1,0:T(1,128)} %reshape.66.again, ...), custom_call_target="tpu_custom_call" | custom-call | tf_op jit(solution)/shard_map/block/pallas_call | solution.py:1043
  164.2 246.6 %all-reduce.4.cloned.1.call-done = (bf16[1,4,768,384]{3,2,1,0:T(8,128)(2,1)}, bf16[2,4,768,384]{3,2,1,0:T(8,128)(2,1)}) async-done(((bf16[1,4,768,384]{3,2,1,0:T(8,128)(2,1)}, bf16[2,4,768,384]{3,2,1,0:T(8,128)(2,1)}), (bf16[1,4,768,384]{3,2,1,0:T(8,128)(2,1)}, bf16[2,4,768,384]{3,2,1,0:T(8,128)(2,1)})) %all-reduce.4.cloned.1.call-update) | async-done | bytes 7077904 | tf_op jit(solution)/shard_map/psum | solution.py:1065
  410.9 3.1 constant_dynamic-slice_fusion
  414.7 5.6 all-gather
  420.3 17.7 %all-gather.1 = f32[16,16,768]{2,1,0:T(8,128)S(1)} all-gather(f32[4,16,768]{2,1,0:T(8,128)S(1)} %bitcast.54), channel_id=3, replica_groups=mesh['grp'=2,'seq'=4,'mlp'=4] {'mlp'}, dimensions={0}, use_global_device_ids=true | all-gather | bytes 983040 | tf_op jit(solution)/shard_map/all_gather | solution.py:1069
  439.6 5.3 all-gather.3
  444.9 13.2 %all-gather.4 = f32[16,4,384]{2,1,0:T(4,128)S(1)} all-gather(f32[4,4,384]{2,1,0:T(4,128)S(1)} %reshape.80), channel_id=6, replica_groups=mesh['grp'=2,'seq'=4,'mlp'=4] {'mlp'}, dimensions={0}, use_global_device_ids=true | all-gather | bytes 122880 | tf_op jit(solution)/shard_map/all_gather | solution.py:1078
  458.8 9.5 %all-gather.5 = bf16[4,2,128]{2,1,0:T(2,128)(2,1)S(1)} all-gather(bf16[1,2,128]{2,1,0:T(2,128)(2,1)S(1)} %bitcast.60), channel_id=1, replica_groups=mesh['grp'=2,'seq'=4,'mlp'=4] {'mlp'}, dimensions={0}, use_global_device_ids=true | all-gather | bytes 2560 | tf_op jit(solution)/shard_map/all_gather | solution.py:1072
  468.4 2.0 convolution_bitcast_fusion
  470.4 2.2 copy.54
  472.6 1.3 reduce_sum.48
  475.6 2.5 fusion
  478.1 3.0 convert_element_type.10
  481.5 1.3 fusion.3
  482.8 1.4 copy.59
  484.2 1.4 copy.60
  485.6 2.9 maximum_bitcast_fusion
  488.5 1.6 pad_maximum_fusion
  490.1 26.3 %all-gather.9.cloned.1.call-done = bf16[4,4,768,384]{3,2,1,0:T(8,128)(2,1)} async-done(((bf16[1,4,768,384]{3,2,1,0:T(8,128)(2,1)}), bf16[4,4,768,384]{3,2,1,0:T(8,128)(2,1)}) %all-gather.9.cloned.1.call-update) | async-done | bytes 9437200 | tf_op jit(solution)/shard_map/all_gather | solution.py:1065
  516.4 12.7 %copy.49 = bf16[4,4,768,384]{2,3,1,0:T(8,128)(2,1)} copy(bf16[4,4,768,384]{3,2,1,0:T(8,128)(2,1)} %all-gather.9.cloned.1.call-done) | data formatting | bytes 18874368 | tf_op jit(solution)/shard_map/all_gather | solution.py:1065
  529.1 12.3 %convert_element_type.8 = f32[4,4,768,384]{2,3,1,0:T(8,128)} convert(bf16[4,4,768,384]{2,3,1,0:T(8,128)(2,1)} %copy.49) | non-fusion elementwise | flops 4718592 | bytes 28311552 | tf_op jit(solution)/shard_map/convert_element_type | solution.py:1065
  541.4 11.3 %slice_add_fusion = f32[2,4,768,384]{2,3,1,0:T(8,128)} fusion(f32[4,4,768,384]{2,3,1,0:T(8,128)} %convert_element_type.8), kind=kLoop, calls=%fused_computation | loop fusion | flops 2359296 | bytes 28311552 | tf_op jit(solution)/shard_map/add | solution.py:1066
  552.7 3.1 slice-done
  555.8 3.4 copy.50
  559.2 8.1 %copy.55 = f32[768,2304]{1,0:T(8,128)} copy(f32[768,2304]{0,1:T(8,128)} %bitcast.45) | data formatting | bytes 14155776
  567.3 2.3 reshape_squeeze.3
  569.6 3.9 copy.51
  573.5 1.6 copy.62
  (48 shorter events, 10.5 us)
Async XLA Ops:
  7.2 403.7 %all-reduce.4.cloned.1.call-start = ((), (), s32[]{:S(2)}) async-start(), calls=%async_computation.2 | async-start | bytes 14155776 | tf_op jit(solution)/shard_map/psum | solution.py:1065
  163.0 0.7 copy-start.10
  163.0 315.1 %all-gather.11.cloned.1.call-start = ((), (), s32[]{:S(2)}) async-start(), calls=%async_computation.1 | async-start | bytes 5898240 | tf_op jit(solution)/shard_map/all_gather | solution.py:1061
  413.9 0.8 copy-start.7
  413.9 102.5 %all-gather.9.cloned.1.call-start = ((), (), s32[]{:S(2)}) async-start(), calls=%async_computation | async-start | bytes 11796480 | tf_op jit(solution)/shard_map/all_gather | solution.py:1065
  414.0 25.6 %copy-start.8 = (f32[4,1,384]{2,1,0:T(1,128)S(1)}, f32[4,1,384]{2,1,0:T(1,128)}, u32[]{:S(2)}) copy-start(f32[4,1,384]{2,1,0:T(1,128)} %get-tuple-element.24) | copy-start | bytes 18436
  414.7 44.2 %copy-start.9 = (bf16[2,128]{1,0:T(2,128)(2,1)S(1)}, bf16[2,128]{1,0:T(2,128)(2,1)}, u32[]{:S(2)}) copy-start(bf16[2,128]{1,0:T(2,128)(2,1)} %cond.1) | copy-start | bytes 1540
  438.1 0.7 copy-start.5
  439.5 28.8 %copy-start.6 = (f32[1,8,6,768]{3,1,2,0:T(8,128)}, f32[1,8,6,768]{3,1,2,0:T(8,128)S(1)}, u32[]{:S(2)}) copy-start(f32[1,8,6,768]{3,1,2,0:T(8,128)S(1)} %copy.61) | copy-start | bytes 442372
  470.4 5.2 copy-start
  484.2 1.4 copy-start.2
  485.6 2.9 copy-start.1
  552.7 3.1 slice-start
  559.2 8.1 %slice-start.1 = ((f32[2,4,768,384]{2,3,1,0:T(8,128)}), f32[2,1,768,384]{2,3,1,0:T(8,128)S(1)}, s32[]{:S(2)}) async-start(f32[2,4,768,384]{2,3,1,0:T(8,128)} %slice_add_fusion), calls=%async_computation.4 | async-start | bytes 4718592 | tf_op jit(solution)/shard_map/slice | solution.py:1067
  573.5 2.1 copy-start.4
  575.1 1.7 copy-start.3
Sparse Core Ops, SparseCore 0:
  163.1 247.6 all-reduce.3
  414.1 36.4 all-gather.10
  452.2 64.2 all-gather.8

commit v2 on v1

--- a/solution.py
+++ b/solution.py
@@ -388,17 +388,17 @@
 
 
 def fast_kernel(
-    chain,
     inputs, cond, again, adaw_h, adab, qkv_h, outw_h, fgain, up_h, upb, down_h, downb, cot_h,
     cos_h, sin_h, cost_h, sint_h,
-    out_o, gin_o, g_o, b_o, vec_o, ubg_o,
+    out_o, gin_o, cond_o, adaw_o, small_o, qkv_o, outw_o, ffn_o,
     adaw, wq, wo, wu, wd, ub, cos_v, sin_v, cost, sint,
     xb, ctb, mod2, n1, i1, ai, ait, q_s, k_s, v_s, kt_s, vt_s, ot_s, lse, att, att_s,
-    ap, n2, i2, fi, fit, gf, gft, oacc, gacc, a_s, gp_s, g_s, osend, orecv, gsend, grecv,
-    gm, do_s, dlt, qm, dom, dqt, gq, b_s, xs, xr, fst, vec, ubg,
-    lsem, ssem, rsem, wss, wrs, yss, yrs,
+    ap, n2, i2, fit, gf, gft, oacc, gacc, a_s, gp_s, g_s, grecv,
+    gm, do_s, dlt, dqt, gq, b_s, xs, vec, vecr, vall, ubg, cstage, sstage,
+    rx, rz, fxr, rxb, fb,
+    lsem, ssem, rsem, wss, wrs, yss, yrs, fss, frs, bss, brs, hss, hrs, vss, vrs, credit,
 ):
-    Z = chain
+    Z = 4
     grp = lax.axis_index("grp")
     seq = lax.axis_index("seq")
     z = lax.axis_index("mlp")
@@ -435,26 +435,24 @@
             )
     loads.append(local(outw_h, wo, 15))
     loads.append(local(up_h.at[:, half], wu.at[z], 16))
-    loads.append(local(down_h.at[rows_of(c * 384, 384)], wd.at[z], 17))
+    for n in range(2):
+        loads.append(
+            local(
+                down_h.at[rows_of(c * 384, 384), pl.ds(n * 384, 384)],
+                wd.at[z, pl.ds(n * 384, 384)],
+                17 + 3 * n,
+            )
+        )
     loads.append(local(cot_h.at[x], ctb.at[rows_of(x * 256, 256)], 18))
     loads.append(local(upb, ub.at[z], 19))
     for item in loads:
         item.start()
 
     barrier = pltpu.get_barrier_semaphore()
-    for device in (TO_CORE, TO_X, TO_Y):
+    peers = [{"seq": (x ^ dx) * 2 + c, "mlp": z ^ dz} for dx in range(2) for dz in range(Z) if dx or dz]
+    for device in [TO_CORE, TO_Y] + peers:
         pl.semaphore_signal(barrier, 1, device_id=device, device_id_type=MESH)
-
-    @pl.when(z > 0)
-    def _():
-        pl.semaphore_signal(barrier, 1, device_id=LEFT, device_id_type=MESH)
-
-    @pl.when(z < Z - 1)
-    def _():
-        pl.semaphore_signal(barrier, 1, device_id=RIGHT, device_id_type=MESH)
-
-    ends = jnp.where(z > 0, 1, 0) + jnp.where(z < Z - 1, 1, 0)
-    pl.semaphore_wait(barrier, 3 + ends)
+    pl.semaphore_wait(barrier, 2 + len(peers))
 
     swap_x = remote(inputs.at[1 - x], xb.at[rows_of(x * 256, 256)], 0, TO_X)
     swap_x.start()
@@ -464,14 +462,15 @@
     def up_half(ref, which):
         return ref.at[rows_of(which * 384, 384)]
 
-    def down_half(ref, which):
-        return ref.at[rows_of(which * 192, 192)]
+    down_half = up_half
 
     def z_copies(j, way, device, first):
         if first:
             src = (
                 up_h.at[rows_of(grp * 384, 384), half],
-                down_h.at[rows_of(c * 384 + grp * 192, 192)],
+                down_h.at[
+                    rows_of(c * 384, 384), pl.ds(pl.multiple_of(grp * 384, 128), 384)
+                ],
                 upb,
             )
         else:
@@ -530,6 +529,248 @@
                 start_all(z_copies(j, 1, LEFT, False))
 
             start_all(y_copies(j, grp))
+
+    orders = ((1, 2, 3, 0), (0, 2, 3, 1), (3, 1, 0, 2), (2, 1, 0, 3))
+
+    def order(n):
+        return pick([orders[a][n] for a in range(Z)], z)
+
+    pending = []
+
+    def act(places, body, sends=()):
+        for place in places:
+            @pl.when(z == place)
+            def _(place=place):
+                body(place)
+                for make in sends:
+                    make(place).start()
+
+            pending.extend((place, make) for make in sends)
+
+    EVERY = (0, 1, 2, 3)
+
+    def ffn_copy(j):
+        return pltpu.make_async_remote_copy(
+            src_ref=g_s.at[1 - x, j], dst_ref=rx.at[j], send_sem=hss.at[j], recv_sem=hrs.at[j],
+            device_id=TO_X, device_id_type=MESH,
+        )
+
+    def add_rows(ref, others):
+        @pl.loop(0, 6)
+        def _(i):
+            rows = rows_of(i * 128, 128)
+            total = ref[rows].astype(F32)
+            for other_ref in others:
+                total = total + other_ref[rows].astype(F32)
+            ref[rows] = total.astype(BF)
+
+    def z_send(n, place):
+        j = orders[place][n]
+        end = place in (0, 3)
+        adjacent_end = 0 if place == 1 else 3
+        if end:
+            target, slot = (1 if place == 0 else 2), j
+        elif j == adjacent_end:
+            target, slot = j, place
+        elif j in (0, 3):
+            target, slot = j, place
+        else:
+            target, slot = j, (0 if j == 1 else 3)
+        return pltpu.make_async_remote_copy(
+            src_ref=g_s.at[x, j], dst_ref=rz.at[slot], send_sem=fss.at[n], recv_sem=frs.at[slot],
+            device_id={"mlp": target}, device_id_type=MESH,
+        )
+
+    def z_wait(slot):
+        pltpu.make_async_remote_copy(
+            src_ref=rz.at[slot], dst_ref=rz.at[slot], send_sem=fss.at[0], recv_sem=frs.at[slot],
+            device_id=LEFT, device_id_type=MESH,
+        ).wait_recv()
+
+    def ffn_x(n):
+        j = order(n)
+        ffn_copy(j).wait_recv()
+        add_rows(g_s.at[x, j], [rx.at[j]])
+        if n < 3:
+            places = EVERY if n == 0 else (0, 3)
+            act(places, lambda place: None, [lambda place: z_send(n, place)])
+
+    def ffn_z(n):
+        def body(place):
+            j = orders[place][n]
+            z_wait(j)
+            add_rows(g_s.at[x, j], [rz.at[j]])
+
+        act((1, 2), body, [lambda place: z_send(n, place)])
+
+    def final_copies(src, kind, first):
+        lanes = pl.ds(pl.multiple_of(c * 384, 128), 384)
+        return [
+            local(src, ffn_o.at[kind, :, lanes], 21 + first),
+            remote(src, ffn_o.at[kind, :, lanes], 16 + first, TO_CORE),
+        ]
+
+    def ffn_own():
+        def body(place):
+            slots = {0: (1, 2), 3: (1, 2), 1: (1, 0), 2: (2, 3)}[place]
+            for slot in slots:
+                z_wait(slot)
+            add_rows(g_s.at[x, place], [rz.at[slot] for slot in slots])
+
+        act(EVERY, body)
+        remote(g_s.at[x, z], fxr, 15, TO_X).start()
+        for item in final_copies(g_s.at[x, z], x, 0):
+            item.start()
+
+    def ffn_last():
+        remote(g_s.at[x, z], fxr, 15, TO_X).wait_recv()
+        for item in final_copies(fxr, 1 - x, 1):
+            item.start()
+
+    def quarter(ref, p, q):
+        return ref.at[p, pl.ds(q * 192, 192)]
+
+    def hop(kind, p, q, place):
+        step = 1 if kind in (0, 2) else -1
+        src = quarter(b_s if kind < 2 else fb, p, q)
+        dst = quarter((wu, wd, fb, fb)[kind], p, q)
+        return pltpu.make_async_remote_copy(
+            src_ref=src, dst_ref=dst, send_sem=bss.at[kind, p, q], recv_sem=brs.at[kind, p, q],
+            device_id={"mlp": place + step}, device_id_type=MESH,
+        )
+
+    def hop_wait(kind, p, q):
+        dst = quarter((wu, wd, fb, fb)[kind], p, q)
+        pltpu.make_async_remote_copy(
+            src_ref=dst, dst_ref=dst, send_sem=bss.at[kind, p, q], recv_sem=brs.at[kind, p, q],
+            device_id=LEFT, device_id_type=MESH,
+        ).wait_recv()
+
+    def hops(kind, p, *qs):
+        return [lambda place, q=q: hop(kind, p, q, place) for q in qs]
+
+    def add_quarter(p, q, refs):
+        total = quarter(b_s, p, q)[...].astype(F32)
+        for ref in refs:
+            total = total + quarter(ref, p, q)[...].astype(F32)
+        quarter(b_s, p, q)[...] = total.astype(BF)
+
+    def sum_0(p):
+        act((0,), lambda place: None, hops(0, p, 3, 2, 1))
+        act((3,), lambda place: None, hops(1, p, 0, 1, 2))
+
+    def relay(kind, p, q):
+        hop_wait(kind, p, q)
+        add_quarter(p, q, [wu if kind == 0 else wd])
+
+    def sum_1(p):
+        act((1,), lambda place: relay(0, p, 3), hops(0, p, 3))
+        act((2,), lambda place: relay(1, p, 0), hops(1, p, 0))
+        act((1,), lambda place: relay(0, p, 2), hops(0, p, 2))
+        act((2,), lambda place: relay(1, p, 1), hops(1, p, 1))
+
+    def sum_2(p):
+        act((2,), lambda place: relay(0, p, 3), hops(0, p, 3))
+        act((1,), lambda place: relay(1, p, 0), hops(1, p, 0))
+
+    def cross(p, place):
+        return pltpu.make_async_remote_copy(
+            src_ref=quarter(b_s, p, place), dst_ref=rxb.at[p], send_sem=hss.at[4 + p],
+            recv_sem=hrs.at[4 + p], device_id=TO_X, device_id_type=MESH,
+        )
+
+    def sum_3(p):
+        def body(place):
+            refs = []
+            if place > 0:
+                hop_wait(0, p, place)
+                refs.append(wu)
+            if place < 3:
+                hop_wait(1, p, place)
+                refs.append(wd)
+            add_quarter(p, place, refs)
+
+        act(EVERY, body, [lambda place: cross(p, place)])
+
+    def sum_4(p):
+        def body(place):
+            cross(p, place).wait_recv()
+            total = quarter(b_s, p, place)[...].astype(F32) + rxb[p].astype(F32)
+            quarter(fb, p, place)[...] = total.astype(BF)
+
+        for place in EVERY:
+            sends = hops(2, p, place) if place < 3 else []
+            sends += hops(3, p, place) if place > 0 else []
+            act((place,), body, sends)
+
+    def sum_5(p):
+        act((1,), lambda place: hop_wait(2, p, 0), hops(2, p, 0))
+        act((2,), lambda place: hop_wait(3, p, 3), hops(3, p, 3))
+        act((1,), lambda place: hop_wait(3, p, 2), hops(3, p, 2))
+        act((2,), lambda place: hop_wait(2, p, 1), hops(2, p, 1))
+
+    def sum_6(p):
+        act((1,), lambda place: hop_wait(3, p, 3), hops(3, p, 3))
+        act((2,), lambda place: hop_wait(2, p, 0), hops(2, p, 0))
+
+    def piece_copies(p):
+        if p == 0:
+            pairs = [
+                (fb.at[0, pl.ds(n * 384, 384)], outw_o.at[rows_of(c * 384, 384), pl.ds(n * 384, 384)])
+                for n in range(2)
+            ]
+        else:
+            pairs = [
+                (
+                    fb.at[p, :, pl.ds(part * 128, 128)],
+                    qkv_o.at[
+                        :, pl.ds(pl.multiple_of(part * D + c * 384 + (p - 1) * 128, 128), 128)
+                    ],
+                )
+                for part in range(3)
+            ]
+        copies = []
+        for n, (src, dst) in enumerate(pairs):
+            copies.append(local(src, dst, 23 + p * 3 + n))
+            copies.append(remote(src, dst, 18 + p * 3 + n, TO_CORE))
+        return copies
+
+    def sum_7(p):
+        def body(place):
+            for q in range(4):
+                if place == 0 and q > 0:
+                    hop_wait(3, p, q)
+                if place == 3 and q < 3:
+                    hop_wait(2, p, q)
+
+        act((0, 3), body)
+        for item in piece_copies(p):
+            item.start()
+
+    plan = {
+        0: [],
+        1: [lambda: ffn_x(1)],
+        2: [lambda: sum_1(0)],
+        3: [lambda: ffn_z(1)],
+        4: [lambda: ffn_x(2), lambda: sum_2(0)],
+        5: [lambda: sum_3(0), lambda: sum_1(1)],
+        6: [lambda: ffn_z(2)],
+        7: [lambda: ffn_x(3), lambda: sum_4(0), lambda: sum_2(1), lambda: out_copies(out_o, 0)[1].start()],
+        8: [lambda: sum_5(0), lambda: sum_3(1), lambda: sum_1(2)],
+        9: [],
+        10: [lambda: sum_6(0), lambda: sum_4(1), lambda: sum_2(2)],
+        11: [lambda: sum_7(0), lambda: sum_5(1), lambda: sum_3(2), lambda: sum_1(3), lambda: ffn_own()],
+        12: [lambda: sum_6(1), lambda: sum_4(2), lambda: sum_2(3)],
+        13: [lambda: sum_7(1), lambda: sum_5(2), lambda: sum_3(3)],
+        14: [
+            lambda: sum_6(2), lambda: sum_4(3), lambda: ffn_last(), lambda: sum_7(2),
+            lambda: sum_5(3), lambda: sum_6(3), lambda: sum_7(3),
+        ],
+    }
+
+    def slot(number):
+        for task in plan[number]:
+            task()
 
     local(adaw_h, adaw, 1).wait()
     for part in range(6):
@@ -599,9 +840,8 @@
     core_rows(ai, own + (1 - x) * 256, 256, 3).start()
     core_rows(ai, other + (1 - x) * 256, 256, 3).wait_recv()
     project_block(1 - x)
-    loads[16].wait()
-    loads[17].wait()
-    loads[19].wait()
+    for item in loads[16:19] + loads[20:]:
+        item.wait()
     weight_step(1)
 
     low_lane = lax.broadcasted_iota(jnp.int32, (1, 128), 1) < 64
@@ -649,7 +889,7 @@
     attend(1)
     weight_step(2)
 
-    loads[18].wait()
+    loads[19].wait()
     swap_c.wait_recv()
 
     @pl.loop(0, 512 // TILE)
@@ -673,6 +913,10 @@
             TO_CORE,
         ).wait_recv()
     loads[15].wait()
+
+    core_rows(ai, own + x * 256, 256, 2).wait_send()
+    core_rows(ai, own + (1 - x) * 256, 256, 3).wait_send()
+    fi = ai
 
     @pl.loop(0, 2)
     def _(b):
@@ -704,25 +948,27 @@
         rows = rows_of(t * 256, 256)
         fit[:, rows] = fi[rows].T
 
-    orders = [sorted(range(Z), key=lambda j, a=a: (abs(j - a), j)) for a in range(Z)]
     coef = 0.7978845608028654
 
     @pl.loop(0, Z)
     def _(k):
-        j = pick([pick([orders[a][n] for a in range(Z)], z) for n in range(Z)], k)
-
-        @pl.when(k >= 3)
+        j = pick([order(n) for n in range(Z)], k)
+
+        @pl.when(k == 2)
         def _():
-            weight_step(k)
-
-        @pl.when(k > 0)
+            weight_step(3)
+
+        @pl.when(k == 3)
+        def _():
+            ffn_x(0)
+
+        @pl.when(k < 3)
         def _():
             for item in y_copies(j, 1 - grp):
                 item.wait_recv()
 
         bias = ub[j][:, pl.ds(0, 384)]
         bias = jnp.where(c == 0, bias, ub[j][:, pl.ds(384, 384)])
-        up_j, down_j = wu[j], wd[j]
 
         @pl.loop(0, 4)
         def _(t):
@@ -733,20 +979,24 @@
             act = (0.5 * pre * (1.0 + th)).astype(BF)
             slope = 0.5 * (1.0 + th) + 0.5 * pre * (1.0 - th * th) * coef * (1.0 + 3.0 * 0.044715 * sq)
             a_s[rows] = act
-            grad_pre = (dot_t(gf[rows], wd[j]) * slope).astype(BF)
+            grad_act = dot_t(gf[rows, :384], wd[j, :384]) + dot_t(gf[rows, 384:], wd[j, 384:])
+            grad_pre = (grad_act * slope).astype(BF)
             gp_s[rows] = grad_pre
             bsum = jnp.sum(grad_pre.astype(F32), axis=0, keepdims=True)
-            out = dot(act, wd[j])
+            out_a = dot(act, wd[j, :384])
+            out_b = dot(act, wd[j, 384:])
             gin = dot_t(grad_pre, wu[j])
 
             @pl.when(k == 0)
             def _():
-                oacc[rows] = out
+                oacc[rows, :384] = out_a
+                oacc[rows, 384:] = out_b
                 gacc[rows] = gin
 
             @pl.when(k > 0)
             def _():
-                oacc[rows] += out
+                oacc[rows, :384] += out_a
+                oacc[rows, 384:] += out_b
                 gacc[rows] += gin
 
             @pl.when(t == 0)
@@ -763,17 +1013,76 @@
             g_s[0, j, rows] = dot(fit[rows], gp_s[...]).astype(BF)
             g_s[1, j, rows] = dot(gft[rows], a_s[...]).astype(BF)
 
-    g_out = local(g_s, g_o, 0)
-    g_out.start()
+        ffn_copy(j).start()
+
+    def give_credit():
+        @pl.when(z > 0)
+        def _():
+            pl.semaphore_signal(credit.at[0], 1, device_id=LEFT, device_id_type=MESH)
+
+        @pl.when(z < Z - 1)
+        def _():
+            pl.semaphore_signal(credit.at[1], 1, device_id=RIGHT, device_id_type=MESH)
+
+    def take_credit():
+        @pl.when(z < Z - 1)
+        def _():
+            pl.semaphore_wait(credit.at[0], 1)
+
+        @pl.when(z > 0)
+        def _():
+            pl.semaphore_wait(credit.at[1], 1)
+
+
+    def weight_waits(k):
+        @pl.when(z - k >= 0)
+        def _():
+            @pl.when(z < Z - 1)
+            def _():
+                for item in z_copies(z - k, 0, RIGHT, False):
+                    item.wait_send()
+
+            for item in y_copies(z - k, grp):
+                item.wait_send()
+
+        @pl.when(z + k <= Z - 1)
+        def _():
+            @pl.when(z > 0)
+            def _():
+                for item in z_copies(z + k, 1, LEFT, False):
+                    item.wait_send()
+
+            for item in y_copies(z + k, grp):
+                item.wait_send()
+
+    @pl.when(z < Z - 1)
+    def _():
+        for item in z_copies(z, 0, RIGHT, False):
+            item.wait_send()
+
+    @pl.when(z > 0)
+    def _():
+        for item in z_copies(z, 1, LEFT, False):
+            item.wait_send()
+
+    pl.loop(1, Z)(weight_waits)
+    give_credit()
+
+    osend, gsend = xs.at[0], xs.at[1]
 
     @pl.loop(0, 512 // TILE)
     def _(i):
         tile = rows_of(i * TILE, TILE)
         far = rows_of(other + i * TILE, TILE)
         gsend[tile] = gacc[far].astype(BF)
-        osend[tile] = oacc[far].astype(BF)
 
     remote(gsend, grecv, 9, TO_CORE).start()
+
+    @pl.loop(0, 512 // TILE)
+    def _(i):
+        osend[rows_of(i * TILE, TILE)] = oacc[rows_of(other + i * TILE, TILE)].astype(BF)
+
+    orecv = att
     remote(osend, orecv, 10, TO_CORE).start()
     remote(gsend, grecv, 9, TO_CORE).wait_recv()
     core_rows(gf, own, 512, 7).wait_send()
@@ -800,35 +1109,28 @@
 
     gproj = gf
     core_rows(gproj, own, 512, 11).start()
-
-    remote(osend, orecv, 10, TO_CORE).wait_recv()
+    slot(0)
+
+    remote(osend, orecv, 10, TO_CORE).wait()
+
+    def rows_out(number, i, values):
+        xs[number, rows_of(i * TILE, TILE)] = values.astype(BF)
+
+    def out_copies(out_ref, number):
+        here, there = rows_of(x * 256, 256), rows_of((1 - x) * 256, 256)
+        return [
+            local(xs.at[number, here], out_ref.at[x], 35 + number),
+            remote(xs.at[number, there], out_ref.at[x], 12 + number, TO_X),
+        ]
 
     @pl.loop(0, 512 // TILE)
     def _(i):
         tile = rows_of(i * TILE, TILE)
         ffn = oacc[rows_of(own + i * TILE, TILE)] + orecv[tile].astype(F32) + downb[...]
         vec[5:6] += jnp.sum(ctb[tile].astype(F32) * ffn, axis=0, keepdims=True)
-        oacc[rows_of(own + i * TILE, TILE)] = (
-            xb[tile].astype(F32) + gate_one * ap[tile] + gate_two * ffn
-        )
-
-    def hand_over(src, out_ref, number):
-        @pl.loop(0, 256 // TILE)
-        def _(i):
-            xs[number, rows_of(i * TILE, TILE)] = src[
-                rows_of(own + (1 - x) * 256 + i * TILE, TILE)
-            ].astype(BF)
-            fst[2 * number, rows_of(i * TILE, TILE)] = src[rows_of(own + x * 256 + i * TILE, TILE)]
-
-        remote(xs.at[number], xr.at[number], 12 + number, TO_X).start()
-        local(fst.at[2 * number], out_ref.at[x], 1 + 2 * number).start()
-
-    def take_over(out_ref, number):
-        remote(xs.at[number], xr.at[number], 12 + number, TO_X).wait_recv()
-        fst[2 * number + 1] = xr[number].astype(F32)
-        local(fst.at[2 * number + 1], out_ref.at[1 - x], 2 + 2 * number).start()
-
-    hand_over(oacc, out_o, 0)
+        rows_out(0, i, xb[tile].astype(F32) + gate_one * ap[tile] + gate_two * ffn)
+
+    out_copies(out_o, 0)[0].start()
 
     core_rows(gproj, other, 512, 11).wait_recv()
 
@@ -853,10 +1155,14 @@
                 ot_s[p].astype(BF), gproj[:, lanes]
             ).astype(BF)
 
+    take_credit()
+    sum_0(0)
+    slot(1)
+
     def attend_back(p):
         for h in range(2):
-            qm[h] = q_s[p] * keep[h]
-            dom[h] = do_s[p] * keep[h]
+            a_s[:, h * 128 : (h + 1) * 128] = q_s[p] * keep[h]
+            gp_s[:, h * 128 : (h + 1) * 128] = do_s[p] * keep[h]
         dqt[...] = jnp.zeros_like(dqt)
 
         @pl.loop(0, 4)
@@ -865,17 +1171,24 @@
             keys, values = k_s[p, rows], v_s[p, rows]
             dv, dk = None, None
             for h in range(2):
-                probs = jnp.exp(dot_t(keys, qm[h]) - lse[p, pl.ds(h, 1), :])
-                grads = dot_t(values, dom[h])
+                qm, dom = a_s[:, h * 128 : (h + 1) * 128], gp_s[:, h * 128 : (h + 1) * 128]
+                probs = jnp.exp(dot_t(keys, qm) - lse[p, pl.ds(h, 1), :])
+                grads = dot_t(values, dom)
                 ds = (probs * (grads - dlt[p, pl.ds(h, 1), :])).astype(BF)
-                dv_h = dot(probs.astype(BF), dom[h])
-                dk_h = dot(ds, qm[h])
+                dv_h = dot(probs.astype(BF), dom)
+                dk_h = dot(ds, qm)
                 dv = dv_h if dv is None else dv + dv_h
                 dk = dk_h if dk is None else dk + dk_h
                 dqt[pl.ds(h * 64, 64)] += dot(kt_s[p, pl.ds(h * 64, 64), rows], ds)
             cos_t, sin_t = cos_v[rows], sin_v[rows]
             gq[rows, pl.ds(128, 128)] = (dk * cos_t - swap_halves(dk) * sin_t).astype(BF)
             gq[rows, pl.ds(256, 128)] = dv.astype(BF)
+
+            @pl.when(t == 1)
+            def _():
+                slot(2 + 3 * p)
+
+        slot(3 + 3 * p)
 
         @pl.loop(0, 4)
         def _(t):
@@ -893,6 +1206,8 @@
             rows = rows_of(r * 256, 256)
             b_s[1 + p, rows] = dot(ait[rows], gq[...]).astype(BF)
 
+        sum_0(1 + p)
+
         @pl.loop(0, 4)
         def _(t):
             rows = rows_of(t * 256, 256)
@@ -902,21 +1217,19 @@
             else:
                 gacc[rows] += part
 
+        slot(4 + 3 * p)
+
+    remote(gsend, grecv, 9, TO_CORE).wait_send()
     for p in range(3):
         attend_back(p)
-        if p == 0:
-            take_over(out_o, 0)
-    remote(gsend, grecv, 9, TO_CORE).wait_send()
-
-    b_out = local(b_s, b_o, 6)
-    b_out.start()
 
     @pl.loop(0, 512 // TILE)
     def _(i):
         gsend[rows_of(i * TILE, TILE)] = gacc[rows_of(other + i * TILE, TILE)].astype(BF)
 
     remote(gsend, grecv, 14, TO_CORE).start()
-    remote(gsend, grecv, 14, TO_CORE).wait_recv()
+    slot(11)
+    remote(gsend, grecv, 14, TO_CORE).wait()
 
     @pl.loop(0, 512 // TILE)
     def _(i):
@@ -926,70 +1239,105 @@
         normed = n1[tile]
         vec[0:1] += jnp.sum(grad, axis=0, keepdims=True)
         vec[1:2] += jnp.sum(grad * normed, axis=0, keepdims=True)
-        gacc[near] = gm[tile] + norm_back(grad * mul_one, normed, i1[tile])
-
-    hand_over(gacc, gin_o, 1)
+        rows_out(1, i, gm[tile] + norm_back(grad * mul_one, normed, i1[tile]))
+
+    for item in out_copies(gin_o, 1):
+        item.start()
     sums = vec[...]
     vec[6:7] = sums[1:2] * (1.0 + scale_one)
     vec[7:8] = sums[4:5] * (1.0 + scale_two)
     vec[1:2] = sums[1:2] * again[...]
     vec[4:5] = sums[4:5] * fgain[...]
-    take_over(gin_o, 1)
-    v_out = local(vec, vec_o, 7)
-    v_out.start()
-    u_out = local(ubg, ubg_o, 8)
-    u_out.start()
-
-    v_out.wait()
-    u_out.wait()
-    g_out.wait()
-    b_out.wait()
+    for core in range(2):
+        @pl.when(c == core)
+        def _():
+            for j in range(4):
+                vec[9 + 2 * core + j // 2, pl.ds((j % 2) * 384, 384)] = ubg[j, 0]
+
+    both = cond[...].astype(F32)
+    vec[13:14, :128] = 0.5 * jnp.where(x == 0, both[0:1], both[1:2])
+    remote(vec, vecr, 30, TO_CORE).start()
+    slot(12)
+    remote(vec, vecr, 30, TO_CORE).wait_recv()
+    chip = 2 * z + x
+    vall[chip] = vec[...] + vecr[...]
+
+    def vec_copy(n, slot):
+        return pltpu.make_async_remote_copy(
+            src_ref=vall.at[slot], dst_ref=vall.at[slot], send_sem=vss.at[n], recv_sem=vrs.at[n],
+            device_id=peers[n], device_id_type=MESH,
+        )
+
+    for n in range(len(peers)):
+        vec_copy(n, chip).start()
+    slot(13)
+    for n in range(len(peers)):
+        vec_copy(n, 2 * peers[n]["mlp"] + peers[n]["seq"] // 2).wait_recv()
+
+    high = lax.Precision.HIGHEST
+    everyone = vall[:, 13, :128]
+    total = vall[0]
+    for n in range(1, 8):
+        total = total + vall[n]
+    acc = None
+    ada_out = []
+    sstage[...] = jnp.zeros_like(sstage)
+    for part in range(6):
+        span = pl.ds(part * D, D)
+        grads = vall[:, part, :]
+        sstage[part : part + 1] = total[part : part + 1]
+        oacc[pl.ds(part * 128, 128)] = lax.dot_general(
+            everyone, grads, (((0,), (0,)), ((), ())), precision=high, preferred_element_type=F32
+        )
+        ada_out.append(local(oacc.at[pl.ds(part * 128, 128)], adaw_o.at[:, span], 37 + part))
+        ada_out[-1].start()
+        piece = lax.dot_general(
+            grads, adaw[:, span].astype(F32), (((1,), (1,)), ((), ())), precision=high,
+            preferred_element_type=F32,
+        )
+        acc = piece if acc is None else acc + piece
+    cstage[...] = acc
+    for n in range(3):
+        sstage[6 + n : 7 + n] = total[6 + n : 7 + n]
+    for core in range(2):
+        halves = [total[9 + 2 * core + j // 2, (j % 2) * 384 : (j % 2 + 1) * 384] for j in range(4)]
+        mine = halves[0]
+        for j in range(1, 4):
+            mine = jnp.where(z == j, halves[j], mine)
+        sstage[9, pl.ds(core * 384, 384)] = mine
+    cond_o[...] = cstage[pl.ds(2 * z, 2), :]
+    small_o[...] = sstage[...]
+    slot(14)
+    for item in ada_out:
+        item.wait()
+
     for number, ref in ((0, out_o), (1, gin_o)):
-        local(fst.at[2 * number], ref.at[x], 1 + 2 * number).wait()
-        local(fst.at[2 * number + 1], ref.at[1 - x], 2 + 2 * number).wait()
-        remote(xs.at[number], xr.at[number], 12 + number, TO_X).wait_send()
+        out_copies(ref, number)[0].wait()
+        out_copies(ref, number)[1].wait()
+    for p in range(4):
+        for item in piece_copies(p):
+            item.wait()
+    for first, (src, kind) in enumerate(((g_s.at[x, z], x), (fxr, 1 - x))):
+        for item in final_copies(src, kind, first):
+            item.wait()
+    for n in range(len(peers)):
+        vec_copy(n, chip).wait_send()
     swap_x.wait_send()
     swap_c.wait_send()
-    core_rows(ai, own + x * 256, 256, 2).wait_send()
-    core_rows(ai, own + (1 - x) * 256, 256, 3).wait_send()
     for p in range(3):
         att_copy(p, False).wait_send()
     core_rows(fi, own, 512, 8).wait_send()
-    remote(osend, orecv, 10, TO_CORE).wait_send()
     core_rows(gproj, own, 512, 11).wait_send()
-    remote(gsend, grecv, 14, TO_CORE).wait_send()
-
-    @pl.when(z < Z - 1)
-    def _():
-        for item in z_copies(z, 0, RIGHT, False):
-            item.wait_send()
-
-    @pl.when(z > 0)
-    def _():
-        for item in z_copies(z, 1, LEFT, False):
-            item.wait_send()
-
-    @pl.loop(1, Z)
-    def _(k):
-        @pl.when(z - k >= 0)
-        def _():
-            @pl.when(z < Z - 1)
-            def _():
-                for item in z_copies(z - k, 0, RIGHT, False):
-                    item.wait_send()
-
-            for item in y_copies(z - k, grp):
-                item.wait_send()
-
-        @pl.when(z + k <= Z - 1)
-        def _():
-            @pl.when(z > 0)
-            def _():
-                for item in z_copies(z + k, 1, LEFT, False):
-                    item.wait_send()
-
-            for item in y_copies(z + k, grp):
-                item.wait_send()
+    remote(vec, vecr, 30, TO_CORE).wait_send()
+    remote(g_s.at[x, z], fxr, 15, TO_X).wait_send()
+    for j in range(4):
+        ffn_copy(j).wait_send()
+    for place in EVERY:
+        @pl.when(z == place)
+        def _(place=place):
+            for where, make in pending:
+                if where == place:
+                    make(place).wait_send()
 
 
 def tables(seg_len, seq_size):
@@ -1022,7 +1370,7 @@
     dma = pltpu.SemaphoreType.DMA
     scratch = [
         V((128, 4608), BF), V((3, 768, 384), BF), V((768, 768), BF), V((Z, 768, 384), BF),
-        V((Z, 384, 768), BF), V((Z, 1, 768), F32), V((1024, 128), F32), V((1024, 128), F32),
+        V((Z, 768, 384), BF), V((Z, 1, 768), F32), V((1024, 128), F32), V((1024, 128), F32),
         V((32, 1024), F32), V((32, 1024), F32),
         V((512, 768), BF), V((512, 768), BF), V((2, 4608), F32), V((512, 768), F32), V((512, 1), F32),
         V((1024, 768), BF), V((768, 1024), BF),
@@ -1030,24 +1378,28 @@
         V((3, 128, 1024), BF), V((3, 128, 1024), BF), V((3, 128, 1024), F32), V((3, 2, 1024), F32),
         V((512, 768), BF), V((512, 384), BF),
         V((512, 768), F32), V((512, 768), F32), V((512, 1), F32),
-        V((1024, 768), BF), V((768, 1024), BF), V((1024, 768), BF), V((768, 1024), BF),
+        V((768, 1024), BF), V((1024, 768), BF), V((768, 1024), BF),
         V((1024, 768), F32), V((1024, 768), F32), V((1024, 384), BF), V((1024, 384), BF),
-        V((2, Z, 768, 384), BF), V((512, 768), BF), V((512, 768), BF), V((512, 768), BF), V((512, 768), BF),
-        V((512, 768), F32), V((3, 1024, 128), BF), V((3, 2, 1024), F32),
-        V((2, 1024, 128), BF), V((2, 1024, 128), BF), V((128, 1024), F32), V((1024, 384), BF),
-        V((4, 768, 384), BF), V((2, 256, 768), BF), V((2, 256, 768), BF), V((4, 256, 768), F32),
-        V((16, 768), F32), V((Z, 1, 384), F32),
-        dma((20,)), dma((16,)), dma((16,)), dma((2, Z, 3)), dma((2, Z, 3)), dma((Z, 2)), dma((Z, 2)),
+        V((2, Z, 768, 384), BF), V((512, 768), BF),
+        V((512, 768), F32), V((3, 1024, 128), BF), V((3, 2, 1024), F32), V((128, 1024), F32),
+        V((1024, 384), BF), V((4, 768, 384), BF), V((2, 512, 768), BF),
+        V((16, 768), F32), V((16, 768), F32), V((2 * Z, 16, 768), F32), V((Z, 1, 384), F32),
+        V((2 * Z, 128), F32), V((16, 768), F32),
+        V((Z, 768, 384), BF), V((Z, 768, 384), BF), V((768, 384), BF), V((4, 192, 384), BF),
+        V((4, 768, 384), BF),
+        dma((43,)), dma((31,)), dma((31,)), dma((2, Z, 3)), dma((2, Z, 3)), dma((Z, 2)), dma((Z, 2)),
+        dma((3,)), dma((4,)), dma((4, 4, 4)), dma((4, 4, 4)), dma((8,)), dma((8,)), dma((7,)), dma((7,)),
+        pltpu.SemaphoreType.REGULAR((2,)),
     ]
-    token = shape(inputs.shape, F32)
-    out, gin, g, b, vec, ubg = pl.pallas_call(
-        functools.partial(fast_kernel, Z),
+    token = shape(inputs.shape, BF)
+    out, gin, grad_cond, grad_ada, small, grad_qkv, grad_out, ffn = pl.pallas_call(
+        fast_kernel,
         out_shape=[
-            token, token, shape((2, Z, 768, 384), BF), shape((4, 768, 384), BF),
-            shape((16, 768), F32), shape((Z, 1, 384), F32),
+            token, token, shape(condition.shape, F32), shape(ada_weight.shape, F32), shape((16, 768), F32),
+            shape(qkv_weight.shape, BF), shape(out_weight.shape, BF), shape((2, 768, 768), BF),
         ],
         in_specs=[hbm, vm, vm, hbm, vm, hbm, hbm, vm, hbm, vm, hbm, vm, hbm, hbm, hbm, hbm, hbm],
-        out_specs=[hbm] * 6,
+        out_specs=[hbm, hbm, vm, hbm, vm, hbm, hbm, hbm],
         scratch_shapes=scratch,
         compiler_params=pltpu.CompilerParams(
             collective_id=0, has_side_effects=True, vmem_limit_bytes=VMEM_LIMIT
@@ -1057,29 +1409,10 @@
         inputs, condition, row(attn_gain), ada_weight, row(ada_bias), qkv_weight, out_weight,
         row(ffn_gain), up_weight, row(up_bias), down_weight, row(down_bias), cotangent, *tabs,
     )
-    g = lax.psum_scatter(g, "mlp", scatter_dimension=1, tiled=True)
-    g = lax.all_gather(g, "seq").astype(F32)[:, :, 0]
-    g = g[:2] + g[2:]
-    grad_up = jnp.concatenate([g[0, 0], g[1, 0]], axis=-1)
-    grad_down = jnp.concatenate([g[0, 1], g[1, 1]], axis=-1).T
-    b = lax.all_gather(lax.psum(b, "mlp"), "seq").astype(F32)
-    b = b[:2] + b[2:]
-    grad_out = b[:, 0].reshape(2, 2, 384, 384).transpose(0, 2, 1, 3).reshape(768, 768)
-    grad_qkv = b[:, 1:].reshape(2, 3, 768, 3, 128).transpose(2, 3, 0, 1, 4).reshape(768, 2304)
-    vec = lax.all_gather(lax.all_gather(vec, "seq"), "mlp")
-    vec = vec.reshape(Z, 2, 2, 16, 768).sum(axis=2)
-    dmod = vec[:, :, :6].reshape(2 * Z, 4608)
-    cond = lax.all_gather(condition, "mlp", tiled=True).astype(F32)
-    high = lax.Precision.HIGHEST
-    grad_ada = jnp.dot(cond.T, dmod, precision=high)
-    mine = lax.dynamic_slice_in_dim(dmod, lax.axis_index("mlp") * 2, 2, 0)
-    grad_cond = jnp.dot(mine, ada_weight.astype(F32).T, precision=high)
-    tail = vec[:, :, 6:9].sum(axis=(0, 1))
-    ubg = lax.all_gather(lax.all_gather(ubg[:, 0], "seq"), "mlp").reshape(Z, 2, 2, Z, 384).sum(axis=(0, 1))
-    grad_ub = lax.dynamic_index_in_dim(ubg, lax.axis_index("mlp"), 1, False).reshape(-1)
+    wide = lambda v: v.astype(F32)
     return (
-        out, gin, grad_cond, tail[0], grad_ada, dmod.sum(axis=0), grad_qkv, grad_out, tail[1],
-        grad_up, grad_ub, grad_down, tail[2],
+        wide(out), wide(gin), grad_cond, small[6], grad_ada, small[:6].reshape(-1), wide(grad_qkv),
+        wide(grad_out), small[7], wide(ffn[0]), small[9], wide(ffn[1]).T, small[8],
     )
 
 

time: 586 us -> 271 us (0.46)
  waiting for transfers between devices: 274 us -> 0 us
  Pallas kernels: 149 us -> 245 us
  blocking collectives: 51.4 us -> 0 us
  local copies, waits for them, and re-layouts: 58.2 us -> 12.4 us
  other arithmetic: 33.3 us -> 13 us
  between operations: 13.9 us -> 0.67 us
    psum x1 -> x0, waiting for transfers between devices: 247 us -> none  [fast_shards(): b = lax.all_gather(lax.psum(b, 'mlp'), 'seq').astype(F32)]
    pallas_call x1, Pallas kernels: 149 us -> 245 us  [fast_shards(): pl.pallas_call(fast_kernel, out_shape=[token, token, shape(condition.shap...]
    all_gather x5 -> x0, blocking collectives: 51.4 us -> none  [the longest x2 23.3 us: fast_shards(): vec = lax.all_gather(lax.all_gather(vec, 'seq'), 'mlp')]
    all_gather x2 -> x0, waiting for transfers between devices: 26.3 us -> none  [the longest x1 26.3 us: fast_shards(): b = lax.all_gather(lax.psum(b, 'mlp'), 'seq').astype(F32)]
    unnamed x32 -> x15, local copies, waits for them, and re-layouts: 22.5 us -> 3.93 us
    all_gather x2 -> x0, local copies, waits for them, and re-layouts: 12.7 us -> none  [the longest x1 12.7 us: fast_shards(): b = lax.all_gather(lax.psum(b, 'mlp'), 'seq').astype(F32)]
    add x2 -> x0, other arithmetic: 11.7 us -> none  [the longest x1 11.3 us: fast_shards(): b = b[:2] + b[2:]]
    transpose x2 -> x0, local copies, waits for them, and re-layouts: 7.27 us -> none  [the longest x1 3.9 us: fast_shards(): b[:, 0].reshape(2, 2, 384, 384).transpose(0, 2, 1, 3).reshape(768, 768)]
  transfers between devices with their start and end apart: 3 -> 0, of which waited for: 2 -> 0; matrix products, arithmetic and copies ran while one was open for 4% -> 0% of each run, Pallas kernels for 0% -> 0%
where the time goes in v2:
time: 271 us
  Pallas kernels  245 us (90%)
  other arithmetic  13 us (5%)
  local copies, waits for them, and re-layouts  12.4 us (5%)
    pallas_call x1, Pallas kernels, fast_shards(): pl.pallas_call(fast_kernel, out_shape=[token, token, shape(condition.shap...  245 us
    convert_element_type x4, other arithmetic, fast_shards(): wide = lambda v: v.astype(F32)  9.65 us
    reshape x5, local copies, waits for them, and re-layouts, fast_shards(): row = lambda v: v.reshape(1, -1)  6.41 us

profile of v2, /device:TPU:0, one launch (start us, length us, event | category | flops | bytes accessed | tf_op | source)
XLA Modules:
  0.0 270.7 jit_solution(11322022907806872972)
XLA Ops:
  0.6 1.3 reshape.49.adab
  2.0 1.3 reshape.48.again
  3.3 1.3 reshape.50.fgain
  4.5 1.3 reshape.51.upb
  5.8 1.3 reshape.52.downb
  7.1 244.6 %block.1 = (bf16[2,256,768]{2,1,0:T(8,128)(2,1)}, bf16[2,256,768]{2,1,0:T(8,128)(2,1)}, f32[2,128]{1,0:T(2,128)}, f32[128,4608]{1,0:T(8,128)}, f32[16,768]{1,0:T...) custom-call(bf16[2,256,768]{2,1,0:T(8,128)(2,1)} %inputs.1, ...), custom_call_target="tpu_custom_call" | custom-call | tf_op jit(solution)/shard_map/block/pallas_call | solution.py:1395
  251.7 1.5 slice_reduce_fusion
  253.1 3.4 %convert_bitcast_fusion = (f32[768,768]{0,1:T(8,128)S(1)}, f32[768,768]{1,0:T(8,128)}) fusion(bf16[2,768,768]{2,1,0:T(8,128)(2,1)} %get-tuple-element.28), kind=kLoop, calls=%fused_computation | loop fusion | flops 1179648 | bytes 7077888 | tf_op jit(solution)/shard_map/transpose | solution.py:1415
  256.5 0.0 copy-start.4
  256.5 1.9 copy.30
  258.5 0.0 copy-done.4
  258.5 0.6 reshape.53
  259.1 0.0 copy-start.1
  259.1 5.6 %convert_element_type.24 = f32[768,2304]{1,0:T(8,128)} convert(bf16[768,2304]{1,0:T(8,128)(2,1)} %get-tuple-element.26) | non-fusion elementwise | flops 1769472 | bytes 10616832 | tf_op jit(solution)/shard_map/convert_element_type | solution.py:1412
  264.7 0.0 copy-start.3
  264.7 0.0 copy-done.1
  264.7 0.0 copy-start.2
  264.7 1.6 convert_element_type.25
  266.3 0.0 copy-done.3
  266.3 0.0 copy-start.5
  266.3 0.0 copy-start
  266.3 1.3 convert_element_type.22
  267.5 0.0 copy-done.2
  267.5 1.3 convert_element_type.23
  268.8 0.0 copy-done.5
  268.8 0.6 copy.33
  269.3 0.0 copy-done
  269.3 1.4 copy.34
  (1 shorter events, 0.0 us)
Async XLA Ops:
  256.5 1.9 copy-start.4
  259.1 5.6 %copy-start.1 = (bf16[768,768]{1,0:T(8,128)(2,1)S(1)}, bf16[768,768]{1,0:T(8,128)(2,1)}, u32[]{:S(2)}) copy-start(bf16[768,768]{1,0:T(8,128)(2,1)} %get-tuple-element.27) | copy-start | bytes 3538948
  264.7 1.6 copy-start.3
  264.7 2.8 %copy-start.2 = (bf16[2,256,768]{2,1,0:T(8,128)(2,1)S(1)}, bf16[2,256,768]{2,1,0:T(8,128)(2,1)}, u32[]{:S(2)}) copy-start(bf16[2,256,768]{2,1,0:T(8,128)(2,1)} %get-tuple-element.22) | copy-start | bytes 2359300
  266.3 2.5 copy-start.5
  266.3 3.1 %copy-start = (f32[128,4608]{1,0:T(8,128)S(1)}, f32[128,4608]{1,0:T(8,128)}, u32[]{:S(2)}) copy-start(f32[128,4608]{1,0:T(8,128)} %get-tuple-element.65) | copy-start | bytes 7077892

commit v3 on v2

--- a/solution.py
+++ b/solution.py
@@ -1,4 +1,3 @@
-import functools
 import math
 
 import jax
@@ -356,6 +355,107 @@
     )
 
 
+FFN_X, FFN_Z, FFN_OWN, FFN_LAST, SUM_0, REL, SUM_3, SUM_4, FW, SUM_7, WL, WR, XS_, ZS, XO, OX, GX = range(17)
+AT_W, AT_F, AT_A, AT_T, AT_N, AT_B, AT_E, AT_D, AT_G = range(9)
+ORDERS = ((1, 2, 0, 3), (0, 2, 1, 3), (3, 1, 2, 0), (2, 1, 3, 0))
+OWN_STEP = 2
+PLAN = {(AT_A, 0, 0): {0: [(WR, 1)], 1: [(WL, 1), (WR, 1)], 2: [(WL, 1), (WR, 1)], 3: [(WL, 1)]},
+ (AT_B, 0, 0): {0: [(OX, 1)], 1: [(OX, 1), (FFN_X, 3, 0)], 2: [(FFN_Z, 0, 0), (ZS, 0, 0), (OX, 1)], 3: [(OX, 1)]},
+ (AT_B, 0, 1): {1: [(FFN_Z, 2, 2), (ZS, 2, 2)], 2: [(REL, 1, 0, 0)]},
+ (AT_B, 0, 2): {0: [(XS_, 3, 2)], 1: [(XS_, 3, 1)], 2: [(XS_, 0, 1)], 3: [(XS_, 0, 2)]},
+ (AT_B, 0, 3): {0: [(ZS, 3, 1)], 1: [(FFN_Z, 3, 0), (ZS, 3, 0)], 2: [(REL, 1, 1, 0)], 3: [(ZS, 0, 1)]},
+ (AT_B, 0, 5): {0: [(SUM_0, 1), (XS_, 0, 0)],
+                1: [(REL, 0, 3, 0), (XS_, 3, 2)],
+                2: [(REL, 0, 3, 0), (XS_, 0, 2)],
+                3: [(SUM_0, 1), (XS_, 3, 0)]},
+ (AT_B, 0, 6): {0: [(FFN_X, 3, 2)], 1: [(FFN_X, 3, 1)], 2: [(SUM_3, 0), (FFN_X, 0, 1)], 3: [(FFN_X, 0, 2)]},
+ (AT_B, 1, 0): {0: [(XS_, 0, 1)], 1: [(REL, 0, 2, 0), (XS_, 1, 0)], 2: [(FFN_Z, 0, 1), (ZS, 0, 1)], 3: [(XS_, 3, 1)]},
+ (AT_B, 1, 1): {0: [(FFN_X, 0, 0), (FFN_OWN, 0)],
+                1: [(FFN_X, 3, 2)],
+                2: [(REL, 1, 0, 1), (XS_, 2, 0), (FFN_X, 0, 2)],
+                3: [(FFN_X, 3, 0), (FFN_OWN, 0)]},
+ (AT_B, 1, 2): {0: [(XO, 0)], 1: [(REL, 1, 0, 0), (XS_, 1, 1)], 2: [(REL, 1, 1, 1), (SUM_4, 0)], 3: [(SUM_3, 0)]},
+ (AT_B, 1, 3): {0: [(SUM_3, 0), (ZS, 3, 2), (FFN_X, 0, 1)],
+                1: [(FFN_Z, 3, 1), (SUM_3, 0), (ZS, 3, 1), (FFN_X, 1, 0), (FFN_OWN, 0)],
+                2: [(XS_, 2, 1)],
+                3: [(ZS, 0, 2), (FFN_X, 3, 1)]},
+ (AT_B, 1, 5): {0: [(SUM_0, 2)],
+                1: [(REL, 0, 3, 1)],
+                2: [(REL, 0, 3, 1), (FFN_X, 2, 0), (FFN_OWN, 0)],
+                3: [(SUM_4, 0), (SUM_0, 2), (XO, 0), (FFN_OWN, 1)]},
+ (AT_B, 1, 6): {0: [(FFN_LAST, 0), (XS_, 0, 2), (FFN_OWN, 1)],
+                1: [(REL, 0, 2, 1), (XO, 0), (FFN_X, 1, 1), (FFN_OWN, 1)],
+                2: [(FFN_Z, 0, 2), (ZS, 0, 2), (XO, 0), (SUM_3, 1)]},
+ (AT_B, 2, 0): {0: [(SUM_4, 0)],
+                1: [(SUM_4, 0)],
+                2: [(FFN_X, 2, 1), (FW, 2, 1, 0), (FW, 3, 3, 0), (FFN_OWN, 1)],
+                3: [(XO, 1)]},
+ (AT_B, 2, 1): {0: [(XO, 1)], 1: [(REL, 1, 0, 1), (XO, 1)], 3: [(FFN_LAST, 0)]},
+ (AT_B, 2, 2): {0: [(FFN_X, 0, 2)],
+                1: [(FFN_Z, 3, 2), (ZS, 3, 2), (FFN_LAST, 0)],
+                2: [(REL, 1, 0, 2), (XO, 1), (FFN_LAST, 0)],
+                3: [(XS_, 3, 2)]},
+ (AT_B, 2, 3): {0: [(SUM_3, 1)], 1: [(SUM_3, 1)], 2: [(REL, 1, 1, 2), (SUM_4, 1)], 3: [(SUM_3, 1), (FFN_LAST, 1)]},
+ (AT_B, 2, 5): {0: [(SUM_0, 3), (FFN_LAST, 1), (FFN_OWN, 2), (XO, 2)],
+                1: [(FW, 3, 2, 0), (REL, 0, 3, 2), (FFN_LAST, 1), (XS_, 1, 2)],
+                2: [(REL, 0, 3, 2), (XS_, 2, 2)],
+                3: [(SUM_0, 3)]},
+ (AT_B, 2, 6): {0: [(SUM_4, 1)],
+                1: [(SUM_4, 1), (REL, 0, 2, 2)],
+                2: [(FW, 2, 1, 1), (FFN_LAST, 1)],
+                3: [(FFN_X, 3, 2), (FFN_OWN, 2), (XO, 2)]},
+ (AT_D, 0): {0: [(SUM_7, 0), (SUM_3, 2), (GX, 1), (SUM_3, 3), (SUM_4, 2), (SUM_7, 1), (SUM_4, 3), (SUM_7, 2),
+                 (SUM_7, 3)],
+             1: [(REL, 1, 0, 2), (REL, 0, 3, 3), (SUM_3, 2), (REL, 0, 2, 3), (FW, 3, 2, 1), (REL, 1, 0, 3), (XO, 2),
+                 (FW, 2, 0, 1), (SUM_4, 2), (SUM_3, 3), (FW, 3, 3, 1), (SUM_7, 1), (FFN_LAST, 2), (GX, 1),
+                 (FW, 3, 2, 2), (FW, 2, 0, 2), (SUM_4, 3), (FW, 3, 2, 3), (FW, 2, 0, 3), (FW, 3, 3, 2), (SUM_7, 2),
+                 (FW, 3, 3, 3), (SUM_7, 3)],
+             2: [(REL, 0, 3, 3), (FW, 3, 3, 1), (SUM_4, 2), (SUM_3, 3), (FW, 2, 0, 1), (SUM_7, 1), (XO, 2),
+                 (SUM_4, 3), (FW, 2, 1, 2), (FW, 3, 3, 2), (GX, 0), (FFN_LAST, 2), (FW, 2, 0, 2), (SUM_7, 2), (GX, 1),
+                 (FW, 3, 3, 3), (FW, 2, 1, 3), (FW, 2, 0, 3), (SUM_7, 3)],
+             3: [(FFN_LAST, 2), (SUM_3, 2), (SUM_7, 0), (GX, 1), (SUM_3, 3), (SUM_4, 2), (SUM_7, 1), (SUM_4, 3),
+                 (SUM_7, 2), (SUM_7, 3)]},
+ (AT_E, 0): {2: [(REL, 1, 0, 3)]},
+ (AT_E, 1): {0: [(GX, 0), (FFN_LAST, 2)],
+             1: [(FW, 3, 3, 0), (FW, 2, 0, 0), (SUM_7, 0), (GX, 0), (FFN_X, 1, 2), (FFN_OWN, 2)],
+             2: [(FW, 2, 0, 0), (REL, 1, 1, 3), (SUM_7, 0), (SUM_3, 2), (FFN_X, 2, 2), (FFN_OWN, 2)],
+             3: [(SUM_4, 1), (GX, 0)]},
+ (AT_G, 0): {0: [(XS_, 1, 0)], 1: [(XS_, 0, 0)], 2: [(XS_, 3, 0)], 3: [(XS_, 2, 0)]},
+ (AT_G, 1): {1: [(XS_, 0, 2)], 2: [(FFN_X, 3, 0), (ZS, 3, 0)]},
+ (AT_G, 2): {0: [(XS_, 2, 1)], 1: [(FFN_X, 0, 2), (ZS, 0, 2)], 3: [(XS_, 1, 1)]},
+ (AT_G, 3): {0: [(XS_, 3, 0), (FFN_X, 2, 1), (ZS, 2, 1)],
+             2: [(XS_, 1, 2)],
+             3: [(XS_, 0, 0), (FFN_X, 1, 1), (ZS, 1, 1)]},
+ (AT_N, 1): {0: [(XS_, 3, 1), (FFN_X, 2, 2), (ZS, 2, 2)],
+             1: [(FFN_Z, 2, 0), (ZS, 2, 0), (FFN_X, 2, 1), (FFN_X, 2, 2), (XS_, 3, 0)],
+             2: [(FFN_X, 1, 1), (FFN_Z, 1, 1), (ZS, 1, 1), (XS_, 0, 0)],
+             3: [(XS_, 0, 1), (FFN_X, 1, 2), (ZS, 1, 2)]},
+ (AT_N, 2): {0: [(FFN_X, 3, 0), (ZS, 3, 0)], 2: [(FFN_X, 1, 2)], 3: [(FFN_X, 0, 0), (ZS, 0, 0)]},
+ (AT_N, 3): {0: [(OX, 0)], 1: [(OX, 0)], 2: [(FFN_Z, 1, 2), (ZS, 1, 2), (OX, 0)], 3: [(OX, 0)]},
+ (AT_N, 4): {0: [(SUM_0, 0), (FFN_X, 3, 1)],
+             1: [(FFN_Z, 2, 1), (ZS, 2, 1)],
+             2: [(FFN_X, 0, 0)],
+             3: [(SUM_0, 0), (FFN_X, 0, 1)]},
+ (AT_T, 1, 0): {0: [(WR, 3), (XS_, 1, 1), (FFN_X, 1, 0), (ZS, 1, 0)],
+                3: [(WL, 3), (XS_, 2, 1), (FFN_X, 2, 0), (ZS, 2, 0)]},
+ (AT_T, 1, 1): {1: [(XS_, 0, 1)]},
+ (AT_T, 1, 2): {2: [(XS_, 3, 1)]},
+ (AT_T, 1, 3): {0: [(XS_, 1, 2)], 1: [(FFN_X, 0, 0), (ZS, 0, 0)], 3: [(XS_, 2, 2)]},
+ (AT_T, 2, 0): {0: [(FFN_X, 1, 1), (ZS, 1, 1)], 2: [(XS_, 3, 2)], 3: [(FFN_X, 2, 1), (ZS, 2, 1)]},
+ (AT_T, 2, 1): {0: [(XS_, 2, 0)], 1: [(FFN_X, 0, 1), (ZS, 0, 1)], 3: [(XS_, 1, 0)]},
+ (AT_T, 2, 2): {1: [(XS_, 2, 0)], 2: [(FFN_X, 3, 1), (ZS, 3, 1)]},
+ (AT_T, 2, 3): {0: [(FFN_X, 1, 2), (ZS, 1, 2)], 2: [(XS_, 1, 0)], 3: [(FFN_X, 2, 2), (ZS, 2, 2)]},
+ (AT_T, 3, 0): {0: [(FFN_X, 2, 0), (ZS, 2, 0)],
+                1: [(XS_, 2, 1)],
+                2: [(FFN_X, 3, 2), (ZS, 3, 2)],
+                3: [(FFN_X, 1, 0), (ZS, 1, 0)]},
+ (AT_T, 3, 1): {0: [(XS_, 2, 2)], 2: [(XS_, 1, 1)], 3: [(XS_, 1, 2)]},
+ (AT_T, 3, 2): {1: [(FFN_X, 2, 0)]},
+ (AT_T, 3, 3): {1: [(XS_, 2, 2)], 2: [(FFN_X, 1, 0), (FFN_Z, 1, 0), (ZS, 1, 0)]},
+ (AT_W, 1): {0: [(WR, 2)], 1: [(WR, 2)], 2: [(WL, 2)], 3: [(WL, 2)]}}
+HALF = (0, 0, 0, 0)
+
+
 BF = jnp.bfloat16
 F32 = jnp.float32
 MESH = pl.DeviceIdType.MESH
@@ -374,9 +474,9 @@
 
 
 def pick(table, index):
-    value = jnp.int32(table[0])
+    value = table[0]
     for place in range(1, len(table)):
-        value = jnp.where(index == place, jnp.int32(table[place]), value)
+        value = jnp.where(index == place, table[place], value)
     return value
 
 
@@ -390,11 +490,11 @@
 def fast_kernel(
     inputs, cond, again, adaw_h, adab, qkv_h, outw_h, fgain, up_h, upb, down_h, downb, cot_h,
     cos_h, sin_h, cost_h, sint_h,
-    out_o, gin_o, cond_o, adaw_o, small_o, qkv_o, outw_o, ffn_o,
+    out_o, gin_o, qkv_o, outw_o, ffn_o, vall_o,
     adaw, wq, wo, wu, wd, ub, cos_v, sin_v, cost, sint,
     xb, ctb, mod2, n1, i1, ai, ait, q_s, k_s, v_s, kt_s, vt_s, ot_s, lse, att, att_s,
     ap, n2, i2, fit, gf, gft, oacc, gacc, a_s, gp_s, g_s, grecv,
-    gm, do_s, dlt, dqt, gq, b_s, xs, vec, vecr, vall, ubg, cstage, sstage,
+    gm, do_s, dlt, dqt, gq, b_s, xs, vec, vecr, vall, ubg,
     rx, rz, fxr, rxb, fb,
     lsem, ssem, rsem, wss, wrs, yss, yrs, fss, frs, bss, brs, hss, hrs, vss, vrs, credit,
 ):
@@ -404,6 +504,8 @@
     z = lax.axis_index("mlp")
     x, c = seq // 2, seq % 2
     D = 768
+    flat = lambda ref: ref[...].reshape(1, -1)
+    again, adab, fgain, downb = flat(again), flat(adab), flat(fgain), flat(downb)
     own = c * 512
     other = (1 - c) * 512
     TO_CORE = {"seq": x * 2 + (1 - c)}
@@ -435,18 +537,12 @@
             )
     loads.append(local(outw_h, wo, 15))
     loads.append(local(up_h.at[:, half], wu.at[z], 16))
-    for n in range(2):
-        loads.append(
-            local(
-                down_h.at[rows_of(c * 384, 384), pl.ds(n * 384, 384)],
-                wd.at[z, pl.ds(n * 384, 384)],
-                17 + 3 * n,
-            )
-        )
+    loads.append(local(down_h.at[rows_of(c * 384, 384)], wd.at[z], 17))
     loads.append(local(cot_h.at[x], ctb.at[rows_of(x * 256, 256)], 18))
-    loads.append(local(upb, ub.at[z], 19))
     for item in loads:
         item.start()
+
+    ub[z] = flat(upb)
 
     barrier = pltpu.get_barrier_semaphore()
     peers = [{"seq": (x ^ dx) * 2 + c, "mlp": z ^ dz} for dx in range(2) for dz in range(Z) if dx or dz]
@@ -462,16 +558,15 @@
     def up_half(ref, which):
         return ref.at[rows_of(which * 384, 384)]
 
-    down_half = up_half
+    def down_half(ref, which):
+        return ref.at[rows_of(which * 192, 192)]
 
     def z_copies(j, way, device, first):
         if first:
             src = (
                 up_h.at[rows_of(grp * 384, 384), half],
-                down_h.at[
-                    rows_of(c * 384, 384), pl.ds(pl.multiple_of(grp * 384, 128), 384)
-                ],
-                upb,
+                down_h.at[rows_of(c * 384 + grp * 192, 192)],
+                ub.at[z],
             )
         else:
             src = (up_half(wu.at[j], grp), down_half(wd.at[j], grp), ub.at[j])
@@ -505,138 +600,108 @@
     def _():
         start_all(z_copies(z, 1, LEFT, True))
 
-    def weight_step(k):
-        @pl.when(z - k >= 0)
-        def _():
-            j = z - k
-            for item in z_copies(j, 0, RIGHT, False):
-                item.wait_recv()
-
-            @pl.when(z < Z - 1)
-            def _():
-                start_all(z_copies(j, 0, RIGHT, False))
-
-            start_all(y_copies(j, grp))
-
-        @pl.when(z + k <= Z - 1)
-        def _():
-            j = z + k
-            for item in z_copies(j, 1, LEFT, False):
-                item.wait_recv()
-
-            @pl.when(z > 0)
-            def _():
-                start_all(z_copies(j, 1, LEFT, False))
-
-            start_all(y_copies(j, grp))
-
-    orders = ((1, 2, 3, 0), (0, 2, 3, 1), (3, 1, 0, 2), (2, 1, 0, 3))
-
     def order(n):
-        return pick([orders[a][n] for a in range(Z)], z)
-
-    pending = []
-
-    def act(places, body, sends=()):
-        for place in places:
-            @pl.when(z == place)
-            def _(place=place):
-                body(place)
-                for make in sends:
-                    make(place).start()
-
-            pending.extend((place, make) for make in sends)
-
-    EVERY = (0, 1, 2, 3)
-
-    def ffn_copy(j):
+        return pick([ORDERS[a][n] for a in range(Z)], z)
+
+    pending = {place: [] for place in range(Z)}
+    CH = 3
+
+    def send(place, *makes):
+        for make in makes:
+            make().start()
+            pending[place].append(make)
+
+    def span(h):
+        return pl.ds(h * (768 // CH), 768 // CH)
+
+    def ffn_copy(j, h):
         return pltpu.make_async_remote_copy(
-            src_ref=g_s.at[1 - x, j], dst_ref=rx.at[j], send_sem=hss.at[j], recv_sem=hrs.at[j],
-            device_id=TO_X, device_id_type=MESH,
+            src_ref=g_s.at[1 - x, j, span(h)], dst_ref=rx.at[j, span(h)], send_sem=hss.at[j, h],
+            recv_sem=hrs.at[j, h], device_id=TO_X, device_id_type=MESH,
         )
 
     def add_rows(ref, others):
-        @pl.loop(0, 6)
+        @pl.loop(0, 768 // CH // 64)
         def _(i):
-            rows = rows_of(i * 128, 128)
+            rows = rows_of(i * 64, 64)
             total = ref[rows].astype(F32)
             for other_ref in others:
                 total = total + other_ref[rows].astype(F32)
             ref[rows] = total.astype(BF)
 
-    def z_send(n, place):
-        j = orders[place][n]
-        end = place in (0, 3)
-        adjacent_end = 0 if place == 1 else 3
-        if end:
+    def z_send(j, h, place):
+        if place in (0, 3):
             target, slot = (1 if place == 0 else 2), j
-        elif j == adjacent_end:
-            target, slot = j, place
         elif j in (0, 3):
             target, slot = j, place
         else:
             target, slot = j, (0 if j == 1 else 3)
-        return pltpu.make_async_remote_copy(
-            src_ref=g_s.at[x, j], dst_ref=rz.at[slot], send_sem=fss.at[n], recv_sem=frs.at[slot],
-            device_id={"mlp": target}, device_id_type=MESH,
-        )
-
-    def z_wait(slot):
+        return lambda: pltpu.make_async_remote_copy(
+            src_ref=g_s.at[x, j, span(h)], dst_ref=rz.at[slot, span(h)], send_sem=fss.at[j, h],
+            recv_sem=frs.at[slot, h], device_id={"mlp": target}, device_id_type=MESH,
+        )
+
+    def z_wait(slot, h):
+        ref = rz.at[slot, span(h)]
         pltpu.make_async_remote_copy(
-            src_ref=rz.at[slot], dst_ref=rz.at[slot], send_sem=fss.at[0], recv_sem=frs.at[slot],
+            src_ref=ref, dst_ref=ref, send_sem=fss.at[0, h], recv_sem=frs.at[slot, h],
             device_id=LEFT, device_id_type=MESH,
         ).wait_recv()
 
-    def ffn_x(n):
-        j = order(n)
-        ffn_copy(j).wait_recv()
-        add_rows(g_s.at[x, j], [rx.at[j]])
-        if n < 3:
-            places = EVERY if n == 0 else (0, 3)
-            act(places, lambda place: None, [lambda place: z_send(n, place)])
-
-    def ffn_z(n):
-        def body(place):
-            j = orders[place][n]
-            z_wait(j)
-            add_rows(g_s.at[x, j], [rz.at[j]])
-
-        act((1, 2), body, [lambda place: z_send(n, place)])
-
-    def final_copies(src, kind, first):
-        lanes = pl.ds(pl.multiple_of(c * 384, 128), 384)
-        return [
-            local(src, ffn_o.at[kind, :, lanes], 21 + first),
-            remote(src, ffn_o.at[kind, :, lanes], 16 + first, TO_CORE),
-        ]
-
-    def ffn_own():
-        def body(place):
-            slots = {0: (1, 2), 3: (1, 2), 1: (1, 0), 2: (2, 3)}[place]
-            for slot in slots:
-                z_wait(slot)
-            add_rows(g_s.at[x, place], [rz.at[slot] for slot in slots])
-
-        act(EVERY, body)
-        remote(g_s.at[x, z], fxr, 15, TO_X).start()
-        for item in final_copies(g_s.at[x, z], x, 0):
+    def ffn_x(place, j, h):
+        ffn_copy(j, h).wait_recv()
+        add_rows(g_s.at[x, j, span(h)], [rx.at[j, span(h)]])
+
+    def ffn_z(place, j, h):
+        z_wait(j, h)
+        add_rows(g_s.at[x, j, span(h)], [rz.at[j, span(h)]])
+
+    def zs(place, j, h):
+        send(place, z_send(j, h, place))
+
+    def xs_(place, j, h):
+        send(place, lambda: ffn_copy(j, h))
+
+    def final_copies(src, kind, h, first):
+        dst = ffn_o.at[kind, span(h), half]
+        return [local(src, dst, 21 + first * CH + h), remote(src, dst, 31 + first * CH + h, TO_CORE)]
+
+    def own_copy(h):
+        return pltpu.make_async_remote_copy(
+            src_ref=g_s.at[x, z, span(h)], dst_ref=fxr.at[span(h)], send_sem=hss.at[5, h],
+            recv_sem=hrs.at[5, h], device_id=TO_X, device_id_type=MESH,
+        )
+
+    def ffn_own(place, h):
+        slots = {0: (1, 2), 3: (1, 2), 1: (1, 0), 2: (2, 3)}[place]
+        for slot in slots:
+            z_wait(slot, h)
+        add_rows(g_s.at[x, place, span(h)], [rz.at[slot, span(h)] for slot in slots])
+        for item in final_copies(g_s.at[x, z, span(h)], x, h, 0):
             item.start()
 
-    def ffn_last():
-        remote(g_s.at[x, z], fxr, 15, TO_X).wait_recv()
-        for item in final_copies(fxr, 1 - x, 1):
+    def xo(place, h):
+        own_copy(h).start()
+
+    def ffn_last(place, h):
+        own_copy(h).wait_recv()
+        for item in final_copies(fxr.at[span(h)], 1 - x, h, 1):
             item.start()
 
     def quarter(ref, p, q):
+        if ref is wd:
+            return ref.at[p, pl.ds(q // 2 * 192, 192), pl.ds(q % 2 * 384, 384)]
         return ref.at[p, pl.ds(q * 192, 192)]
 
     def hop(kind, p, q, place):
         step = 1 if kind in (0, 2) else -1
-        src = quarter(b_s if kind < 2 else fb, p, q)
-        dst = quarter((wu, wd, fb, fb)[kind], p, q)
-        return pltpu.make_async_remote_copy(
-            src_ref=src, dst_ref=dst, send_sem=bss.at[kind, p, q], recv_sem=brs.at[kind, p, q],
-            device_id={"mlp": place + step}, device_id_type=MESH,
+        return lambda: pltpu.make_async_remote_copy(
+            src_ref=quarter(b_s if kind < 2 else fb, p, q),
+            dst_ref=quarter((wu, wd, fb, fb)[kind], p, q),
+            send_sem=bss.at[kind, p, q],
+            recv_sem=brs.at[kind, p, q],
+            device_id={"mlp": place + step},
+            device_id_type=MESH,
         )
 
     def hop_wait(kind, p, q):
@@ -646,72 +711,50 @@
             device_id=LEFT, device_id_type=MESH,
         ).wait_recv()
 
-    def hops(kind, p, *qs):
-        return [lambda place, q=q: hop(kind, p, q, place) for q in qs]
-
     def add_quarter(p, q, refs):
         total = quarter(b_s, p, q)[...].astype(F32)
         for ref in refs:
             total = total + quarter(ref, p, q)[...].astype(F32)
         quarter(b_s, p, q)[...] = total.astype(BF)
 
-    def sum_0(p):
-        act((0,), lambda place: None, hops(0, p, 3, 2, 1))
-        act((3,), lambda place: None, hops(1, p, 0, 1, 2))
-
-    def relay(kind, p, q):
+    def sum_0(place, p):
+        kind, blocks = (0, (3, 2, 1)) if place == 0 else (1, (0, 1, 2))
+        send(place, *[hop(kind, p, q, place) for q in blocks])
+
+    def rel(place, kind, q, p):
         hop_wait(kind, p, q)
-        add_quarter(p, q, [wu if kind == 0 else wd])
-
-    def sum_1(p):
-        act((1,), lambda place: relay(0, p, 3), hops(0, p, 3))
-        act((2,), lambda place: relay(1, p, 0), hops(1, p, 0))
-        act((1,), lambda place: relay(0, p, 2), hops(0, p, 2))
-        act((2,), lambda place: relay(1, p, 1), hops(1, p, 1))
-
-    def sum_2(p):
-        act((2,), lambda place: relay(0, p, 3), hops(0, p, 3))
-        act((1,), lambda place: relay(1, p, 0), hops(1, p, 0))
+        add_quarter(p, q, [wd if kind else wu])
+        send(place, hop(kind, p, q, place))
 
     def cross(p, place):
-        return pltpu.make_async_remote_copy(
-            src_ref=quarter(b_s, p, place), dst_ref=rxb.at[p], send_sem=hss.at[4 + p],
-            recv_sem=hrs.at[4 + p], device_id=TO_X, device_id_type=MESH,
-        )
-
-    def sum_3(p):
-        def body(place):
-            refs = []
-            if place > 0:
-                hop_wait(0, p, place)
-                refs.append(wu)
-            if place < 3:
-                hop_wait(1, p, place)
-                refs.append(wd)
-            add_quarter(p, place, refs)
-
-        act(EVERY, body, [lambda place: cross(p, place)])
-
-    def sum_4(p):
-        def body(place):
-            cross(p, place).wait_recv()
-            total = quarter(b_s, p, place)[...].astype(F32) + rxb[p].astype(F32)
-            quarter(fb, p, place)[...] = total.astype(BF)
-
-        for place in EVERY:
-            sends = hops(2, p, place) if place < 3 else []
-            sends += hops(3, p, place) if place > 0 else []
-            act((place,), body, sends)
-
-    def sum_5(p):
-        act((1,), lambda place: hop_wait(2, p, 0), hops(2, p, 0))
-        act((2,), lambda place: hop_wait(3, p, 3), hops(3, p, 3))
-        act((1,), lambda place: hop_wait(3, p, 2), hops(3, p, 2))
-        act((2,), lambda place: hop_wait(2, p, 1), hops(2, p, 1))
-
-    def sum_6(p):
-        act((1,), lambda place: hop_wait(3, p, 3), hops(3, p, 3))
-        act((2,), lambda place: hop_wait(2, p, 0), hops(2, p, 0))
+        return lambda: pltpu.make_async_remote_copy(
+            src_ref=quarter(b_s, p, place), dst_ref=rxb.at[p], send_sem=hss.at[4, p],
+            recv_sem=hrs.at[4, p], device_id=TO_X, device_id_type=MESH,
+        )
+
+    def sum_3(place, p):
+        refs = []
+        if place > 0:
+            hop_wait(0, p, place)
+            refs.append(wu)
+        if place < 3:
+            hop_wait(1, p, place)
+            refs.append(wd)
+        add_quarter(p, place, refs)
+        send(place, cross(p, place))
+
+    def sum_4(place, p):
+        cross(p, place)().wait_recv()
+        total = quarter(b_s, p, place)[...].astype(F32) + rxb[p].astype(F32)
+        quarter(fb, p, place)[...] = total.astype(BF)
+        if place < 3:
+            send(place, hop(2, p, place, place))
+        if place > 0:
+            send(place, hop(3, p, place, place))
+
+    def fw(place, kind, q, p):
+        hop_wait(kind, p, q)
+        send(place, hop(kind, p, q, place))
 
     def piece_copies(p):
         if p == 0:
@@ -731,51 +774,58 @@
             ]
         copies = []
         for n, (src, dst) in enumerate(pairs):
-            copies.append(local(src, dst, 23 + p * 3 + n))
+            copies.append(local(src, dst, 43 + p * 3 + n))
             copies.append(remote(src, dst, 18 + p * 3 + n, TO_CORE))
         return copies
 
-    def sum_7(p):
-        def body(place):
-            for q in range(4):
-                if place == 0 and q > 0:
-                    hop_wait(3, p, q)
-                if place == 3 and q < 3:
-                    hop_wait(2, p, q)
-
-        act((0, 3), body)
+    def sum_7(place, p):
+        for q in range(4):
+            if place == 0 and q > 0:
+                hop_wait(3, p, q)
+            if place == 3 and q < 3:
+                hop_wait(2, p, q)
         for item in piece_copies(p):
             item.start()
 
-    plan = {
-        0: [],
-        1: [lambda: ffn_x(1)],
-        2: [lambda: sum_1(0)],
-        3: [lambda: ffn_z(1)],
-        4: [lambda: ffn_x(2), lambda: sum_2(0)],
-        5: [lambda: sum_3(0), lambda: sum_1(1)],
-        6: [lambda: ffn_z(2)],
-        7: [lambda: ffn_x(3), lambda: sum_4(0), lambda: sum_2(1), lambda: out_copies(out_o, 0)[1].start()],
-        8: [lambda: sum_5(0), lambda: sum_3(1), lambda: sum_1(2)],
-        9: [],
-        10: [lambda: sum_6(0), lambda: sum_4(1), lambda: sum_2(2)],
-        11: [lambda: sum_7(0), lambda: sum_5(1), lambda: sum_3(2), lambda: sum_1(3), lambda: ffn_own()],
-        12: [lambda: sum_6(1), lambda: sum_4(2), lambda: sum_2(3)],
-        13: [lambda: sum_7(1), lambda: sum_5(2), lambda: sum_3(3)],
-        14: [
-            lambda: sum_6(2), lambda: sum_4(3), lambda: ffn_last(), lambda: sum_7(2),
-            lambda: sum_5(3), lambda: sum_6(3), lambda: sum_7(3),
-        ],
-    }
-
-    def slot(number):
-        for task in plan[number]:
-            task()
+    def wl(place, k):
+        for item in z_copies(place - k, 0, RIGHT, False):
+            item.wait_recv()
+        if place < 3:
+            start_all(z_copies(place - k, 0, RIGHT, False))
+        start_all(y_copies(place - k, grp))
+
+    def wr(place, k):
+        for item in z_copies(place + k, 1, LEFT, False):
+            item.wait_recv()
+        if place > 0:
+            start_all(z_copies(place + k, 1, LEFT, False))
+        start_all(y_copies(place + k, grp))
+
+    def cross_rows(out_ref, number, part):
+        rows = rows_of((1 - x) * 256 + part * 128, 128)
+        return remote(
+            xs.at[number, rows], out_ref.at[x, pl.ds(part * 128, 128)], 12 + number * 2 + part, TO_X
+        )
+
+    def ox(place, part):
+        cross_rows(out_o, 0, part).start()
+
+    def gx(place, part):
+        cross_rows(gin_o, 1, part).start()
+
+    jobs = (ffn_x, ffn_z, ffn_own, ffn_last, sum_0, rel, sum_3, sum_4, fw, sum_7, wl, wr, xs_, zs, xo, ox, gx)
+
+    def slot(name, here=None):
+        for place, names in PLAN.get(name, {}).items():
+            @pl.when(z == place if here is None else (z == place) & here)
+            def _(place=place, names=names):
+                for job, *rest in names:
+                    jobs[job](place, *rest)
 
     local(adaw_h, adaw, 1).wait()
     for part in range(6):
-        span = pl.ds(part * D, D)
-        mod2[:, span] = dot(cond[...], adaw[:, span]) + adab[:, span]
+        lanes = pl.ds(part * D, D)
+        mod2[:, lanes] = dot(cond[...], adaw[:, lanes]) + adab[:, part * D : (part + 1) * D]
     modrow = mod2[pl.ds(x, 1), :]
     shift_one, scale_one, gate_one, shift_two, scale_two, gate_two = [
         modrow[:, part * D : (part + 1) * D] for part in range(6)
@@ -787,8 +837,8 @@
         return center * inv, inv
 
     TILE = 64
-    mul_one = again[...] * (1.0 + scale_one)
-    mul_two = fgain[...] * (1.0 + scale_two)
+    mul_one = again * (1.0 + scale_one)
+    mul_two = fgain * (1.0 + scale_two)
 
     def norm_one_block(block):
         @pl.loop(0, 256 // TILE)
@@ -807,42 +857,42 @@
     for item in loads[2:15]:
         item.wait()
 
-    def project_block(block):
-        @pl.loop(0, 2)
-        def _(half_core):
-            start = half_core * 512 + block * 256
-            rows = rows_of(start, 256)
-            tile = ai[rows]
-            ait[:, rows] = tile.T
-            cos_t, sin_t = cos_v[rows], sin_v[rows]
-
-            @pl.loop(0, 3)
-            def _(p):
-                projected = dot(tile, wq[p])
-                query = projected[:, :128]
-                key = projected[:, 128:256]
-                value = projected[:, 256:].astype(BF)
-                query = (query * cos_t + swap_halves(query) * sin_t).astype(BF)
-                key = (key * cos_t + swap_halves(key) * sin_t).astype(BF)
-                q_s[p, rows] = query * jnp.asarray(0.125, BF)
-                k_s[p, rows] = key
-                v_s[p, rows] = value
-                kt_s[p, :, rows] = key.T
-                vt_s[p, :, rows] = value.T
+    def project_rows(start):
+        rows = rows_of(start, 256)
+        tile = ai[rows]
+        cos_t, sin_t = cos_v[rows], sin_v[rows]
+
+        @pl.loop(0, 3)
+        def _(p):
+            projected = dot(tile, wq[p])
+            query = projected[:, :128]
+            key = projected[:, 128:256]
+            value = projected[:, 256:].astype(BF)
+            query = (query * cos_t + swap_halves(query) * sin_t).astype(BF)
+            key = (key * cos_t + swap_halves(key) * sin_t).astype(BF)
+            q_s[p, rows] = query * jnp.asarray(0.125, BF)
+            k_s[p, rows] = key
+            v_s[p, rows] = value
+            kt_s[p, :, rows] = key.T
+            vt_s[p, :, rows] = value.T
+
+        ait[:, rows] = tile.T
 
     loads[0].wait()
     norm_one_block(x)
     core_rows(ai, own + x * 256, 256, 2).start()
+    project_rows(own + x * 256)
     core_rows(ai, other + x * 256, 256, 2).wait_recv()
-    project_block(x)
+    project_rows(other + x * 256)
     swap_x.wait_recv()
     norm_one_block(1 - x)
     core_rows(ai, own + (1 - x) * 256, 256, 3).start()
+    project_rows(own + (1 - x) * 256)
     core_rows(ai, other + (1 - x) * 256, 256, 3).wait_recv()
-    project_block(1 - x)
-    for item in loads[16:19] + loads[20:]:
+    project_rows(other + (1 - x) * 256)
+    for item in loads[16:18]:
         item.wait()
-    weight_step(1)
+    slot((AT_W, 0))
 
     low_lane = lax.broadcasted_iota(jnp.int32, (1, 128), 1) < 64
     keep = [low_lane.astype(F32).astype(BF), (~low_lane).astype(F32).astype(BF)]
@@ -856,40 +906,53 @@
         )
 
     def attend(p):
-        @pl.loop(0, 4)
+        @pl.loop(0, 2)
         def _(t):
-            cols = rows_of(t * 256, 256)
+            cols = rows_of(t * 512, 512)
             query = q_s[p, cols]
-            keys = k_s[p]
             outs = []
             for h in range(2):
                 masked = query * keep[h]
-                scores = dot_t(keys, masked)
-                top = jnp.max(scores, axis=0, keepdims=True)
-                expd = jnp.exp(scores - top)
-                total = jnp.sum(expd, axis=0, keepdims=True)
+                held = (oacc, gacc)[h]
+                top = None
+                for i in range(4):
+                    keys = pl.ds(i * 256, 256)
+                    scores = dot_t(k_s[p, keys], masked)
+                    held[keys, :512] = scores
+                    top = scores if top is None else jnp.maximum(top, scores)
+                top = jnp.max(top, axis=0, keepdims=True)
+                out, total = None, None
+                for i in range(4):
+                    keys = pl.ds(i * 256, 256)
+                    expd = jnp.exp(held[keys, :512] - top)
+                    part = dot(vt_s[p, pl.ds(h * 64, 64), keys], expd.astype(BF))
+                    out = part if out is None else out + part
+                    total = expd if total is None else total + expd
+                total = jnp.sum(total, axis=0, keepdims=True)
                 lse[p, pl.ds(h, 1), cols] = top + jnp.log(total)
-                out = dot(vt_s[p, pl.ds(h * 64, 64), :], expd.astype(BF)) / total
+                out = out / total
                 ot_s[p, pl.ds(h * 64, 64), cols] = out
                 outs.append(out)
             natural = jnp.concatenate(outs, axis=0).T.astype(BF)
             lanes = pl.ds(pl.multiple_of(c * 384 + p * 128, 128), 128)
 
-            @pl.when(t // 2 == c)
+            @pl.when(t == c)
             def _():
-                att[rows_of((t % 2) * 256, 256), lanes] = natural
-
-            @pl.when(t // 2 != c)
+                att[:, lanes] = natural
+
+            @pl.when(t != c)
             def _():
-                att_s[rows_of((t % 2) * 256, 256), pl.ds(p * 128, 128)] = natural
+                att_s[:, pl.ds(p * 128, 128)] = natural
+
+            for n in range(2):
+                slot((AT_A, p, n), t == n)
 
         att_copy(p, True).start()
 
     attend(0)
     attend(1)
-    weight_step(2)
-
-    loads[19].wait()
+
+    loads[18].wait()
     swap_c.wait_recv()
 
     @pl.loop(0, 512 // TILE)
@@ -934,19 +997,21 @@
             fi[rows_of(own + at, TILE)] = (normed * mul_two + shift_two).astype(BF)
 
     core_rows(fi, own, 512, 8).start()
+    slot((AT_W, 1))
+
+    def turn(src, dst, start):
+        @pl.loop(0, 2)
+        def _(t):
+            rows = rows_of(start + t * 256, 256)
+            dst[:, rows] = src[rows].T
+
+    turn(gf, gft, own)
     core_rows(gf, other, 512, 7).wait_recv()
-
-    @pl.loop(0, 4)
-    def _(t):
-        rows = rows_of(t * 256, 256)
-        gft[:, rows] = gf[rows].T
-
+    turn(gf, gft, other)
+    turn(fi, fit, own)
     core_rows(fi, other, 512, 8).wait_recv()
-
-    @pl.loop(0, 4)
-    def _(t):
-        rows = rows_of(t * 256, 256)
-        fit[:, rows] = fi[rows].T
+    turn(fi, fit, other)
+    slot((AT_W, 2))
 
     coef = 0.7978845608028654
 
@@ -954,15 +1019,10 @@
     def _(k):
         j = pick([order(n) for n in range(Z)], k)
 
-        @pl.when(k == 2)
-        def _():
-            weight_step(3)
-
-        @pl.when(k == 3)
-        def _():
-            ffn_x(0)
-
-        @pl.when(k < 3)
+        for n in range(Z):
+            slot((AT_F, n), k == n)
+
+        @pl.when(k != OWN_STEP)
         def _():
             for item in y_copies(j, 1 - grp):
                 item.wait_recv()
@@ -979,25 +1039,25 @@
             act = (0.5 * pre * (1.0 + th)).astype(BF)
             slope = 0.5 * (1.0 + th) + 0.5 * pre * (1.0 - th * th) * coef * (1.0 + 3.0 * 0.044715 * sq)
             a_s[rows] = act
-            grad_act = dot_t(gf[rows, :384], wd[j, :384]) + dot_t(gf[rows, 384:], wd[j, 384:])
-            grad_pre = (grad_act * slope).astype(BF)
+            grad_pre = (dot_t(gf[rows], wd[j]) * slope).astype(BF)
             gp_s[rows] = grad_pre
             bsum = jnp.sum(grad_pre.astype(F32), axis=0, keepdims=True)
-            out_a = dot(act, wd[j, :384])
-            out_b = dot(act, wd[j, 384:])
+            out = dot(act, wd[j])
             gin = dot_t(grad_pre, wu[j])
 
             @pl.when(k == 0)
             def _():
-                oacc[rows, :384] = out_a
-                oacc[rows, 384:] = out_b
+                oacc[rows] = out
                 gacc[rows] = gin
 
             @pl.when(k > 0)
             def _():
-                oacc[rows, :384] += out_a
-                oacc[rows, 384:] += out_b
+                oacc[rows] += out
                 gacc[rows] += gin
+
+            for m in range(Z):
+                for n in range(4):
+                    slot((AT_T, m, n), (k == m) & (t == n))
 
             @pl.when(t == 0)
             def _():
@@ -1013,7 +1073,8 @@
             g_s[0, j, rows] = dot(fit[rows], gp_s[...]).astype(BF)
             g_s[1, j, rows] = dot(gft[rows], a_s[...]).astype(BF)
 
-        ffn_copy(j).start()
+        for n in range(Z):
+            slot((AT_G, n), k == n)
 
     def give_credit():
         @pl.when(z > 0)
@@ -1109,30 +1170,27 @@
 
     gproj = gf
     core_rows(gproj, own, 512, 11).start()
-    slot(0)
+    slot((AT_N, 1))
 
     remote(osend, orecv, 10, TO_CORE).wait()
 
     def rows_out(number, i, values):
         xs[number, rows_of(i * TILE, TILE)] = values.astype(BF)
 
-    def out_copies(out_ref, number):
-        here, there = rows_of(x * 256, 256), rows_of((1 - x) * 256, 256)
-        return [
-            local(xs.at[number, here], out_ref.at[x], 35 + number),
-            remote(xs.at[number, there], out_ref.at[x], 12 + number, TO_X),
-        ]
+    def out_copy(out_ref, number):
+        return local(xs.at[number, rows_of(x * 256, 256)], out_ref.at[x], 55 + number)
 
     @pl.loop(0, 512 // TILE)
     def _(i):
         tile = rows_of(i * TILE, TILE)
-        ffn = oacc[rows_of(own + i * TILE, TILE)] + orecv[tile].astype(F32) + downb[...]
+        ffn = oacc[rows_of(own + i * TILE, TILE)] + orecv[tile].astype(F32) + downb
         vec[5:6] += jnp.sum(ctb[tile].astype(F32) * ffn, axis=0, keepdims=True)
         rows_out(0, i, xb[tile].astype(F32) + gate_one * ap[tile] + gate_two * ffn)
 
-    out_copies(out_o, 0)[0].start()
+    out_copy(out_o, 0).start()
 
     core_rows(gproj, other, 512, 11).wait_recv()
+    slot((AT_N, 2))
 
     @pl.loop(0, 4)
     def _(t):
@@ -1147,6 +1205,8 @@
                     product[h * 64 : (h + 1) * 64], axis=0, keepdims=True
                 )
 
+    slot((AT_N, 3))
+
     for p in range(3):
         @pl.loop(0, 2)
         def _(n):
@@ -1156,8 +1216,7 @@
             ).astype(BF)
 
     take_credit()
-    sum_0(0)
-    slot(1)
+    slot((AT_N, 4))
 
     def attend_back(p):
         for h in range(2):
@@ -1184,11 +1243,8 @@
             gq[rows, pl.ds(128, 128)] = (dk * cos_t - swap_halves(dk) * sin_t).astype(BF)
             gq[rows, pl.ds(256, 128)] = dv.astype(BF)
 
-            @pl.when(t == 1)
-            def _():
-                slot(2 + 3 * p)
-
-        slot(3 + 3 * p)
+            for n in range(4):
+                slot((AT_B, p, n), t == n)
 
         @pl.loop(0, 4)
         def _(t):
@@ -1206,7 +1262,7 @@
             rows = rows_of(r * 256, 256)
             b_s[1 + p, rows] = dot(ait[rows], gq[...]).astype(BF)
 
-        sum_0(1 + p)
+        slot((AT_B, p, 5))
 
         @pl.loop(0, 4)
         def _(t):
@@ -1217,7 +1273,7 @@
             else:
                 gacc[rows] += part
 
-        slot(4 + 3 * p)
+        slot((AT_B, p, 6))
 
     remote(gsend, grecv, 9, TO_CORE).wait_send()
     for p in range(3):
@@ -1227,9 +1283,9 @@
     def _(i):
         gsend[rows_of(i * TILE, TILE)] = gacc[rows_of(other + i * TILE, TILE)].astype(BF)
 
-    remote(gsend, grecv, 14, TO_CORE).start()
-    slot(11)
-    remote(gsend, grecv, 14, TO_CORE).wait()
+    remote(gsend, grecv, 11 + 26, TO_CORE).start()
+    slot((AT_E, 0))
+    remote(gsend, grecv, 11 + 26, TO_CORE).wait()
 
     @pl.loop(0, 512 // TILE)
     def _(i):
@@ -1241,13 +1297,13 @@
         vec[1:2] += jnp.sum(grad * normed, axis=0, keepdims=True)
         rows_out(1, i, gm[tile] + norm_back(grad * mul_one, normed, i1[tile]))
 
-    for item in out_copies(gin_o, 1):
-        item.start()
+    out_copy(gin_o, 1).start()
+    slot((AT_E, 1))
     sums = vec[...]
     vec[6:7] = sums[1:2] * (1.0 + scale_one)
     vec[7:8] = sums[4:5] * (1.0 + scale_two)
-    vec[1:2] = sums[1:2] * again[...]
-    vec[4:5] = sums[4:5] * fgain[...]
+    vec[1:2] = sums[1:2] * again
+    vec[4:5] = sums[4:5] * fgain
     for core in range(2):
         @pl.when(c == core)
         def _():
@@ -1257,7 +1313,7 @@
     both = cond[...].astype(F32)
     vec[13:14, :128] = 0.5 * jnp.where(x == 0, both[0:1], both[1:2])
     remote(vec, vecr, 30, TO_CORE).start()
-    slot(12)
+    slot((AT_E, 2))
     remote(vec, vecr, 30, TO_CORE).wait_recv()
     chip = 2 * z + x
     vall[chip] = vec[...] + vecr[...]
@@ -1270,56 +1326,25 @@
 
     for n in range(len(peers)):
         vec_copy(n, chip).start()
-    slot(13)
+    slot((AT_D, 0))
     for n in range(len(peers)):
         vec_copy(n, 2 * peers[n]["mlp"] + peers[n]["seq"] // 2).wait_recv()
 
-    high = lax.Precision.HIGHEST
-    everyone = vall[:, 13, :128]
-    total = vall[0]
-    for n in range(1, 8):
-        total = total + vall[n]
-    acc = None
-    ada_out = []
-    sstage[...] = jnp.zeros_like(sstage)
-    for part in range(6):
-        span = pl.ds(part * D, D)
-        grads = vall[:, part, :]
-        sstage[part : part + 1] = total[part : part + 1]
-        oacc[pl.ds(part * 128, 128)] = lax.dot_general(
-            everyone, grads, (((0,), (0,)), ((), ())), precision=high, preferred_element_type=F32
-        )
-        ada_out.append(local(oacc.at[pl.ds(part * 128, 128)], adaw_o.at[:, span], 37 + part))
-        ada_out[-1].start()
-        piece = lax.dot_general(
-            grads, adaw[:, span].astype(F32), (((1,), (1,)), ((), ())), precision=high,
-            preferred_element_type=F32,
-        )
-        acc = piece if acc is None else acc + piece
-    cstage[...] = acc
-    for n in range(3):
-        sstage[6 + n : 7 + n] = total[6 + n : 7 + n]
-    for core in range(2):
-        halves = [total[9 + 2 * core + j // 2, (j % 2) * 384 : (j % 2 + 1) * 384] for j in range(4)]
-        mine = halves[0]
-        for j in range(1, 4):
-            mine = jnp.where(z == j, halves[j], mine)
-        sstage[9, pl.ds(core * 384, 384)] = mine
-    cond_o[...] = cstage[pl.ds(2 * z, 2), :]
-    small_o[...] = sstage[...]
-    slot(14)
-    for item in ada_out:
-        item.wait()
+    vall_out = local(vall, vall_o, 57)
+    vall_out.start()
+    vall_out.wait()
 
     for number, ref in ((0, out_o), (1, gin_o)):
-        out_copies(ref, number)[0].wait()
-        out_copies(ref, number)[1].wait()
+        out_copy(ref, number).wait()
+        for part in range(2):
+            cross_rows(ref, number, part).wait()
     for p in range(4):
         for item in piece_copies(p):
             item.wait()
-    for first, (src, kind) in enumerate(((g_s.at[x, z], x), (fxr, 1 - x))):
-        for item in final_copies(src, kind, first):
+    for h in range(CH):
+        for item in final_copies(g_s.at[x, z, span(h)], x, h, 0) + final_copies(fxr.at[span(h)], 1 - x, h, 1):
             item.wait()
+        own_copy(h).wait_send()
     for n in range(len(peers)):
         vec_copy(n, chip).wait_send()
     swap_x.wait_send()
@@ -1329,15 +1354,93 @@
     core_rows(fi, own, 512, 8).wait_send()
     core_rows(gproj, own, 512, 11).wait_send()
     remote(vec, vecr, 30, TO_CORE).wait_send()
-    remote(g_s.at[x, z], fxr, 15, TO_X).wait_send()
-    for j in range(4):
-        ffn_copy(j).wait_send()
-    for place in EVERY:
+    for place in range(Z):
         @pl.when(z == place)
         def _(place=place):
-            for where, make in pending:
-                if where == place:
-                    make(place).wait_send()
+            for make in pending[place]:
+                make().wait_send()
+
+
+def finish_kernel(
+    out_h, gin_h, qkv_h, outw_h, ffn_h, vall_h, adaw_h,
+    out_o, gin_o, cond_o, again_o, adaw_o, adab_o, qkv_o, outw_o, fgain_o, up_o, upb_o, down_o, downb_o,
+    tok_b, qkv_b, outw_b, ffn_b, adaw, vall, tok_f, qkv_f, outw_f, ffn_f, adaw_f, cond_s, isem, osem,
+):
+    z = lax.axis_index("mlp")
+    D = 768
+    loads, steps = [], []
+
+    def step(src, buffer, result, dst, turn=False):
+        number = len(steps)
+        loads.append(pltpu.make_async_copy(src, buffer, isem.at[number]))
+        store = pltpu.make_async_copy(result, dst, osem.at[number])
+
+        def body():
+            loads[number].wait()
+            values = buffer[...].astype(F32)
+            result[...] = values.T if turn else values
+            store.start()
+
+        steps.append((body, store))
+
+    vall_copy = pltpu.make_async_copy(vall_h, vall, isem.at[30])
+    adaw_copy = pltpu.make_async_copy(adaw_h, adaw, isem.at[31])
+    for n in range(6):
+        rows = pl.ds(n * 128, 128)
+        step(qkv_h.at[rows], qkv_b.at[rows], qkv_f.at[rows], qkv_o.at[rows])
+    for n in range(2):
+        rows = pl.ds(n * 384, 384)
+        step(outw_h.at[rows], outw_b.at[rows], outw_f.at[rows], outw_o.at[rows])
+        step(ffn_h.at[0, rows], ffn_b.at[0, rows], ffn_f.at[0, rows], up_o.at[rows])
+    for n in range(3):
+        rows = pl.ds(n * 256, 256)
+        step(ffn_h.at[1, rows], ffn_b.at[1, rows], ffn_f.at[1, :, rows], down_o.at[:, rows], True)
+    for n in range(2):
+        step(out_h.at[n], tok_b.at[0, n], tok_f.at[0, n], out_o.at[n])
+        step(gin_h.at[n], tok_b.at[1, n], tok_f.at[1, n], gin_o.at[n])
+    for item in loads[:6] + [vall_copy, adaw_copy] + loads[6:]:
+        item.start()
+    for body, _ in steps[:6]:
+        body()
+    vall_copy.wait()
+    adaw_copy.wait()
+    high = lax.Precision.HIGHEST
+    everyone = vall[:, 13, :128]
+    total = vall[0]
+    for n in range(1, 8):
+        total = total + vall[n]
+    acc, ada_out = None, []
+    for part in range(6):
+        lanes = pl.ds(part * D, D)
+        grads = vall[:, part, :]
+        adab_o[lanes] = total[part]
+        adaw_f[part] = lax.dot_general(
+            everyone, grads, (((0,), (0,)), ((), ())), precision=high, preferred_element_type=F32
+        )
+        ada_out.append(pltpu.make_async_copy(adaw_f.at[part], adaw_o.at[:, lanes], osem.at[26 + part]))
+        ada_out[-1].start()
+        piece = lax.dot_general(
+            grads, adaw[:, lanes].astype(F32), (((1,), (1,)), ((), ())), precision=high,
+            preferred_element_type=F32,
+        )
+        acc = piece if acc is None else acc + piece
+    for body, _ in steps[6:]:
+        body()
+    cond_s[...] = acc
+    cond_o[...] = cond_s[pl.ds(2 * z, 2), :]
+    again_o[...] = total[6]
+    fgain_o[...] = total[7]
+    downb_o[...] = total[8]
+    for core in range(2):
+        halves = [total[9 + 2 * core + j // 2, (j % 2) * 384 : (j % 2 + 1) * 384] for j in range(4)]
+        mine = halves[0]
+        for j in range(1, 4):
+            mine = jnp.where(z == j, halves[j], mine)
+        upb_o[pl.ds(core * 384, 384)] = mine
+    for item in ada_out:
+        item.wait()
+    for _, store in steps:
+        store.wait()
 
 
 def tables(seg_len, seq_size):
@@ -1365,12 +1468,11 @@
     tabs = [jnp.asarray(t) for t in tables(inputs.shape[1], lax.axis_size("seq"))]
     hbm, vm = pl.BlockSpec(memory_space=pl.ANY), pl.BlockSpec(memory_space=pltpu.VMEM)
     shape = jax.ShapeDtypeStruct
-    row = lambda v: v.reshape(1, -1)
     V = pltpu.VMEM
     dma = pltpu.SemaphoreType.DMA
     scratch = [
         V((128, 4608), BF), V((3, 768, 384), BF), V((768, 768), BF), V((Z, 768, 384), BF),
-        V((Z, 768, 384), BF), V((Z, 1, 768), F32), V((1024, 128), F32), V((1024, 128), F32),
+        V((Z, 384, 768), BF), V((Z, 1, 768), F32), V((1024, 128), F32), V((1024, 128), F32),
         V((32, 1024), F32), V((32, 1024), F32),
         V((512, 768), BF), V((512, 768), BF), V((2, 4608), F32), V((512, 768), F32), V((512, 1), F32),
         V((1024, 768), BF), V((768, 1024), BF),
@@ -1384,36 +1486,51 @@
         V((512, 768), F32), V((3, 1024, 128), BF), V((3, 2, 1024), F32), V((128, 1024), F32),
         V((1024, 384), BF), V((4, 768, 384), BF), V((2, 512, 768), BF),
         V((16, 768), F32), V((16, 768), F32), V((2 * Z, 16, 768), F32), V((Z, 1, 384), F32),
-        V((2 * Z, 128), F32), V((16, 768), F32),
         V((Z, 768, 384), BF), V((Z, 768, 384), BF), V((768, 384), BF), V((4, 192, 384), BF),
         V((4, 768, 384), BF),
-        dma((43,)), dma((31,)), dma((31,)), dma((2, Z, 3)), dma((2, Z, 3)), dma((Z, 2)), dma((Z, 2)),
-        dma((3,)), dma((4,)), dma((4, 4, 4)), dma((4, 4, 4)), dma((8,)), dma((8,)), dma((7,)), dma((7,)),
+        dma((63,)), dma((38,)), dma((38,)), dma((2, Z, 3)), dma((2, Z, 3)), dma((Z, 2)), dma((Z, 2)),
+        dma((Z, 3)), dma((Z, 3)), dma((4, 4, 4)), dma((4, 4, 4)), dma((6, 4)), dma((6, 4)), dma((7,)), dma((7,)),
         pltpu.SemaphoreType.REGULAR((2,)),
     ]
     token = shape(inputs.shape, BF)
-    out, gin, grad_cond, grad_ada, small, grad_qkv, grad_out, ffn = pl.pallas_call(
+    vall_shape = shape((2 * Z, 16, 768), F32)
+    ffn_shape = shape((2, 768, 768), BF)
+    out, gin, qkv, outw, ffn, vall = pl.pallas_call(
         fast_kernel,
         out_shape=[
-            token, token, shape(condition.shape, F32), shape(ada_weight.shape, F32), shape((16, 768), F32),
-            shape(qkv_weight.shape, BF), shape(out_weight.shape, BF), shape((2, 768, 768), BF),
+            token, token, shape(qkv_weight.shape, BF), shape(out_weight.shape, BF), ffn_shape, vall_shape,
         ],
         in_specs=[hbm, vm, vm, hbm, vm, hbm, hbm, vm, hbm, vm, hbm, vm, hbm, hbm, hbm, hbm, hbm],
-        out_specs=[hbm, hbm, vm, hbm, vm, hbm, hbm, hbm],
+        out_specs=[hbm] * 6,
         scratch_shapes=scratch,
         compiler_params=pltpu.CompilerParams(
             collective_id=0, has_side_effects=True, vmem_limit_bytes=VMEM_LIMIT
         ),
         name="block",
     )(
-        inputs, condition, row(attn_gain), ada_weight, row(ada_bias), qkv_weight, out_weight,
-        row(ffn_gain), up_weight, row(up_bias), down_weight, row(down_bias), cotangent, *tabs,
-    )
-    wide = lambda v: v.astype(F32)
-    return (
-        wide(out), wide(gin), grad_cond, small[6], grad_ada, small[:6].reshape(-1), wide(grad_qkv),
-        wide(grad_out), small[7], wide(ffn[0]), small[9], wide(ffn[1]).T, small[8],
-    )
+        inputs, condition, attn_gain, ada_weight, ada_bias, qkv_weight, out_weight,
+        ffn_gain, up_weight, up_bias, down_weight, down_bias, cotangent, *tabs,
+    )
+    same = lambda v: shape(v.shape, F32)
+    tokens = shape(inputs.shape, F32)
+    return pl.pallas_call(
+        finish_kernel,
+        out_shape=[
+            tokens, tokens, same(condition), same(attn_gain), same(ada_weight), same(ada_bias),
+            same(qkv_weight), same(out_weight), same(ffn_gain), same(up_weight), same(up_bias),
+            same(down_weight), same(down_bias),
+        ],
+        in_specs=[hbm] * 7,
+        out_specs=[hbm, hbm, vm, vm, hbm, vm, hbm, hbm, vm, hbm, vm, hbm, vm],
+        scratch_shapes=[
+            V((2, *inputs.shape), BF), V(qkv_weight.shape, BF), V(out_weight.shape, BF), V((2, 768, 768), BF),
+            V(ada_weight.shape, BF), V((2 * Z, 16, 768), F32), V((2, *inputs.shape), F32),
+            V(qkv_weight.shape, F32), V(out_weight.shape, F32), V((2, 768, 768), F32), V((6, 128, 768), F32),
+            V((2 * Z, 128), F32), dma((32,)), dma((32,)),
+        ],
+        compiler_params=pltpu.CompilerParams(vmem_limit_bytes=VMEM_LIMIT),
+        name="finish",
+    )(out, gin, qkv, outw, ffn, vall, ada_weight)
 
 
 def solution(mesh):

time: 271 us -> 199 us (0.73)
  Pallas kernels: 245 us -> 198 us
  other arithmetic: 13 us -> 0 us
  local copies, waits for them, and re-layouts: 12.4 us -> 0 us
    pallas_call x1 -> x2, Pallas kernels: 245 us -> 198 us  [the longest x1 185 us: fast_shards(): pl.pallas_call(fast_kernel, out_shape=[token, token, shape(qkv_weight.sha...]
    convert_element_type x4 -> x0, other arithmetic: 9.65 us -> none  [fast_shards(): wide = lambda v: v.astype(F32)]
    reshape x6 -> x0, local copies, waits for them, and re-layouts: 7.02 us -> none  [the longest x5 6.41 us: fast_shards(): row = lambda v: v.reshape(1, -1)]
    unnamed x15 -> x0, local copies, waits for them, and re-layouts: 3.93 us -> none
    transpose x1 -> x0, other arithmetic: 3.39 us -> none  [fast_shards(): wide(ffn[1])]
where the time goes in v3:
time: 199 us; the launch traced here: 198 us
  Pallas kernels  198 us (99%)
    pallas_call x1, Pallas kernels, fast_shards(): pl.pallas_call(fast_kernel, out_shape=[token, token, shape(qkv_weight.sha...  185 us
    pallas_call x1, Pallas kernels, fast_shards(): pl.pallas_call(finish_kernel, out_shape=[tokens, tokens, same(condition),...  12.3 us

profile of v3, /device:TPU:0, one launch (start us, length us, event | category | flops | bytes accessed | tf_op | source)
XLA Modules:
  0.0 198.5 jit_solution(9796239762007145934)
XLA Ops:
  0.6 185.4 %block.1 = (bf16[2,256,768]{2,1,0:T(8,128)(2,1)}, bf16[2,256,768]{2,1,0:T(8,128)(2,1)}, bf16[768,2304]{1,0:T(8,128)(2,1)}, bf16[768,768]{1,0:T(8,128)(2,1)}, bf1...) custom-call(bf16[2,256,768]{2,1,0:T(8,128)(2,1)} %inputs.1, bf16[2,128]{1,0:T(2,128)(2,1)} %cond.1, f32[768]{0:T(1024)} %again.1, ...), custom_call_target="tpu_custom_call" | custom-call | tf_op jit(solution)/shard_map/block/pallas_call | solution.py:1498
  186.0 12.3 %finish.1 = (f32[2,256,768]{2,1,0:T(8,128)}, f32[2,256,768]{2,1,0:T(8,128)}, f32[2,128]{1,0:T(2,128)}, f32[768]{0:T(1024)}, f32[128,4608]{1,0:T(8,128)}, /*index...) custom-call(bf16[2,256,768]{2,1,0:T(8,128)(2,1)} %get-tuple-element., ...), custom_call_target="tpu_custom_call" | custom-call | tf_op jit(solution)/shard_map/finish/pallas_call | solution.py:1516

commit v4 on v3

--- a/solution.py
+++ b/solution.py
@@ -9,7 +9,7 @@
 from jax.sharding import PartitionSpec as P
 
 HEADS = 12
-VMEM_LIMIT = 62 * 2**20
+VMEM_LIMIT = 63 * 2**20
 
 
 gelu_coef = 0.7978845608028654
@@ -355,104 +355,100 @@
     )
 
 
-FFN_X, FFN_Z, FFN_OWN, FFN_LAST, SUM_0, REL, SUM_3, SUM_4, FW, SUM_7, WL, WR, XS_, ZS, XO, OX, GX = range(17)
+FFN_X, FFN_Z, FFN_OWN, FFN_LAST, SUM_0, REL, SUM_3, SUM_4, FW, SUM_7, WL, WR, XS_, ZS, XO, OX, GX, WD_ = range(18)
 AT_W, AT_F, AT_A, AT_T, AT_N, AT_B, AT_E, AT_D, AT_G = range(9)
-ORDERS = ((1, 2, 0, 3), (0, 2, 1, 3), (3, 1, 2, 0), (2, 1, 3, 0))
-OWN_STEP = 2
-PLAN = {(AT_A, 0, 0): {0: [(WR, 1)], 1: [(WL, 1), (WR, 1)], 2: [(WL, 1), (WR, 1)], 3: [(WL, 1)]},
- (AT_B, 0, 0): {0: [(OX, 1)], 1: [(OX, 1), (FFN_X, 3, 0)], 2: [(FFN_Z, 0, 0), (ZS, 0, 0), (OX, 1)], 3: [(OX, 1)]},
- (AT_B, 0, 1): {1: [(FFN_Z, 2, 2), (ZS, 2, 2)], 2: [(REL, 1, 0, 0)]},
- (AT_B, 0, 2): {0: [(XS_, 3, 2)], 1: [(XS_, 3, 1)], 2: [(XS_, 0, 1)], 3: [(XS_, 0, 2)]},
- (AT_B, 0, 3): {0: [(ZS, 3, 1)], 1: [(FFN_Z, 3, 0), (ZS, 3, 0)], 2: [(REL, 1, 1, 0)], 3: [(ZS, 0, 1)]},
- (AT_B, 0, 5): {0: [(SUM_0, 1), (XS_, 0, 0)],
-                1: [(REL, 0, 3, 0), (XS_, 3, 2)],
-                2: [(REL, 0, 3, 0), (XS_, 0, 2)],
-                3: [(SUM_0, 1), (XS_, 3, 0)]},
- (AT_B, 0, 6): {0: [(FFN_X, 3, 2)], 1: [(FFN_X, 3, 1)], 2: [(SUM_3, 0), (FFN_X, 0, 1)], 3: [(FFN_X, 0, 2)]},
- (AT_B, 1, 0): {0: [(XS_, 0, 1)], 1: [(REL, 0, 2, 0), (XS_, 1, 0)], 2: [(FFN_Z, 0, 1), (ZS, 0, 1)], 3: [(XS_, 3, 1)]},
- (AT_B, 1, 1): {0: [(FFN_X, 0, 0), (FFN_OWN, 0)],
-                1: [(FFN_X, 3, 2)],
-                2: [(REL, 1, 0, 1), (XS_, 2, 0), (FFN_X, 0, 2)],
-                3: [(FFN_X, 3, 0), (FFN_OWN, 0)]},
- (AT_B, 1, 2): {0: [(XO, 0)], 1: [(REL, 1, 0, 0), (XS_, 1, 1)], 2: [(REL, 1, 1, 1), (SUM_4, 0)], 3: [(SUM_3, 0)]},
- (AT_B, 1, 3): {0: [(SUM_3, 0), (ZS, 3, 2), (FFN_X, 0, 1)],
-                1: [(FFN_Z, 3, 1), (SUM_3, 0), (ZS, 3, 1), (FFN_X, 1, 0), (FFN_OWN, 0)],
-                2: [(XS_, 2, 1)],
-                3: [(ZS, 0, 2), (FFN_X, 3, 1)]},
- (AT_B, 1, 5): {0: [(SUM_0, 2)],
-                1: [(REL, 0, 3, 1)],
-                2: [(REL, 0, 3, 1), (FFN_X, 2, 0), (FFN_OWN, 0)],
-                3: [(SUM_4, 0), (SUM_0, 2), (XO, 0), (FFN_OWN, 1)]},
- (AT_B, 1, 6): {0: [(FFN_LAST, 0), (XS_, 0, 2), (FFN_OWN, 1)],
-                1: [(REL, 0, 2, 1), (XO, 0), (FFN_X, 1, 1), (FFN_OWN, 1)],
-                2: [(FFN_Z, 0, 2), (ZS, 0, 2), (XO, 0), (SUM_3, 1)]},
- (AT_B, 2, 0): {0: [(SUM_4, 0)],
-                1: [(SUM_4, 0)],
-                2: [(FFN_X, 2, 1), (FW, 2, 1, 0), (FW, 3, 3, 0), (FFN_OWN, 1)],
-                3: [(XO, 1)]},
- (AT_B, 2, 1): {0: [(XO, 1)], 1: [(REL, 1, 0, 1), (XO, 1)], 3: [(FFN_LAST, 0)]},
- (AT_B, 2, 2): {0: [(FFN_X, 0, 2)],
-                1: [(FFN_Z, 3, 2), (ZS, 3, 2), (FFN_LAST, 0)],
-                2: [(REL, 1, 0, 2), (XO, 1), (FFN_LAST, 0)],
-                3: [(XS_, 3, 2)]},
- (AT_B, 2, 3): {0: [(SUM_3, 1)], 1: [(SUM_3, 1)], 2: [(REL, 1, 1, 2), (SUM_4, 1)], 3: [(SUM_3, 1), (FFN_LAST, 1)]},
- (AT_B, 2, 5): {0: [(SUM_0, 3), (FFN_LAST, 1), (FFN_OWN, 2), (XO, 2)],
-                1: [(FW, 3, 2, 0), (REL, 0, 3, 2), (FFN_LAST, 1), (XS_, 1, 2)],
-                2: [(REL, 0, 3, 2), (XS_, 2, 2)],
+ORDERS = ((1, 2, 3, 0), (0, 2, 3, 1), (3, 1, 0, 2), (2, 1, 0, 3))
+OWN_STEP = 3
+PLAN = {(AT_A, 1, 1): {0: [(WR, 2)], 1: [(WR, 2)], 2: [(WL, 2)], 3: [(WL, 2)]},
+ (AT_A, 2, 0): {0: [(WD_, 1)], 1: [(WD_, 0)], 2: [(WD_, 1)], 3: [(WD_, 2)]},
+ (AT_B, 0, 0): {0: [(FFN_X, 2, 2), (OX, 1)],
+                1: [(FFN_Z, 3, 2), (ZS, 3, 2)],
+                2: [(REL, 1, 0, 0)],
+                3: [(FFN_X, 1, 2), (OX, 1)]},
+ (AT_B, 0, 1): {0: [(XS_, 1, 1)],
+                1: [(REL, 0, 3, 0), (XS_, 2, 1)],
+                2: [(REL, 1, 1, 0), (XS_, 1, 1)],
+                3: [(XS_, 2, 1)]},
+ (AT_B, 0, 5): {0: [(SUM_0, 1)], 1: [(REL, 0, 2, 0)], 3: [(SUM_0, 1)]},
+ (AT_B, 1, 0): {0: [(XS_, 1, 2)],
+                1: [(XS_, 2, 2)],
+                2: [(REL, 1, 0, 1), (REL, 0, 3, 0), (XS_, 1, 2)],
+                3: [(XS_, 2, 2)]},
+ (AT_B, 1, 1): {0: [(FFN_X, 1, 1), (XS_, 0, 0)],
+                1: [(REL, 0, 3, 1), (REL, 1, 0, 0), (FFN_X, 2, 1), (XS_, 1, 0), (FFN_Z, 2, 1), (ZS, 2, 1)],
+                2: [(REL, 1, 1, 1), (SUM_3, 0), (FFN_X, 1, 1), (FFN_Z, 1, 1), (ZS, 1, 1)],
+                3: [(FFN_X, 2, 1), (XS_, 3, 0)]},
+ (AT_B, 1, 5): {0: [(SUM_0, 2)], 2: [(REL, 0, 3, 1), (XS_, 2, 0)], 3: [(SUM_0, 2)]},
+ (AT_B, 2, 0): {0: [(FFN_X, 1, 2), (XS_, 0, 1)],
+                1: [(REL, 0, 2, 1), (SUM_3, 0), (FFN_X, 2, 2)],
+                2: [(FFN_X, 1, 2)],
+                3: [(FFN_X, 2, 2), (XS_, 3, 1)]},
+ (AT_B, 2, 1): {0: [(FFN_X, 0, 0), (FFN_OWN, 0), (XO, 0), (SUM_3, 0)],
+                1: [(REL, 1, 0, 1), (FFN_X, 1, 0), (FFN_OWN, 0), (SUM_3, 1), (REL, 0, 3, 2)],
+                2: [(SUM_4, 0), (REL, 1, 0, 2), (XS_, 2, 1)],
+                3: [(FFN_X, 3, 0), (FFN_OWN, 0), (XO, 0), (SUM_3, 0)]},
+ (AT_B, 2, 5): {0: [(SUM_0, 3)],
+                1: [(SUM_4, 0), (XO, 0)],
+                2: [(SUM_3, 1), (REL, 1, 1, 2), (FFN_X, 2, 0), (FFN_OWN, 0)],
                 3: [(SUM_0, 3)]},
- (AT_B, 2, 6): {0: [(SUM_4, 1)],
-                1: [(SUM_4, 1), (REL, 0, 2, 2)],
-                2: [(FW, 2, 1, 1), (FFN_LAST, 1)],
-                3: [(FFN_X, 3, 2), (FFN_OWN, 2), (XO, 2)]},
- (AT_D, 0): {0: [(SUM_7, 0), (SUM_3, 2), (GX, 1), (SUM_3, 3), (SUM_4, 2), (SUM_7, 1), (SUM_4, 3), (SUM_7, 2),
-                 (SUM_7, 3)],
-             1: [(REL, 1, 0, 2), (REL, 0, 3, 3), (SUM_3, 2), (REL, 0, 2, 3), (FW, 3, 2, 1), (REL, 1, 0, 3), (XO, 2),
-                 (FW, 2, 0, 1), (SUM_4, 2), (SUM_3, 3), (FW, 3, 3, 1), (SUM_7, 1), (FFN_LAST, 2), (GX, 1),
-                 (FW, 3, 2, 2), (FW, 2, 0, 2), (SUM_4, 3), (FW, 3, 2, 3), (FW, 2, 0, 3), (FW, 3, 3, 2), (SUM_7, 2),
-                 (FW, 3, 3, 3), (SUM_7, 3)],
-             2: [(REL, 0, 3, 3), (FW, 3, 3, 1), (SUM_4, 2), (SUM_3, 3), (FW, 2, 0, 1), (SUM_7, 1), (XO, 2),
-                 (SUM_4, 3), (FW, 2, 1, 2), (FW, 3, 3, 2), (GX, 0), (FFN_LAST, 2), (FW, 2, 0, 2), (SUM_7, 2), (GX, 1),
-                 (FW, 3, 3, 3), (FW, 2, 1, 3), (FW, 2, 0, 3), (SUM_7, 3)],
-             3: [(FFN_LAST, 2), (SUM_3, 2), (SUM_7, 0), (GX, 1), (SUM_3, 3), (SUM_4, 2), (SUM_7, 1), (SUM_4, 3),
-                 (SUM_7, 2), (SUM_7, 3)]},
- (AT_E, 0): {2: [(REL, 1, 0, 3)]},
- (AT_E, 1): {0: [(GX, 0), (FFN_LAST, 2)],
-             1: [(FW, 3, 3, 0), (FW, 2, 0, 0), (SUM_7, 0), (GX, 0), (FFN_X, 1, 2), (FFN_OWN, 2)],
-             2: [(FW, 2, 0, 0), (REL, 1, 1, 3), (SUM_7, 0), (SUM_3, 2), (FFN_X, 2, 2), (FFN_OWN, 2)],
-             3: [(SUM_4, 1), (GX, 0)]},
+ (AT_B, 3, 0): {1: [(REL, 0, 2, 2)]},
+ (AT_B, 3, 1): {0: [(FFN_X, 0, 1), (FFN_OWN, 1)], 2: [(REL, 0, 3, 2)], 3: [(FFN_X, 3, 1), (FFN_OWN, 1)]},
+ (AT_B, 3, 3): {1: [(SUM_4, 1), (XS_, 1, 1)], 2: [(XO, 0)], 3: [(SUM_3, 1)]},
+ (AT_D, 0): {0: [(SUM_4, 1), (XO, 1), (XS_, 0, 2), (SUM_3, 2), (ZS, 2, 2), (FFN_LAST, 1), (SUM_3, 3), (ZS, 1, 1),
+                 (FFN_X, 0, 2), (FFN_OWN, 2), (SUM_4, 2), (XO, 2), (SUM_4, 3), (GX, 0), (SUM_7, 0), (ZS, 1, 2),
+                 (FFN_LAST, 2), (GX, 1), (SUM_7, 1), (SUM_7, 2), (SUM_7, 3)],
+             1: [(REL, 0, 2, 3), (FFN_X, 1, 1), (SUM_3, 2), (REL, 1, 0, 3), (FFN_X, 1, 2), (FW, 2, 0, 0),
+                 (FW, 3, 2, 1), (FW, 2, 0, 1), (GX, 0), (SUM_3, 3), (SUM_4, 2), (FFN_Z, 2, 2), (FW, 3, 3, 0),
+                 (SUM_7, 0), (ZS, 2, 2), (FW, 3, 2, 2), (GX, 1), (FFN_OWN, 1), (SUM_4, 3), (FW, 3, 3, 1), (SUM_7, 1),
+                 (FW, 2, 0, 2), (XO, 1), (FW, 3, 3, 2), (SUM_7, 2), (FW, 2, 0, 3), (FW, 3, 2, 3), (FFN_LAST, 1),
+                 (FFN_OWN, 2), (XO, 2), (FW, 3, 3, 3), (SUM_7, 3), (FFN_LAST, 2)],
+             2: [(FW, 2, 1, 1), (FFN_LAST, 0), (FW, 3, 3, 0), (REL, 0, 3, 3), (SUM_4, 2), (XS_, 2, 2), (FW, 3, 3, 1),
+                 (SUM_3, 3), (FW, 2, 0, 0), (SUM_7, 0), (FFN_Z, 1, 2), (FFN_X, 2, 2), (FW, 2, 0, 1), (SUM_7, 1),
+                 (GX, 0), (FW, 3, 3, 2), (SUM_4, 3), (FW, 2, 1, 2), (GX, 1), (FFN_OWN, 1), (ZS, 1, 2), (XO, 1),
+                 (FFN_OWN, 2), (FW, 2, 1, 3), (FW, 3, 3, 3), (XO, 2), (FW, 2, 0, 2), (SUM_7, 2), (FFN_LAST, 1),
+                 (FW, 2, 0, 3), (SUM_7, 3), (FFN_LAST, 2)],
+             3: [(SUM_4, 1), (SUM_3, 2), (FFN_LAST, 1), (XS_, 3, 2), (ZS, 1, 2), (SUM_4, 2), (GX, 0), (SUM_3, 3),
+                 (FFN_X, 3, 2), (FFN_OWN, 2), (ZS, 2, 1), (XO, 2), (ZS, 2, 2), (SUM_7, 0), (SUM_4, 3), (GX, 1),
+                 (SUM_7, 1), (FFN_LAST, 2), (SUM_7, 2), (SUM_7, 3)]},
+ (AT_E, 0): {2: [(REL, 1, 0, 3), (FW, 2, 1, 0), (FFN_X, 2, 1)]},
+ (AT_E, 1): {0: [(SUM_3, 1), (FFN_LAST, 0), (SUM_4, 0)],
+             1: [(FW, 3, 2, 0), (REL, 0, 3, 3), (XS_, 1, 2), (REL, 1, 0, 2), (FFN_LAST, 0)],
+             2: [(SUM_4, 1), (REL, 1, 1, 3), (SUM_3, 2)],
+             3: [(XO, 1), (SUM_4, 0), (FFN_LAST, 0)]},
  (AT_G, 0): {0: [(XS_, 1, 0)], 1: [(XS_, 0, 0)], 2: [(XS_, 3, 0)], 3: [(XS_, 2, 0)]},
- (AT_G, 1): {1: [(XS_, 0, 2)], 2: [(FFN_X, 3, 0), (ZS, 3, 0)]},
- (AT_G, 2): {0: [(XS_, 2, 1)], 1: [(FFN_X, 0, 2), (ZS, 0, 2)], 3: [(XS_, 1, 1)]},
- (AT_G, 3): {0: [(XS_, 3, 0), (FFN_X, 2, 1), (ZS, 2, 1)],
-             2: [(XS_, 1, 2)],
-             3: [(XS_, 0, 0), (FFN_X, 1, 1), (ZS, 1, 1)]},
- (AT_N, 1): {0: [(XS_, 3, 1), (FFN_X, 2, 2), (ZS, 2, 2)],
-             1: [(FFN_Z, 2, 0), (ZS, 2, 0), (FFN_X, 2, 1), (FFN_X, 2, 2), (XS_, 3, 0)],
-             2: [(FFN_X, 1, 1), (FFN_Z, 1, 1), (ZS, 1, 1), (XS_, 0, 0)],
-             3: [(XS_, 0, 1), (FFN_X, 1, 2), (ZS, 1, 2)]},
- (AT_N, 2): {0: [(FFN_X, 3, 0), (ZS, 3, 0)], 2: [(FFN_X, 1, 2)], 3: [(FFN_X, 0, 0), (ZS, 0, 0)]},
- (AT_N, 3): {0: [(OX, 0)], 1: [(OX, 0)], 2: [(FFN_Z, 1, 2), (ZS, 1, 2), (OX, 0)], 3: [(OX, 0)]},
- (AT_N, 4): {0: [(SUM_0, 0), (FFN_X, 3, 1)],
-             1: [(FFN_Z, 2, 1), (ZS, 2, 1)],
-             2: [(FFN_X, 0, 0)],
-             3: [(SUM_0, 0), (FFN_X, 0, 1)]},
- (AT_T, 1, 0): {0: [(WR, 3), (XS_, 1, 1), (FFN_X, 1, 0), (ZS, 1, 0)],
-                3: [(WL, 3), (XS_, 2, 1), (FFN_X, 2, 0), (ZS, 2, 0)]},
- (AT_T, 1, 1): {1: [(XS_, 0, 1)]},
- (AT_T, 1, 2): {2: [(XS_, 3, 1)]},
- (AT_T, 1, 3): {0: [(XS_, 1, 2)], 1: [(FFN_X, 0, 0), (ZS, 0, 0)], 3: [(XS_, 2, 2)]},
- (AT_T, 2, 0): {0: [(FFN_X, 1, 1), (ZS, 1, 1)], 2: [(XS_, 3, 2)], 3: [(FFN_X, 2, 1), (ZS, 2, 1)]},
- (AT_T, 2, 1): {0: [(XS_, 2, 0)], 1: [(FFN_X, 0, 1), (ZS, 0, 1)], 3: [(XS_, 1, 0)]},
- (AT_T, 2, 2): {1: [(XS_, 2, 0)], 2: [(FFN_X, 3, 1), (ZS, 3, 1)]},
- (AT_T, 2, 3): {0: [(FFN_X, 1, 2), (ZS, 1, 2)], 2: [(XS_, 1, 0)], 3: [(FFN_X, 2, 2), (ZS, 2, 2)]},
- (AT_T, 3, 0): {0: [(FFN_X, 2, 0), (ZS, 2, 0)],
-                1: [(XS_, 2, 1)],
-                2: [(FFN_X, 3, 2), (ZS, 3, 2)],
-                3: [(FFN_X, 1, 0), (ZS, 1, 0)]},
- (AT_T, 3, 1): {0: [(XS_, 2, 2)], 2: [(XS_, 1, 1)], 3: [(XS_, 1, 2)]},
- (AT_T, 3, 2): {1: [(FFN_X, 2, 0)]},
- (AT_T, 3, 3): {1: [(XS_, 2, 2)], 2: [(FFN_X, 1, 0), (FFN_Z, 1, 0), (ZS, 1, 0)]},
- (AT_W, 1): {0: [(WR, 2)], 1: [(WR, 2)], 2: [(WL, 2)], 3: [(WL, 2)]}}
+ (AT_G, 1): {0: [(XS_, 2, 0)],
+             1: [(FFN_X, 0, 0), (ZS, 0, 0), (XS_, 0, 2)],
+             2: [(FFN_X, 3, 0), (ZS, 3, 0), (XS_, 3, 2)],
+             3: [(XS_, 1, 0)]},
+ (AT_G, 2): {0: [(FFN_X, 2, 0), (ZS, 2, 0), (XS_, 3, 0)], 3: [(FFN_X, 1, 0), (ZS, 1, 0), (XS_, 0, 0)]},
+ (AT_G, 3): {0: [(FFN_X, 3, 0), (ZS, 3, 0), (XS_, 3, 2)],
+             1: [(XS_, 3, 1), (FFN_X, 2, 0), (FFN_Z, 2, 0), (ZS, 2, 0)],
+             2: [(XS_, 0, 1), (FFN_X, 1, 0), (FFN_Z, 1, 0), (ZS, 1, 0)],
+             3: [(FFN_X, 0, 0), (ZS, 0, 0), (XS_, 0, 2)]},
+ (AT_N, 1): {0: [(FFN_X, 3, 1), (ZS, 3, 1), (XS_, 2, 2)],
+             1: [(FFN_X, 3, 0), (XS_, 3, 2)],
+             2: [(FFN_X, 0, 0), (XS_, 0, 2), (FFN_Z, 0, 0), (ZS, 0, 0)],
+             3: [(FFN_X, 0, 1), (ZS, 0, 1), (XS_, 1, 2)]},
+ (AT_N, 2): {1: [(FFN_X, 3, 1), (OX, 0), (FFN_Z, 3, 0), (ZS, 3, 0)],
+             2: [(FFN_X, 0, 1), (OX, 0), (FFN_Z, 0, 1), (ZS, 0, 1)]},
+ (AT_N, 3): {0: [(FFN_X, 3, 2), (ZS, 3, 2), (OX, 0)],
+             1: [(FFN_Z, 3, 1), (ZS, 3, 1)],
+             3: [(FFN_X, 0, 2), (ZS, 0, 2), (OX, 0)]},
+ (AT_N, 4): {0: [(SUM_0, 0)],
+             1: [(FFN_X, 3, 2), (OX, 1)],
+             2: [(FFN_X, 0, 2), (OX, 1), (FFN_Z, 0, 2), (ZS, 0, 2)],
+             3: [(SUM_0, 0)]},
+ (AT_T, 0, 0): {1: [(WD_, 3)], 2: [(WD_, 0)]},
+ (AT_T, 1, 0): {1: [(XS_, 0, 1)], 2: [(XS_, 3, 1)]},
+ (AT_T, 1, 1): {0: [(WD_, 3)], 3: [(WD_, 0)]},
+ (AT_T, 2, 0): {0: [(XS_, 2, 1), (FFN_X, 1, 0), (ZS, 1, 0)], 3: [(XS_, 1, 1), (FFN_X, 2, 0), (ZS, 2, 0)]},
+ (AT_T, 2, 1): {1: [(FFN_X, 0, 1), (ZS, 0, 1), (XS_, 2, 0)], 2: [(FFN_X, 3, 1), (ZS, 3, 1), (XS_, 1, 0)]},
+ (AT_T, 3, 0): {0: [(FFN_X, 2, 1), (ZS, 2, 1), (XS_, 3, 1)],
+                1: [(XS_, 3, 0), (FFN_X, 0, 2), (ZS, 0, 2)],
+                2: [(XS_, 0, 0), (FFN_X, 3, 2), (ZS, 3, 2)],
+                3: [(FFN_X, 1, 1), (ZS, 1, 1), (XS_, 0, 1)]},
+ (AT_W, 0): {0: [(WR, 1)], 1: [(WL, 1), (WR, 1)], 2: [(WL, 1), (WR, 1)], 3: [(WL, 1)]},
+ (AT_W, 4): {0: [(WD_, 2), (WR, 3)], 1: [(WD_, 2)], 2: [(WD_, 3)], 3: [(WD_, 1), (WL, 3)]}}
 HALF = (0, 0, 0, 0)
 
 
@@ -491,10 +487,10 @@
     inputs, cond, again, adaw_h, adab, qkv_h, outw_h, fgain, up_h, upb, down_h, downb, cot_h,
     cos_h, sin_h, cost_h, sint_h,
     out_o, gin_o, qkv_o, outw_o, ffn_o, vall_o,
-    adaw, wq, wo, wu, wd, ub, cos_v, sin_v, cost, sint,
-    xb, ctb, mod2, n1, i1, ai, ait, q_s, k_s, v_s, kt_s, vt_s, ot_s, lse, att, att_s,
+    wq, wo, wu, wd, ub, cos_v, sin_v, cost, sint,
+    xb, ctb, mod2, n1, i1, ai, ait, q_s, k_s, v_s, kt_s, vt_s, ot_s, lse, att,
     ap, n2, i2, fit, gf, gft, oacc, gacc, a_s, gp_s, g_s, grecv,
-    gm, do_s, dlt, dqt, gq, b_s, xs, vec, vecr, vall, ubg,
+    do_s, dlt, dqt, gq, b_s, xs, vec, vecr, vall, ubg,
     rx, rz, fxr, rxb, fb,
     lsem, ssem, rsem, wss, wrs, yss, yrs, fss, frs, bss, brs, hss, hrs, vss, vrs, credit,
 ):
@@ -524,7 +520,7 @@
         return pltpu.make_async_copy(src, dst, lsem.at[index])
 
     half = pl.ds(pl.multiple_of(c * 384, 128), 384)
-    loads = [local(inputs.at[x], xb.at[rows_of(x * 256, 256)], 0), local(adaw_h, adaw, 1)]
+    loads = [local(inputs.at[x], xb.at[rows_of(x * 256, 256)], 0), ]
     loads += [local(cos_h, cos_v, 2), local(sin_h, sin_v, 3), local(cost_h, cost, 4), local(sint_h, sint, 5)]
     for p in range(3):
         for part in range(3):
@@ -539,7 +535,11 @@
     loads.append(local(up_h.at[:, half], wu.at[z], 16))
     loads.append(local(down_h.at[rows_of(c * 384, 384)], wd.at[z], 17))
     loads.append(local(cot_h.at[x], ctb.at[rows_of(x * 256, 256)], 18))
-    for item in loads:
+    adaw = [
+        local(adaw_h.at[:, pl.ds(part * D, D)], fit.at[pl.ds(part * 128, 128), pl.ds(0, D)], 15 + 43 + part)
+        for part in range(6)
+    ]
+    for item in [loads[0]] + adaw + loads[1:]:
         item.start()
 
     ub[z] = flat(upb)
@@ -555,22 +555,25 @@
     swap_c = remote(cot_h.at[1 - x], ctb.at[rows_of(x * 256, 256)], 1, TO_X)
     swap_c.start()
 
-    def up_half(ref, which):
-        return ref.at[rows_of(which * 384, 384)]
-
-    def down_half(ref, which):
-        return ref.at[rows_of(which * 192, 192)]
+    def rows_at(ref, rows, which, part=None):
+        start = which * rows
+        if part is None:
+            return ref.at[rows_of(start, rows)]
+        return ref.at[pl.ds(pl.multiple_of(start + part * (rows // 2), 16), rows // 2)]
+
+    here = grp * 2 + x
 
     def z_copies(j, way, device, first):
+        own_up, own_down = rows_at(wu.at[j], 192, here), rows_at(wd.at[j], 96, here)
         if first:
             src = (
-                up_h.at[rows_of(grp * 384, 384), half],
-                down_h.at[rows_of(c * 384 + grp * 192, 192)],
+                up_h.at[rows_of(here * 192, 192), half],
+                down_h.at[rows_of(c * 384 + here * 96, 96)],
                 ub.at[z],
             )
         else:
-            src = (up_half(wu.at[j], grp), down_half(wd.at[j], grp), ub.at[j])
-        dst = (up_half(wu.at[j], grp), down_half(wd.at[j], grp), ub.at[j])
+            src = (own_up, own_down, ub.at[j])
+        dst = (own_up, own_down, ub.at[j])
         return [
             pltpu.make_async_remote_copy(
                 src_ref=src[i], dst_ref=dst[i], send_sem=wss.at[way, j, i], recv_sem=wrs.at[way, j, i],
@@ -579,14 +582,28 @@
             for i in range(3)
         ]
 
-    def y_copies(j, which):
+    def pair_copies(j, kind, which, part, device):
         return [
             pltpu.make_async_remote_copy(
-                src_ref=ref, dst_ref=ref, send_sem=yss.at[j, i], recv_sem=yrs.at[j, i],
-                device_id=TO_Y, device_id_type=MESH,
+                src_ref=ref, dst_ref=ref, send_sem=yss.at[j, kind, i], recv_sem=yrs.at[j, kind, i],
+                device_id=device, device_id_type=MESH,
             )
-            for i, ref in enumerate((up_half(wu.at[j], which), down_half(wd.at[j], which)))
+            for i, ref in enumerate((rows_at(wu.at[j], 192, which, part), rows_at(wd.at[j], 96, which, part)))
         ]
+
+    by_x, by_y, across = grp * 2 + 1 - x, (1 - grp) * 2 + x, (1 - grp) * 2 + 1 - x
+
+    def quarter_sends(j):
+        return pair_copies(j, 0, here, None, TO_X) + pair_copies(j, 1, here, None, TO_Y)
+
+    def quarter_waits(j):
+        return pair_copies(j, 0, by_x, None, TO_X) + pair_copies(j, 1, by_y, None, TO_Y)
+
+    def across_sends(j):
+        return pair_copies(j, 2, by_y, 0, TO_X) + pair_copies(j, 3, by_x, 1, TO_Y)
+
+    def across_waits(j):
+        return pair_copies(j, 2, across, 0, TO_X) + pair_copies(j, 3, across, 1, TO_Y)
 
     def start_all(items):
         for item in items:
@@ -792,14 +809,19 @@
             item.wait_recv()
         if place < 3:
             start_all(z_copies(place - k, 0, RIGHT, False))
-        start_all(y_copies(place - k, grp))
+        start_all(quarter_sends(place - k))
 
     def wr(place, k):
         for item in z_copies(place + k, 1, LEFT, False):
             item.wait_recv()
         if place > 0:
             start_all(z_copies(place + k, 1, LEFT, False))
-        start_all(y_copies(place + k, grp))
+        start_all(quarter_sends(place + k))
+
+    def wd_(place, j):
+        for item in quarter_waits(j):
+            item.wait_recv()
+        start_all(across_sends(j))
 
     def cross_rows(out_ref, number, part):
         rows = rows_of((1 - x) * 256 + part * 128, 128)
@@ -813,7 +835,7 @@
     def gx(place, part):
         cross_rows(gin_o, 1, part).start()
 
-    jobs = (ffn_x, ffn_z, ffn_own, ffn_last, sum_0, rel, sum_3, sum_4, fw, sum_7, wl, wr, xs_, zs, xo, ox, gx)
+    jobs = (ffn_x, ffn_z, ffn_own, ffn_last, sum_0, rel, sum_3, sum_4, fw, sum_7, wl, wr, xs_, zs, xo, ox, gx, wd_)
 
     def slot(name, here=None):
         for place, names in PLAN.get(name, {}).items():
@@ -822,10 +844,10 @@
                 for job, *rest in names:
                     jobs[job](place, *rest)
 
-    local(adaw_h, adaw, 1).wait()
     for part in range(6):
         lanes = pl.ds(part * D, D)
-        mod2[:, lanes] = dot(cond[...], adaw[:, lanes]) + adab[:, part * D : (part + 1) * D]
+        adaw[part].wait()
+        mod2[:, lanes] = dot(cond[...], fit[part * 128 : (part + 1) * 128, :D]) + adab[:, part * D : (part + 1) * D]
     modrow = mod2[pl.ds(x, 1), :]
     shift_one, scale_one, gate_one, shift_two, scale_two, gate_two = [
         modrow[:, part * D : (part + 1) * D] for part in range(6)
@@ -854,7 +876,7 @@
         part = ref.at[rows_of(start, size)]
         return remote(part, part, index, TO_CORE)
 
-    for item in loads[2:15]:
+    for item in loads[1:14]:
         item.wait()
 
     def project_rows(start):
@@ -884,16 +906,18 @@
     project_rows(own + x * 256)
     core_rows(ai, other + x * 256, 256, 2).wait_recv()
     project_rows(other + x * 256)
+    slot((AT_W, 5))
     swap_x.wait_recv()
     norm_one_block(1 - x)
     core_rows(ai, own + (1 - x) * 256, 256, 3).start()
     project_rows(own + (1 - x) * 256)
     core_rows(ai, other + (1 - x) * 256, 256, 3).wait_recv()
     project_rows(other + (1 - x) * 256)
-    for item in loads[16:18]:
+    for item in loads[15:17]:
         item.wait()
     slot((AT_W, 0))
 
+    att_s = a_s.at[pl.ds(0, 512)]
     low_lane = lax.broadcasted_iota(jnp.int32, (1, 128), 1) < 64
     keep = [low_lane.astype(F32).astype(BF), (~low_lane).astype(F32).astype(BF)]
 
@@ -952,7 +976,7 @@
     attend(0)
     attend(1)
 
-    loads[18].wait()
+    loads[17].wait()
     swap_c.wait_recv()
 
     @pl.loop(0, 512 // TILE)
@@ -975,7 +999,7 @@
             4 + p,
             TO_CORE,
         ).wait_recv()
-    loads[15].wait()
+    loads[14].wait()
 
     core_rows(ai, own + x * 256, 256, 2).wait_send()
     core_rows(ai, own + (1 - x) * 256, 256, 3).wait_send()
@@ -985,6 +1009,8 @@
     def _(b):
         rows = rows_of(b * 256, 256)
         ap[rows] = dot(att[rows], wo[...])
+        slot((AT_W, 3), b == 0)
+        slot((AT_W, 4), b == 1)
 
         @pl.loop(0, 256 // TILE)
         def _(i):
@@ -1013,6 +1039,9 @@
     turn(fi, fit, other)
     slot((AT_W, 2))
 
+    for p in range(3):
+        att_copy(p, False).wait_send()
+
     coef = 0.7978845608028654
 
     @pl.loop(0, Z)
@@ -1024,20 +1053,20 @@
 
         @pl.when(k != OWN_STEP)
         def _():
-            for item in y_copies(j, 1 - grp):
+            for item in across_waits(j):
                 item.wait_recv()
 
         bias = ub[j][:, pl.ds(0, 384)]
         bias = jnp.where(c == 0, bias, ub[j][:, pl.ds(384, 384)])
 
-        @pl.loop(0, 4)
+        @pl.loop(0, 2)
         def _(t):
-            rows = rows_of(t * 256, 256)
+            rows = rows_of(t * 512, 512)
             pre = dot(fi[rows], wu[j]) + bias
             sq = pre * pre
-            th = jnp.tanh(coef * (pre + 0.044715 * pre * sq))
-            act = (0.5 * pre * (1.0 + th)).astype(BF)
-            slope = 0.5 * (1.0 + th) + 0.5 * pre * (1.0 - th * th) * coef * (1.0 + 3.0 * 0.044715 * sq)
+            upper = 0.5 + 0.5 * jnp.tanh(pre * (coef + (coef * 0.044715) * sq))
+            act = (pre * upper).astype(BF)
+            slope = upper + pre * (2.0 * upper * (1.0 - upper)) * (coef + (3.0 * 0.044715 * coef) * sq)
             a_s[rows] = act
             grad_pre = (dot_t(gf[rows], wd[j]) * slope).astype(BF)
             gp_s[rows] = grad_pre
@@ -1056,7 +1085,7 @@
                 gacc[rows] += gin
 
             for m in range(Z):
-                for n in range(4):
+                for n in range(2):
                     slot((AT_T, m, n), (k == m) & (t == n))
 
             @pl.when(t == 0)
@@ -1067,11 +1096,8 @@
             def _():
                 ubg[j] += bsum
 
-        @pl.loop(0, 3)
-        def _(r):
-            rows = rows_of(r * 256, 256)
-            g_s[0, j, rows] = dot(fit[rows], gp_s[...]).astype(BF)
-            g_s[1, j, rows] = dot(gft[rows], a_s[...]).astype(BF)
+        g_s[0, j] = dot(fit[...], gp_s[...]).astype(BF)
+        g_s[1, j] = dot(gft[...], a_s[...]).astype(BF)
 
         for n in range(Z):
             slot((AT_G, n), k == n)
@@ -1103,7 +1129,7 @@
                 for item in z_copies(z - k, 0, RIGHT, False):
                     item.wait_send()
 
-            for item in y_copies(z - k, grp):
+            for item in quarter_sends(z - k) + across_sends(z - k):
                 item.wait_send()
 
         @pl.when(z + k <= Z - 1)
@@ -1113,7 +1139,7 @@
                 for item in z_copies(z + k, 1, LEFT, False):
                     item.wait_send()
 
-            for item in y_copies(z + k, grp):
+            for item in quarter_sends(z + k) + across_sends(z + k):
                 item.wait_send()
 
     @pl.when(z < Z - 1)
@@ -1164,7 +1190,7 @@
         vec[3:4] += jnp.sum(grad, axis=0, keepdims=True)
         vec[4:5] += jnp.sum(grad * normed, axis=0, keepdims=True)
         middle = ctb[tile].astype(F32) + norm_back(grad * mul_two, normed, i2[tile])
-        gm[tile] = middle
+        n2[tile] = middle
         gf[near] = (gate_one * middle).astype(BF)
         vec[2:3] += jnp.sum(middle * ap[tile], axis=0, keepdims=True)
 
@@ -1224,9 +1250,9 @@
             gp_s[:, h * 128 : (h + 1) * 128] = do_s[p] * keep[h]
         dqt[...] = jnp.zeros_like(dqt)
 
-        @pl.loop(0, 4)
+        @pl.loop(0, 2)
         def _(t):
-            rows = rows_of(t * 256, 256)
+            rows = rows_of(t * 512, 512)
             keys, values = k_s[p, rows], v_s[p, rows]
             dv, dk = None, None
             for h in range(2):
@@ -1240,10 +1266,10 @@
                 dk = dk_h if dk is None else dk + dk_h
                 dqt[pl.ds(h * 64, 64)] += dot(kt_s[p, pl.ds(h * 64, 64), rows], ds)
             cos_t, sin_t = cos_v[rows], sin_v[rows]
-            gq[rows, pl.ds(128, 128)] = (dk * cos_t - swap_halves(dk) * sin_t).astype(BF)
-            gq[rows, pl.ds(256, 128)] = dv.astype(BF)
-
-            for n in range(4):
+            gq[p, rows, pl.ds(128, 128)] = (dk * cos_t - swap_halves(dk) * sin_t).astype(BF)
+            gq[p, rows, pl.ds(256, 128)] = dv.astype(BF)
+
+            for n in range(2):
                 slot((AT_B, p, n), t == n)
 
         @pl.loop(0, 4)
@@ -1255,29 +1281,24 @@
             for h in range(2):
                 u, w = block[h * 64 : h * 64 + 32], block[h * 64 + 32 : h * 64 + 64]
                 parts += [u * cos_t + w * sin_t, w * cos_t - u * sin_t]
-            gq[rows, pl.ds(0, 128)] = jnp.concatenate(parts, axis=0).T.astype(BF)
-
-        @pl.loop(0, 3)
-        def _(r):
-            rows = rows_of(r * 256, 256)
-            b_s[1 + p, rows] = dot(ait[rows], gq[...]).astype(BF)
-
+            gq[p, rows, pl.ds(0, 128)] = jnp.concatenate(parts, axis=0).T.astype(BF)
+
+        b_s[1 + p] = dot(ait[...], gq[p]).astype(BF)
         slot((AT_B, p, 5))
-
-        @pl.loop(0, 4)
-        def _(t):
-            rows = rows_of(t * 256, 256)
-            part = dot_t(gq[rows], wq[p])
-            if p == 0:
-                gacc[rows] = part
-            else:
-                gacc[rows] += part
-
-        slot((AT_B, p, 6))
 
     remote(gsend, grecv, 9, TO_CORE).wait_send()
     for p in range(3):
         attend_back(p)
+
+    @pl.loop(0, 4)
+    def _(t):
+        rows = rows_of(t * 256, 256)
+        part = dot_t(gq[0, rows], wq[0])
+        for p in range(1, 3):
+            part = part + dot_t(gq[p, rows], wq[p])
+        gacc[rows] = part
+        for n in range(4):
+            slot((AT_B, 3, n), t == n)
 
     @pl.loop(0, 512 // TILE)
     def _(i):
@@ -1295,7 +1316,7 @@
         normed = n1[tile]
         vec[0:1] += jnp.sum(grad, axis=0, keepdims=True)
         vec[1:2] += jnp.sum(grad * normed, axis=0, keepdims=True)
-        rows_out(1, i, gm[tile] + norm_back(grad * mul_one, normed, i1[tile]))
+        rows_out(1, i, n2[tile] + norm_back(grad * mul_one, normed, i1[tile]))
 
     out_copy(gin_o, 1).start()
     slot((AT_E, 1))
@@ -1349,8 +1370,6 @@
         vec_copy(n, chip).wait_send()
     swap_x.wait_send()
     swap_c.wait_send()
-    for p in range(3):
-        att_copy(p, False).wait_send()
     core_rows(fi, own, 512, 8).wait_send()
     core_rows(gproj, own, 512, 11).wait_send()
     remote(vec, vecr, 30, TO_CORE).wait_send()
@@ -1471,24 +1490,24 @@
     V = pltpu.VMEM
     dma = pltpu.SemaphoreType.DMA
     scratch = [
-        V((128, 4608), BF), V((3, 768, 384), BF), V((768, 768), BF), V((Z, 768, 384), BF),
+        V((3, 768, 384), BF), V((768, 768), BF), V((Z, 768, 384), BF),
         V((Z, 384, 768), BF), V((Z, 1, 768), F32), V((1024, 128), F32), V((1024, 128), F32),
         V((32, 1024), F32), V((32, 1024), F32),
         V((512, 768), BF), V((512, 768), BF), V((2, 4608), F32), V((512, 768), F32), V((512, 1), F32),
         V((1024, 768), BF), V((768, 1024), BF),
         V((3, 1024, 128), BF), V((3, 1024, 128), BF), V((3, 1024, 128), BF),
         V((3, 128, 1024), BF), V((3, 128, 1024), BF), V((3, 128, 1024), F32), V((3, 2, 1024), F32),
-        V((512, 768), BF), V((512, 384), BF),
+        V((512, 768), BF),
         V((512, 768), F32), V((512, 768), F32), V((512, 1), F32),
         V((768, 1024), BF), V((1024, 768), BF), V((768, 1024), BF),
         V((1024, 768), F32), V((1024, 768), F32), V((1024, 384), BF), V((1024, 384), BF),
         V((2, Z, 768, 384), BF), V((512, 768), BF),
-        V((512, 768), F32), V((3, 1024, 128), BF), V((3, 2, 1024), F32), V((128, 1024), F32),
-        V((1024, 384), BF), V((4, 768, 384), BF), V((2, 512, 768), BF),
+        V((3, 1024, 128), BF), V((3, 2, 1024), F32), V((128, 1024), F32),
+        V((3, 1024, 384), BF), V((4, 768, 384), BF), V((2, 512, 768), BF),
         V((16, 768), F32), V((16, 768), F32), V((2 * Z, 16, 768), F32), V((Z, 1, 384), F32),
         V((Z, 768, 384), BF), V((Z, 768, 384), BF), V((768, 384), BF), V((4, 192, 384), BF),
         V((4, 768, 384), BF),
-        dma((63,)), dma((38,)), dma((38,)), dma((2, Z, 3)), dma((2, Z, 3)), dma((Z, 2)), dma((Z, 2)),
+        dma((64,)), dma((38,)), dma((38,)), dma((2, Z, 3)), dma((2, Z, 3)), dma((Z, 4, 2)), dma((Z, 4, 2)),
         dma((Z, 3)), dma((Z, 3)), dma((4, 4, 4)), dma((4, 4, 4)), dma((6, 4)), dma((6, 4)), dma((7,)), dma((7,)),
         pltpu.SemaphoreType.REGULAR((2,)),
     ]

time: 199 us -> 189 us (0.950)
  Pallas kernels: 198 us -> 188 us
    pallas_call x1, Pallas kernels: 185 us -> 175 us  [fast_shards(): pl.pallas_call(fast_kernel, out_shape=[token, token, shape(qkv_weight.sha...]
where the time goes in v4:
time: 189 us; the launch traced here: 188 us
  Pallas kernels  188 us (99%)
    pallas_call x1, Pallas kernels, fast_shards(): pl.pallas_call(fast_kernel, out_shape=[token, token, shape(qkv_weight.sha...  175 us
    pallas_call x1, Pallas kernels, fast_shards(): pl.pallas_call(finish_kernel, out_shape=[tokens, tokens, same(condition),...  12.3 us

profile of v4, /device:TPU:0, one launch (start us, length us, event | category | flops | bytes accessed | tf_op | source)
XLA Modules:
  0.0 188.5 jit_solution(11568397307409440913)
XLA Ops:
  0.6 175.4 %block.1 = (bf16[2,256,768]{2,1,0:T(8,128)(2,1)}, bf16[2,256,768]{2,1,0:T(8,128)(2,1)}, bf16[768,2304]{1,0:T(8,128)(2,1)}, bf16[768,768]{1,0:T(8,128)(2,1)}, bf1...) custom-call(bf16[2,256,768]{2,1,0:T(8,128)(2,1)} %inputs.1, bf16[2,128]{1,0:T(2,128)(2,1)} %cond.1, f32[768]{0:T(1024)} %again.1, ...), custom_call_target="tpu_custom_call" | custom-call | tf_op jit(solution)/shard_map/block/pallas_call | solution.py:1517
  176.0 12.3 %finish.1 = (f32[2,256,768]{2,1,0:T(8,128)}, f32[2,256,768]{2,1,0:T(8,128)}, f32[2,128]{1,0:T(2,128)}, f32[768]{0:T(1024)}, f32[128,4608]{1,0:T(8,128)}, /*index...) custom-call(bf16[2,256,768]{2,1,0:T(8,128)(2,1)} %get-tuple-element., ...), custom_call_target="tpu_custom_call" | custom-call | tf_op jit(solution)/shard_map/finish/pallas_call | solution.py:1535
